TPU v7x, 128 devices: a whole 4x4x4 slice. The times are simulated.
128 devices in a mesh: ctx: 16 (over y, x_hi, core), smp: 8 (over z, x_lo).
Axes of the slice: x: 4 (x_hi: 2, x_lo: 2; x = x_hi * 2 + x_lo), y: 4, z: 4, core: 2. Of those that a mesh axis runs over, the one named last changes fastest.
Arguments:
- prompt_input: bfloat16 [2048, 16384], P('smp', 'ctx'), may hold values from -6 to 6
- prompt_gate: bfloat16 [2048, 16384], P('smp', 'ctx'), may hold values from -6 to 6
- filters: float32 [2048, 16384], P('smp', 'ctx')
- skip: float32 [2048], replicated, may hold values from 0.2 to 1.8
- sample_input: bfloat16 [256, 1024, 2048], P(('ctx', 'smp')), may hold values from -6 to 6
- sample_gate: bfloat16 [256, 1024, 2048], P(('ctx', 'smp')), may hold values from -6 to 6
- lengths: int32 [256], P(('ctx', 'smp')), may hold values from 1 to 1024
Outputs:
- prompt_output: bfloat16 [2048, 16384], P('smp', 'ctx')
- sample_output: bfloat16 [256, 1024, 2048], P(('ctx', 'smp'))
All inputs are finite; a program needn't handle non-finite values.
Results may differ from a plain program's by a relative error of at most 0.001.
Values sent between devices are 32-bit elements; how exact they have to be, the bound alone decides.
No kernel may reach another device: no remote copies, remote signals or barrier semaphores. Data moves between devices by JAX's collectives and lax.ppermute only.
A program may use at most 128 MiB of HBM per device.

v0:
```python
import math

import jax
import jax.numpy as jnp
from jax import lax
from jax.sharding import PartitionSpec as P


def tables(first, second, period):
    angles = (
        2.0 * math.pi / period * (first[:, None] * second[None, :] % period).astype(jnp.float32)
    )
    return (jnp.cos(angles), jnp.sin(angles))


def product_of(pattern, left, right):
    return jnp.einsum(pattern, left, right, precision=lax.Precision.HIGHEST)


def rotate(real_part, imag_part, cosine, sine_table, inverse):
    if inverse:
        return (
            real_part * cosine - imag_part * sine_table,
            real_part * sine_table + imag_part * cosine,
        )
    return (
        real_part * cosine + imag_part * sine_table,
        imag_part * cosine - real_part * sine_table,
    )


def first_section(values, cosine, sine_table):
    real_part = product_of("...nm,nk->...km", values, cosine)
    imag_part = -product_of("...nm,nk->...km", values, sine_table)
    return (real_part, imag_part)


def transform(real_part, imag_part, cosine, sine_table, inverse):
    real_cos = product_of("...m,mj->...j", real_part, cosine)
    real_sin = product_of("...m,mj->...j", real_part, sine_table)
    imag_cos = product_of("...m,mj->...j", imag_part, cosine)
    imag_sin = product_of("...m,mj->...j", imag_part, sine_table)
    if inverse:
        return (real_cos - imag_sin, real_sin + imag_cos)
    return (real_cos + imag_sin, imag_cos - real_sin)


def last_section(real_part, imag_part, cosine, sine_table):
    return product_of("...km,kn->...nm", real_part, cosine) - product_of(
        "...km,kn->...nm", imag_part, sine_table
    )


def multiply_spectra(spec_real, spec_imag):
    prod_real = spec_real[0] * spec_real[1] - spec_imag[0] * spec_imag[1]
    prod_imag = spec_real[0] * spec_imag[1] + spec_imag[0] * spec_real[1]
    return (prod_real, prod_imag)


def gather_tail(tail_piece):
    partial_tail = lax.all_gather(tail_piece[None, None], "ctx", axis=1, tiled=True)
    return lax.all_gather(partial_tail, "smp", axis=0, tiled=True)


def on_device(prompt_input, prompt_gate, filters, skip, sample_input, sample_gate, lengths):
    ctx_count = lax.axis_size("ctx")
    smp_count = lax.axis_size("smp")
    position = lax.axis_index("ctx")
    width_dev, span = prompt_input.shape
    radix = 2 * ctx_count
    period = radix * span
    signal = prompt_input.astype(jnp.float32)
    paired = jnp.stack([signal, filters])
    block_index = jnp.arange(ctx_count, dtype=jnp.int32)
    freq_first = jnp.arange(radix, dtype=jnp.int32)
    block_out = jnp.arange(ctx_count + 1, dtype=jnp.int32)
    offsets = jnp.arange(span, dtype=jnp.int32)
    cos_first, sin_first = tables(block_index, freq_first, radix)
    cos_second, sin_second = tables(offsets, offsets, span)
    cos_last, sin_last = tables(freq_first, block_out, radix)
    slice_len = span // ctx_count
    regrouped = lax.all_to_all(
        paired.reshape(2, width_dev, 1, span), "ctx", split_axis=3, concat_axis=2, tiled=True
    )
    real_part, imag_part = first_section(regrouped, cos_first, sin_first)
    owned = position * slice_len + jnp.arange(slice_len, dtype=jnp.int32)
    twist_cos, twist_sin = tables(freq_first, owned, period)
    real_part, imag_part = rotate(real_part, imag_part, twist_cos, twist_sin, False)
    spectra_in = lax.all_to_all(
        jnp.stack([real_part, imag_part]), "ctx", split_axis=3, concat_axis=4, tiled=True
    )
    spec_real, spec_imag = transform(spectra_in[0], spectra_in[1], cos_second, sin_second, False)
    prod_real, prod_imag = multiply_spectra(spec_real, spec_imag)
    time_real, time_imag = transform(prod_real, prod_imag, cos_second, sin_second, True)
    local_freq = position * 2 + jnp.arange(2, dtype=jnp.int32)
    twist_cos, twist_sin = tables(local_freq, offsets, period)
    time_real, time_imag = rotate(time_real, time_imag, twist_cos, twist_sin, True)
    returned = lax.all_to_all(
        jnp.stack([time_real, time_imag]), "ctx", split_axis=3, concat_axis=2, tiled=True
    )
    result = last_section(returned[0], returned[1], cos_last, sin_last) / period
    own_blocks = lax.all_to_all(
        result[:, :ctx_count], "ctx", split_axis=1, concat_axis=2, tiled=True
    )
    convolved = own_blocks.reshape(width_dev, span)
    spread_tail = gather_tail(result[:, ctx_count])
    tail_state = spread_tail.transpose(0, 2, 1, 3).reshape(width_dev * smp_count, span)
    skip_local = lax.dynamic_slice_in_dim(skip, lax.axis_index("smp") * width_dev, width_dev)
    prompt_output = (
        prompt_gate.astype(jnp.float32) * (convolved + skip_local[:, None] * signal)
    ).astype(jnp.bfloat16)
    active = offsets[None, :] < lengths[:, None]
    blended = sample_gate.astype(jnp.float32) * (
        tail_state.T[None, :, :] + skip[None, None, :] * sample_input.astype(jnp.float32)
    )
    sample_output = jnp.where(active[:, :, None], blended, jnp.zeros_like(blended)).astype(
        jnp.bfloat16
    )
    return (prompt_output, sample_output)


def solution(mesh):
    return jax.shard_map(
        on_device,
        mesh=mesh,
        in_specs=(
            P("smp", "ctx"),
            P("smp", "ctx"),
            P("smp", "ctx"),
            P(),
            P(("ctx", "smp"), None, None),
            P(("ctx", "smp"), None, None),
            P(("ctx", "smp")),
        ),
        out_specs=(P("smp", "ctx"), P(("ctx", "smp"), None, None)),
        check_vma=False,
    )
```

profile of v0, /device:TPU:1, one launch (start us, length us, event | category | flops | bytes accessed | tf_op | source)
XLA Modules:
  0.0 789.8 jit_solution(7252635256761599117)
XLA Ops:
  7.2 1.2 copy.50
  8.4 1.6 copy.51
  10.0 0.1 convert_bitcast_fusion
  10.1 0.1 maximum_bitcast_fusion
  10.2 2.9 copy.52
  13.1 8.6 %all-to-all-start = ((f32[2,256,1,1024]{1,0,2,3:T(2,128)}), f32[2,256,1,1024]{1,0,2,3:T(2,128)S(1)}, u32[]{:S(2)}, u32[]{:S(2)}) async-start(f32[2,256,1,1024]{1,0,2,3:T(2,128)} %copy.52), calls=%async_computation | async-start | bytes 4194304 | tf_op jit(solution)/shard_map/all_to_all | solution.py:82
  21.8 0.2 fusion.66
  22.0 28.1 %all-to-all-done = f32[2,256,1,1024]{1,0,2,3:T(2,128)S(1)} async-done(((f32[2,256,1,1024]{1,0,2,3:T(2,128)}), f32[2,256,1,1024]{1,0,2,3:T(2,128)S(1)}, u32[]{:S(2)}, u32[]{:S(2)}) %all-to-all-start) | async-done | bytes 2097184 | tf_op jit(solution)/shard_map/all_to_all | solution.py:82
  50.1 0.2 copy.53
  50.2 4.3 fusion.42
  54.5 5.4 add_bitcast_fusion
  59.9 1.7 pad_maximum_fusion
  61.6 8.7 %copy.56 = f32[2,2,256,32,64]{2,4,1,0,3:T(8,128)} copy(f32[2,2,256,32,64]{2,3,4,1,0:T(8,128)S(1)} %pad_maximum_fusion) | data formatting | bytes 16777216 | tf_op jit(solution)/shard_map/stack | solution.py:90
  70.2 5.4 all-to-all-start.1
  75.6 0.0 all-gather.6.cloned.1.call-start
  75.7 0.2 fusion.94
  75.9 95.8 %all-to-all-done.1 = f32[2,2,256,32,64]{2,4,1,0,3:T(8,128)} async-done(((f32[2,2,256,32,64]{2,4,1,0,3:T(8,128)}), f32[2,2,256,32,64]{2,4,1,0,3:T(8,128)}, u32[]{:S(2)}, u32[]{:S(2)}) %all-to-all-start.1) | async-done | bytes 8388640 | tf_op jit(solution)/shard_map/all_to_all | solution.py:89
  171.7 4.0 copy.57
  175.7 1.1 fusion.145
  176.9 0.5 copy.58
  177.4 43.2 %fusion.11 = f32[2,256,2,1024]{3,1,2,0:T(8,128)S(1)} fusion(f32[2,256,2,1024]{1,3,2,0:T(8,128)S(1)} %bitcast.129), kind=kOutput, calls=%fused_computation.17 | convolution fusion | flops 12899581952 | bytes 8388608 | tf_op jit(solution)/shard_map/...m,mj->...j/dot_general | solution.py:17
  220.6 0.3 copy.60
  220.9 43.4 %fusion.13 = f32[2,256,2,1024]{3,1,2,0:T(8,128)S(1)} fusion(f32[2,256,2,1024]{1,3,2,0:T(8,128)S(1)} %bitcast.131), kind=kOutput, calls=%fused_computation.19 | convolution fusion | flops 12899581952 | bytes 8388608 | tf_op jit(solution)/shard_map/...m,mj->...j/dot_general | solution.py:17
  264.3 43.3 %fusion.39 = f32[2,256,2,1024]{3,1,2,0:T(8,128)S(1)} fusion(f32[2,256,2,1024]{3,1,2,0:T(8,128)S(1)} %fusion.11, f32[2,256,2,1024]{1,3,2,0:T(8,128)S(1)} %bitcast.132), kind=kOutput, calls=%fused_computation.42 | convolution fusion | flops 12900630528 | bytes 12582912 | tf_op jit(solution)/shard_map/...m,mj->...j/dot_general | solution.py:17
  307.6 43.6 %fusion.36 = f32[2,256,2,1024]{3,1,2,0:T(8,128)S(1)} fusion(f32[2,256,2,1024]{3,1,2,0:T(8,128)S(1)} %fusion.13, f32[2,256,2,1024]{1,3,2,0:T(8,128)S(1)} %bitcast.130), kind=kOutput, calls=%fused_computation.41 | convolution fusion | flops 12900630528 | bytes 12582912 | tf_op jit(solution)/shard_map/...m,mj->...j/dot_general | solution.py:17
  351.2 1.4 multiply_add_fusion
  352.6 23.7 %fusion.5 = f32[256,2,1024]{2,0,1:T(8,128)S(1)} fusion(f32[1,256,2,1024]{3,1,2,0:T(8,128)S(1)} %get-tuple-element.10), kind=kOutput, calls=%fused_computation.11 | convolution fusion | flops 6457131008 | bytes 4194304 | tf_op jit(solution)/shard_map/...m,mj->...j/dot_general | solution.py:17
  376.4 23.8 %fusion.3 = f32[256,2,1024]{2,0,1:T(8,128)S(1)} fusion(f32[1,256,2,1024]{3,1,2,0:T(8,128)S(1)} %get-tuple-element.11), kind=kOutput, calls=%fused_computation.9 | convolution fusion | flops 6457131008 | bytes 4194304 | tf_op jit(solution)/shard_map/...m,mj->...j/dot_general | solution.py:17
  400.1 23.6 %fusion.46 = f32[256,2,1024]{2,0,1:T(8,128)S(1)} fusion(f32[256,2,1024]{2,0,1:T(8,128)S(1)} %fusion.5, f32[1,256,2,1024]{3,1,2,0:T(8,128)S(1)} %get-tuple-element.11), kind=kOutput, calls=%fused_computation.48 | convolution fusion | flops 6457655296 | bytes 6291456 | tf_op jit(solution)/shard_map/...m,mj->...j/dot_general | solution.py:17
  423.8 24.1 %subtract_bitcast_fusion.1 = (f32[1,256,2,1024]{3,1,2,0:T(8,128)S(1)}, f32[1,256,2,1024]{3,1,2,0:T(8,128)S(1)}) fusion(f32[256,2,1024]{2,0,1:T(8,128)S(1)} %fusion.46, f32[2,1024]{1,0:T(2,128)S(1)} %get-tuple-element.19, f32[2,1024]{1,0:T(2,128)S(1)} %get-tuple-element.18, f32[256,2,1024]{2,0,1:T(8,128)S(1)} %fusion.3, ...), kind=kOutput, calls=%fused_computation.36 | convolution fusion | flops 6460801024 | bytes 10502144 | tf_op jit(solution)/shard_map/...m,mj->...j/dot_general | solution.py:17
  447.9 2.3 pad_maximum_fusion.1
  450.2 7.2 copy.64
  457.4 55.3 %all_to_all.51 = f32[2,256,2,1024]{1,2,0,3:T(2,128)S(1)} all-to-all(f32[2,256,2,1024]{1,2,0,3:T(2,128)} %copy.64), channel_id=1, replica_groups=mesh['ctx'=16,'smp'=8] {'ctx'}, dimensions={3} | all-to-all | bytes 8388608 | tf_op jit(solution)/shard_map/all_to_all | solution.py:98
  512.8 0.8 copy.65
  513.6 1.7 fusion.146
  515.3 2.9 copy.66
  518.2 2.7 squeeze.10
  520.9 0.0 copy-start
  521.0 2.8 fusion.71
  523.7 2.9 copy.67
  526.7 2.7 squeeze.11
  529.4 3.1 multiply_bitcast_fusion
  532.5 0.0 copy-start.1
  532.5 1.1 copy-done.1
  533.6 0.7 slice.57
  534.3 0.0 all-gather.6.cloned.1.call-update
  534.3 0.0 all-gather.4.cloned.1.call-start
  534.4 38.2 %all-gather.6.cloned.1.call-done = f32[4096,1,64]{0,1,2:T(1,128)} async-done(((f32[256,1,64]{0,1,2:T(1,128)}), f32[4096,1,64]{0,1,2:T(1,128)}) %all-gather.6.cloned.1.call-update) | async-done | bytes 1048592 | tf_op jit(solution)/shard_map/all_gather | solution.py:61
  572.6 3.7 reduce
  576.3 0.3 copy.80
  576.6 1.7 copy.69
  578.3 0.0 all-gather.4.cloned.1.call-update
  578.3 1.6 copy.68
  579.9 7.0 all-to-all-start.3
  586.9 0.2 copy.49
  587.1 0.1 dynamic_slice.3
  587.2 0.1 iota_compare_fusion
  587.3 27.8 %all-to-all-done.3 = f32[256,16,64]{0,2,1:T(8,128)S(1)} async-done(((f32[256,16,64]{0,2,1:T(8,128)}), f32[256,16,64]{0,2,1:T(8,128)S(1)}, u32[]{:S(2)}, u32[]{:S(2)}) %all-to-all-start.3) | async-done | bytes 1048608 | tf_op jit(solution)/shard_map/all_to_all | solution.py:102
  615.1 0.2 fusion.58
  615.3 1.0 copy.71
  616.3 141.3 %all-gather.4.cloned.1.call-done = f32[8,16,256,64]{2,3,1,0:T(8,128)} async-done(((f32[1,16,256,64]{2,3,1,0:T(8,128)}), f32[8,16,256,64]{2,3,1,0:T(8,128)}) %all-gather.4.cloned.1.call-update) | async-done | bytes 8388624 | tf_op jit(solution)/shard_map/all_gather | solution.py:62
  757.6 9.9 %copy.70 = f32[8,256,16,64]{1,0,3,2:T(8,128)S(1)} copy(f32[8,256,16,64]{1,3,2,0:T(8,128)} %bitcast.127) | data formatting | bytes 16777216 | tf_op jit(solution)/shard_map/transpose | solution.py:107
  767.4 4.1 copy.81
  771.6 11.2 %select_convert_fusion = bf16[2,1024,2048]{2,1,0:T(8,128)(2,1)} fusion(bf16[2,1024,2048]{2,1,0:T(8,128)(2,1)} %param.11, bf16[2,1024,2048]{2,1,0:T(8,128)(2,1)} %param.12, f32[2048]{0:T(1024)S(1)} %copy-done.3, f32[1024,2048]{1,0:T(8,128)S(1)} %bitcast.121, pred[2,1024]{1,0:T(4,128)(4,1)S(1)} %iota_compare_fusion), kind=kLoop, calls=%fused_computation | loop fusion | flops 29360128 | bytes 33564672 | tf_op jit(solution)/shard_map/convert_element_type | solution.py:116
  (11 shorter events, 0.0 us)
Async XLA Ops:
  13.1 36.9 %all-to-all-start = ((f32[2,256,1,1024]{1,0,2,3:T(2,128)}), f32[2,256,1,1024]{1,0,2,3:T(2,128)S(1)}, u32[]{:S(2)}, u32[]{:S(2)}) async-start(f32[2,256,1,1024]{1,0,2,3:T(2,128)} %copy.52), calls=%async_computation | async-start | bytes 4194304 | tf_op jit(solution)/shard_map/all_to_all | solution.py:82
  70.2 101.5 %all-to-all-start.1 = ((f32[2,2,256,32,64]{2,4,1,0,3:T(8,128)}), f32[2,2,256,32,64]{2,4,1,0,3:T(8,128)}, u32[]{:S(2)}, u32[]{:S(2)}) async-start(f32[2,2,256,32,64]{2,4,1,0,3:T(8,128)} %copy.56), calls=%async_computation.1 | async-start | bytes 16777216 | tf_op jit(solution)/shard_map/all_to_all | solution.py:89
  75.6 496.9 %all-gather.6.cloned.1.call-start = ((), (), s32[]{:S(2)}) async-start(), calls=%async_computation.5 | async-start | bytes 1114112 | tf_op jit(solution)/shard_map/all_gather | solution.py:61
  520.9 2.8 copy-start
  532.5 1.1 copy-start.1
  534.3 223.2 %all-gather.4.cloned.1.call-start = ((), (), s32[]{:S(2)}) async-start(), calls=%async_computation.4 | async-start | bytes 9437184 | tf_op jit(solution)/shard_map/all_gather | solution.py:62
  576.3 2.0 slice-start
  578.3 8.6 %copy-start.2 = (bf16[256,1024]{1,0:T(8,128)(2,1)S(1)}, bf16[256,1024]{1,0:T(8,128)(2,1)}, u32[]{:S(2)}) copy-start(bf16[256,1024]{1,0:T(8,128)(2,1)} %param.8) | copy-start | bytes 1572868
  578.3 8.8 %copy-start.3 = (f32[2048]{0:T(1024)S(1)}, f32[2048]{0:T(1024)}, u32[]{:S(2)}) copy-start(f32[2048]{0:T(1024)} %param.10) | copy-start | bytes 24580
  578.3 8.9 %copy-start.4 = (s32[2]{0:T(128)S(1)}, s32[2]{0:T(128)}, u32[]{:S(2)}) copy-start(s32[2]{0:T(128)} %param.13) | copy-start | bytes 28
  579.9 35.2 %all-to-all-start.3 = ((f32[256,16,64]{0,2,1:T(8,128)}), f32[256,16,64]{0,2,1:T(8,128)S(1)}, u32[]{:S(2)}, u32[]{:S(2)}) async-start(f32[256,16,64]{0,2,1:T(8,128)} %copy.68), calls=%async_computation.3 | async-start | bytes 2097152 | tf_op jit(solution)/shard_map/all_to_all | solution.py:102
Sparse Core Ops, SparseCore 0:
  534.4 38.0 all-gather.5
  578.4 179.0 all-gather.3
where the time goes:
time: 794 us; the launch traced here: 790 us
  waiting for transfers between devices  331 us (42%)
  matrix products  284 us (36%)
  local copies, waits for them, and re-layouts  62.1 us (8%)
  blocking collectives  55.3 us (7%)
  other arithmetic  21.3 us (3%)
  starting transfers between devices  21.1 us (3%)
  between operations  14.6 us (2%)
    dot_general x12, matrix products, product_of(): return jnp.einsum(pattern, left, right, precision=lax.Precision.HIGHEST)  284 us
    all_gather x1, waiting for transfers between devices, gather_tail(): return lax.all_gather(partial_tail, 'smp', axis=0, tiled=True)  141 us
    all_to_all x1, waiting for transfers between devices, on_device(): lax.all_to_all(jnp.stack([real_part, imag_part]), 'ctx', split_axis=3, co...  95.8 us
    all_to_all x1, blocking collectives, on_device(): lax.all_to_all(jnp.stack([time_real, time_imag]), 'ctx', split_axis=3, co...  55.3 us
    all_gather x1, waiting for transfers between devices, gather_tail(): lax.all_gather(tail_piece[None, None], 'ctx', axis=1, tiled=True)  38.2 us
    all_to_all x1, waiting for transfers between devices, on_device(): lax.all_to_all(paired.reshape(2, width_dev, 1, span), 'ctx', split_axis=3...  28.1 us
    all_to_all x1, waiting for transfers between devices, on_device(): lax.all_to_all(result[:, :ctx_count], 'ctx', split_axis=1, concat_axis=2,...  27.8 us
  transfers between devices with their start and end apart: 5, of which 5 were waited for; matrix products, arithmetic and copies ran while one was open for 0% of the time, Pallas kernels for 0%

commit v1 on v0

v1 whole, which is shorter than its diff:
```python
import functools

import jax
import jax.numpy as jnp
import numpy as np
from jax import lax
from jax.experimental import pallas as pl
from jax.experimental.pallas import tpu as pltpu
from jax.sharding import PartitionSpec as P

F32 = jnp.float32
BF16 = jnp.bfloat16
R = 128
ROWS = 8
SIDE = 4
AXES = ("ctx", "smp")

FIRST = ((1, 1, 1), (3, 3, 3), (2, 2, 2))
SECOND = ((2, 0, 0), (0, 2, 0), (0, 0, 2))
THIRD = ((1, 0, 0), (0, 1, 0), (0, 0, 1))
HELD_FIRST = ((0, 0, 0),) + FIRST
HELD_SECOND = tuple(
    tuple((a + b) % SIDE for a, b in zip(o, h)) for o in ((0, 0, 0),) + SECOND for h in HELD_FIRST
)


def chip_of(index):
    ctx, smp = divmod(index, 8)
    return ((ctx >> 1 & 1) * 2 + (smp & 1), ctx >> 2, smp >> 1, ctx & 1)


def index_of(x, y, z, core):
    x, y, z = x % SIDE, y % SIDE, z % SIDE
    return ((y * 2 + x // 2) * 2 + core) * 8 + z * 2 + x % 2


def take_from(array, offset, mirrored=False):
    pairs = []
    for index in range(2 * SIDE**3):
        x, y, z, core = chip_of(index)
        sign = -1 if mirrored and core else 1
        source = index_of(x + sign * offset[0], y + sign * offset[1], z + sign * offset[2], core)
        pairs.append((source, index))
    return lax.ppermute(array, AXES, pairs)


def swap_cores(array):
    pairs = []
    for index in range(2 * SIDE**3):
        x, y, z, core = chip_of(index)
        pairs.append((index, index_of(x, y, z, 1 - core)))
    return lax.ppermute(array, AXES, pairs)


def halves(values):
    high = values.astype(BF16)
    return high, (values - high.astype(F32)).astype(BF16)


def np_halves(values):
    values = np.asarray(values, np.float32)
    high = values.astype(jnp.bfloat16)
    low = (values - high.astype(np.float32)).astype(jnp.bfloat16)
    return high, low


@functools.cache
def tables():
    period = R * R
    r = np.arange(R)
    shifted = r + 0.25
    outer = 2 * np.pi * np.outer(shifted, r) / R
    first = np.concatenate([np.cos(outer), -np.sin(outer)], 0)
    inner = 2 * np.pi * (np.outer(r, r) % R) / R
    c, s = np.cos(inner), np.sin(inner)
    second = np.block([[c, -s], [s, c]])
    back = np.block([[c, s], [-s, c]])
    twist = 2 * np.pi * np.outer(shifted, r) / period
    turn = np.stack([np.cos(twist), np.sin(twist)]).astype(np.float32)
    real = np.concatenate([np.cos(outer.T), -np.sin(outer.T)], 1)
    tail = -np.concatenate([np.sin(outer.T), np.cos(outer.T)], 1)[:ROWS]
    last = np.concatenate([real, tail, np.zeros((ROWS, 2 * R))], 0)
    f_hi, f_lo = np_halves(first)
    l_hi, l_lo = np_halves(last)
    return (
        np.concatenate([f_hi, f_lo], 1),
        np.stack(np_halves(second)),
        np.stack(np_halves(back)),
        np.stack([l_hi, l_lo]),
        turn,
        (turn / period).astype(np.float32),
    )


def dot(left, right):
    return jnp.dot(left, right, preferred_element_type=F32)


def spread_kernel(signal_ref, filter_ref, out_ref):
    blocks, _, width = out_ref.shape[:3]
    for k in range(blocks):
        rows = pl.ds(k * width, width)
        for r in range(ROWS):
            cols = pl.ds(r * R, R)
            out_ref[k, 0, :, r, :] = signal_ref[rows, cols].astype(F32)
            out_ref[k, 1, :, r, :] = filter_ref[rows, cols]


def conv_kernel(
    base_ref, skip_ref, in_ref, first_ref, second_ref, back_ref, last_ref, turn_ref, unturn_ref, out_ref, tail_ref
):
    ctx_count = in_ref.shape[0]
    width = in_ref.shape[2]
    f_both = first_ref[...]
    f_hi = first_ref[:, :R]

    def two(pair, carry):
        chans = [2 * pair, 2 * pair + 1]
        signal = [in_ref[:, 0, c].reshape(R, R) for c in chans]
        taps = [in_ref[:, 1, c].reshape(R, R) for c in chans]
        x = jnp.concatenate(signal, 1).astype(BF16)
        h_hi, h_lo = halves(jnp.concatenate(taps, 1))
        xs = dot(f_both, jnp.concatenate([x, x], 0))
        hs = dot(f_both, jnp.concatenate([h_hi, h_hi], 0)) + dot(f_hi, h_lo)
        cos, sin = turn_ref[0], turn_ref[1]
        rows = []
        for spec in (xs, hs):
            for k in range(2):
                re, im = spec[:R, k * R : (k + 1) * R], spec[R:, k * R : (k + 1) * R]
                rows.append(jnp.concatenate([re * cos + im * sin, im * cos - re * sin], 1))
        hi, lo = halves(jnp.concatenate(rows, 0))
        spectra = dot(hi, second_ref[0]) + dot(lo, second_ref[0]) + dot(hi, second_ref[1])
        prods = []
        for k in range(2):
            xr, xi = spectra[k * R : (k + 1) * R, :R], spectra[k * R : (k + 1) * R, R:]
            hr, hi_ = spectra[(2 + k) * R : (3 + k) * R, :R], spectra[(2 + k) * R : (3 + k) * R, R:]
            prods.append(jnp.concatenate([xr * hr - xi * hi_, xr * hi_ + xi * hr], 1))
        hi, lo = halves(jnp.concatenate(prods, 0))
        timed = dot(hi, back_ref[0]) + dot(lo, back_ref[0]) + dot(hi, back_ref[1])
        cos, sin = unturn_ref[0], unturn_ref[1]
        cols = []
        for k in range(2):
            re, im = timed[k * R : (k + 1) * R, :R], timed[k * R : (k + 1) * R, R:]
            cols.append(jnp.concatenate([re * cos - im * sin, re * sin + im * cos], 0))
        hi, lo = halves(jnp.concatenate(cols, 1))
        result = dot(last_ref[0], hi) + dot(last_ref[0], lo) + dot(last_ref[1], hi)
        for k in range(2):
            skip = skip_ref[base_ref[0] + chans[k]]
            conv = result[:R, k * R : (k + 1) * R] + skip * signal[k]
            out_ref[:, chans[k]] = conv.reshape(ctx_count, ROWS, R)
            tail_ref[chans[k]] = result[R : R + ROWS, k * R : (k + 1) * R]
        return carry

    lax.fori_loop(0, width // 2, two, 0)


def finish_kernel(conv_ref, gate_ref, out_ref):
    blocks, width = conv_ref.shape[:2]
    for k in range(blocks):
        rows = pl.ds(k * width, width)
        for r in range(ROWS):
            cols = pl.ds(r * R, R)
            out_ref[rows, cols] = (gate_ref[rows, cols].astype(F32) * conv_ref[k, :, r, :]).astype(BF16)


def sample_kernel(
    place_ref, lengths_ref, skip_ref, input_ref, gate_ref, *rest
):
    pieces, (out_ref, tail_ref, sem) = rest[:8], rest[8:]
    step = pl.program_id(0)
    width = 16

    @pl.when(step == 0)
    def _():
        for array, piece_ref in enumerate(pieces):
            other, part = divmod(array, 4)
            core = place_ref[3] if other == 0 else 1 - place_ref[3]
            sign = 1 - 2 * core
            extra = (0, 0, 0) if part == 0 else THIRD[part - 1]
            for slot, held in enumerate(HELD_SECOND):
                x, y, z = [
                    (place_ref[i] + held[i] + sign * extra[i] + SIDE) % SIDE for i in range(3)
                ]
                channel = (z * 2 + x % 2) * 256 + core * 128 + (y * 2 + x // 2) * width
                copy = pltpu.make_async_copy(
                    piece_ref.at[pl.ds(slot * width, width)],
                    tail_ref.at[pl.ds(pl.multiple_of(channel, width), width)],
                    sem,
                )
                copy.start()
        pltpu.make_async_copy(tail_ref, tail_ref, sem).wait()

    positions = step * R + lax.broadcasted_iota(jnp.int32, (R, 1), 0)
    for block in range(tail_ref.shape[0] // R):
        cols = pl.ds(block * R, R)
        state = tail_ref[cols, step, :].T
        for i in range(input_ref.shape[0]):
            blended = gate_ref[i, :, cols].astype(F32) * (
                state + skip_ref[:, cols] * input_ref[i, :, cols].astype(F32)
            )
            out_ref[i, :, cols] = jnp.where(positions < lengths_ref[i], blended, 0.0).astype(BF16)


VMEM = pl.BlockSpec(memory_space=pltpu.VMEM)
SMEM = pl.BlockSpec(memory_space=pltpu.SMEM)


def on_device(prompt_input, prompt_gate, filters, skip, sample_input, sample_gate, lengths):
    width_dev, span = prompt_input.shape
    ctx_count = 16
    width = width_dev // ctx_count
    ctx, smp = lax.axis_index("ctx"), lax.axis_index("smp")
    core = ctx % 2
    place = jnp.stack([(ctx // 2 % 2) * 2 + smp % 2, ctx // 4, smp // 2, core]).astype(jnp.int32)
    base = (smp * width_dev + (core * 8 + ctx // 2) * width).astype(jnp.int32).reshape(1)

    spread = pl.pallas_call(
        spread_kernel,
        grid=(ctx_count,),
        in_specs=[pl.BlockSpec((width, span), lambda k: (k % 2 * 8 + k // 2, 0))] * 2,
        out_specs=pl.BlockSpec((1, 2, width, ROWS, R), lambda k: (k, 0, 0, 0, 0)),
        out_shape=jax.ShapeDtypeStruct((ctx_count, 2, width, ROWS, R), F32),
        name="spread",
    )(prompt_input, filters)
    regrouped = lax.all_to_all(spread, "ctx", split_axis=0, concat_axis=0, tiled=True)

    convolved, tail = pl.pallas_call(
        conv_kernel,
        in_specs=[SMEM, SMEM] + [VMEM] * 7,
        out_specs=[VMEM, VMEM],
        out_shape=[
            jax.ShapeDtypeStruct((ctx_count, width, ROWS, R), F32),
            jax.ShapeDtypeStruct((width, ROWS, R), F32),
        ],
        compiler_params=pltpu.CompilerParams(vmem_limit_bytes=40 * 2**20),
        name="conv",
    )(base, skip, regrouped, *tables())

    held = jnp.concatenate([tail] + [take_from(tail, o) for o in FIRST], 0)
    held = jnp.concatenate([held] + [take_from(held, o) for o in SECOND], 0)
    mine = [held] + [take_from(held, o, mirrored=True) for o in THIRD]
    other = [swap_cores(part) for part in mine]

    returned = lax.all_to_all(convolved, "ctx", split_axis=0, concat_axis=0, tiled=True)
    prompt_output = pl.pallas_call(
        finish_kernel,
        grid=(ctx_count,),
        in_specs=[
            pl.BlockSpec((1, width, ROWS, R), lambda k: (k, 0, 0, 0)),
            pl.BlockSpec((width, span), lambda k: (k % 2 * 8 + k // 2, 0)),
        ],
        out_specs=pl.BlockSpec((width, span), lambda k: (k % 2 * 8 + k // 2, 0)),
        out_shape=jax.ShapeDtypeStruct((width_dev, span), BF16),
        name="finish",
    )(returned, prompt_gate)

    local, length, channels = sample_input.shape
    block = pl.BlockSpec((local, R, channels), lambda j: (0, j, 0))
    sample_output = pl.pallas_call(
        sample_kernel,
        grid=(length // R,),
        in_specs=[SMEM, SMEM, pl.BlockSpec((1, channels), lambda j: (0, 0)), block, block]
        + [pl.BlockSpec(memory_space=pl.ANY)] * 8,
        out_specs=block,
        out_shape=jax.ShapeDtypeStruct(sample_input.shape, BF16),
        scratch_shapes=[
            pltpu.VMEM((channels, ROWS, R), F32),
            pltpu.SemaphoreType.DMA,
        ],
        compiler_params=pltpu.CompilerParams(vmem_limit_bytes=40 * 2**20),
        name="samples",
    )(place, lengths, skip.reshape(1, channels), sample_input, sample_gate, *mine, *other)
    return prompt_output, sample_output


def solution(mesh):
    return jax.shard_map(
        on_device,
        mesh=mesh,
        in_specs=(
            P("smp", "ctx"),
            P("smp", "ctx"),
            P("smp", "ctx"),
            P(),
            P(("ctx", "smp"), None, None),
            P(("ctx", "smp"), None, None),
            P(("ctx", "smp")),
        ),
        out_specs=(P("smp", "ctx"), P(("ctx", "smp"), None, None)),
        check_vma=False,
    )
```

time: 794 us -> 167 us (0.21)
  matrix products: 284 us -> 0 us
  waiting for transfers between devices: 331 us -> 58.9 us
  blocking collectives: 55.3 us -> 0 us
  local copies, waits for them, and re-layouts: 62.1 us -> 7.29 us
  Pallas kernels: 0 us -> 52 us
  starting transfers between devices: 21.1 us -> 46.6 us
  other arithmetic: 21.3 us -> 0.08 us
  between operations: 14.6 us -> 0.81 us
    dot_general x12 -> x0, matrix products: 284 us -> none  [product_of(): return jnp.einsum(pattern, left, right, precision=lax.Precision.HIGHEST)]
    all_gather x2 -> x0, waiting for transfers between devices: 179 us -> none  [the longest x1 141 us: gather_tail(): return lax.all_gather(partial_tail, 'smp', axis=0, tiled=True)]
    all_to_all x3 -> x2, waiting for transfers between devices: 152 us -> 45.6 us  [the longest x1 28.5 us: on_device(): lax.all_to_all(spread, 'ctx', split_axis=0, concat_axis=0, tiled=True)]
    all_to_all x1 -> x0, blocking collectives: 55.3 us -> none  [on_device(): lax.all_to_all(jnp.stack([time_real, time_imag]), 'ctx', split_axis=3, co...]
    pallas_call x0 -> x4, Pallas kernels: none -> 52 us  [the longest x1 22.6 us: on_device(): pl.pallas_call(sample_kernel, grid=(length // R,), in_specs=[SMEM, SMEM,...]
    ppermute x0 -> x13, starting transfers between devices: none -> 33.9 us  [the longest x9 18.7 us: take_from(): return lax.ppermute(array, AXES, pairs)]
    another operation x2 -> x0, local copies, waits for them, and re-layouts: 15.9 us -> none  [the longest x1 8.66 us: on_device(): jnp.stack([real_part, imag_part])]
    ppermute x0 -> x13, waiting for transfers between devices: none -> 13.2 us  [the longest x9 13.2 us: take_from(): return lax.ppermute(array, AXES, pairs)]
  transfers between devices with their start and end apart: 5 -> 15, of which waited for: 5 -> 8; matrix products, arithmetic and copies ran while one was open for 0% -> 0% of each run, Pallas kernels for 0% -> 5%
where the time goes in v1:
time: 167 us; the launch traced here: 166 us
  waiting for transfers between devices  58.9 us (35%)
  Pallas kernels  52 us (31%)
  starting transfers between devices  46.6 us (28%)
  local copies, waits for them, and re-layouts  7.29 us (4%)
    all_to_all x1, waiting for transfers between devices, on_device(): lax.all_to_all(spread, 'ctx', split_axis=0, concat_axis=0, tiled=True)  28.5 us
    pallas_call x1, Pallas kernels, on_device(): pl.pallas_call(sample_kernel, grid=(length // R,), in_specs=[SMEM, SMEM,...  22.6 us
    ppermute x9, starting transfers between devices, take_from(): return lax.ppermute(array, AXES, pairs)  18.7 us
    all_to_all x1, waiting for transfers between devices, on_device(): lax.all_to_all(convolved, 'ctx', split_axis=0, concat_axis=0, tiled=True)  17.2 us
    ppermute x4, starting transfers between devices, swap_cores(): return lax.ppermute(array, AXES, pairs)  15.2 us
    ppermute x9, waiting for transfers between devices, take_from(): return lax.ppermute(array, AXES, pairs)  13.2 us
    pallas_call x1, Pallas kernels, on_device(): pl.pallas_call(conv_kernel, in_specs=[SMEM, SMEM] + [VMEM] * 7, out_specs...  10.7 us
    pallas_call x1, Pallas kernels, on_device(): pl.pallas_call(spread_kernel, grid=(ctx_count,), in_specs=[pl.BlockSpec((...  9.6 us
  transfers between devices with their start and end apart: 15, of which 8 were waited for; matrix products, arithmetic and copies ran while one was open for 0% of the time, Pallas kernels for 5%

profile of v1, /device:TPU:1, one launch (start us, length us, event | category | flops | bytes accessed | tf_op | source)
XLA Modules:
  0.0 165.6 jit_solution(14450177107481731067)
XLA Ops:
  0.6 0.0 copy-start.8
  0.6 0.0 copy-start.9
  0.7 9.6 %spread.1 = f32[16,2,16,8,128]{4,3,2,1,0:T(8,128)} custom-call(bf16[256,1024]{1,0:T(8,128)(2,1)} %signal_ref.1, f32[256,1024]{1,0:T(8,128)} %filter_ref.1), custom_call_target="tpu_custom_call" | custom-call | tf_op jit(solution)/shard_map/spread/pallas_call | solution.py:217
  10.3 8.4 %all-to-all-start = ((f32[16,2,16,8,128]{4,3,2,1,0:T(8,128)}), f32[16,2,16,8,128]{4,3,2,1,0:T(8,128)S(1)}, u32[]{:S(2)}, u32[]{:S(2)}) async-start(f32[16,2,16,8,128]{4,3,2,1,0:T(8,128)} %spread.1), calls=%async_computation | async-start | bytes 4194304 | tf_op jit(solution)/shard_map/all_to_all | solution.py:225
  18.7 28.5 %all-to-all-done.in_ref = f32[16,2,16,8,128]{4,3,2,1,0:T(8,128)S(1)} async-done(((f32[16,2,16,8,128]{4,3,2,1,0:T(8,128)}), f32[16,2,16,8,128]{4,3,2,1,0:T(8,128)S(1)}, u32[]{:S(2)}, u32[]{:S(2)}) %all-to-all-start) | async-done | bytes 2097184 | tf_op jit(solution)/shard_map/all_to_all | solution.py:225
  47.2 0.0 copy-start.1
  47.2 0.9 copy-done.1
  48.1 0.0 copy-start.2
  48.1 0.9 copy-done.2
  49.1 0.0 copy-start.3
  49.1 0.9 copy-done.3
  50.0 0.0 copy-start.4
  50.0 0.9 copy-done.4
  50.9 0.0 copy-start.5
  50.9 0.9 copy-done.5
  51.8 0.0 copy-start.6
  51.8 0.9 copy-done.6
  52.7 0.0 copy-start.7
  52.7 0.7 copy-done.7
  53.4 10.7 %conv.1 = (f32[16,16,8,128]{3,2,1,0:T(8,128)S(1)}, f32[16,8,128]{2,1,0:T(8,128)S(1)}) custom-call(s32[1]{0:T(128)} %bitcast.base_ref, f32[2048]{0:T(1024)S(1)} %copy-done.7, f32[16,2,16,8,128]{4,3,2,1,0:T(8,128)S(1)} %all-to-all-done.in_ref, bf16[256,256]{1,0:T(8,128)(2,1)S(1)} %copy-done.6, bf16[2,256,256]{2,1,0:T(8,128)(2,1)S(1)} %copy-done.2, ...), custom_call_target="tpu_custom_call" | custom-call | tf_op jit(solution)/shard_map/conv/pallas_call | solution.py:227
  64.1 0.0 copy-start
  64.2 1.0 copy-done
  65.1 5.0 %collective-permute-start.2 = (f32[16,8,128]{2,1,0:T(8,128)S(1)}, f32[16,8,128]{2,1,0:T(8,128)S(1)}, u32[]{:S(2)}, u32[]{:S(2)}) collective-permute-start(f32[16,8,128]{2,1,0:T(8,128)S(1)} %get-tuple-element.5), channel_id=1, source_target_pairs={{84,0},{85,1},{86,2},{87,3},{80,4},{81,5},{82,6},{83,7},{92,8},{93... | collective-permute-start | bytes 196616 | tf_op jit(solution)/shard_map/ppermute | solution.py:44
  70.2 0.1 collective-permute-start.1
  70.2 6.8 %collective-permute-start = (f32[16,8,128]{2,1,0:T(8,128)S(1)}, f32[16,8,128]{2,1,0:T(8,128)S(1)}, u32[]{:S(2)}, u32[]{:S(2)}) collective-permute-start(f32[16,8,128]{2,1,0:T(8,128)S(1)} %get-tuple-element.5), channel_id=1, source_target_pairs={{35,0},{50,1},{37,2},{52,3},{39,4},{54,5},{33,6},{48,7},{43,8},{58... | collective-permute-start | bytes 196616 | tf_op jit(solution)/shard_map/ppermute | solution.py:44
  77.1 1.3 collective-permute-done
  78.4 0.3 collective-permute-done.1
  78.7 0.0 collective-permute-done.2
  78.7 0.7 collective-permute-start.3
  79.4 2.4 %collective-permute-start.4 = (f32[64,8,128]{2,1,0:T(8,128)S(1)}, f32[64,8,128]{2,1,0:T(8,128)S(1)}, u32[]{:S(2)}, u32[]{:S(2)}) collective-permute-start(f32[64,8,128]{2,1,0:T(8,128)S(1)} %get-tuple-element.6), channel_id=1, source_target_pairs={{64,0},{65,1},{66,2},{67,3},{68,4},{69,5},{70,6},{71,7},{72,8},{73... | collective-permute-start | bytes 786440 | tf_op jit(solution)/shard_map/ppermute | solution.py:44
  81.8 0.7 collective-permute-start.5
  82.4 3.5 %collective-permute-done.3 = f32[64,8,128]{2,1,0:T(8,128)S(1)} collective-permute-done((f32[64,8,128]{2,1,0:T(8,128)S(1)}, f32[64,8,128]{2,1,0:T(8,128)S(1)}, u32[]{:S(2)}, u32[]{:S(2)}) %collective-permute-start.3) | collective-permute-done | bytes 262176 | tf_op jit(solution)/shard_map/ppermute | solution.py:44
  86.0 0.4 collective-permute-done.4
  86.4 2.3 %collective-permute-done.5 = f32[64,8,128]{2,1,0:T(8,128)S(1)} collective-permute-done((f32[64,8,128]{2,1,0:T(8,128)S(1)}, f32[64,8,128]{2,1,0:T(8,128)S(1)}, u32[]{:S(2)}, u32[]{:S(2)}) %collective-permute-start.5) | collective-permute-done | bytes 262176 | tf_op jit(solution)/shard_map/ppermute | solution.py:44
  88.8 0.2 collective-permute-start.8
  89.0 1.4 collective-permute-start.7
  90.5 1.4 collective-permute-start.6
  91.9 6.7 %collective-permute-start.9 = (f32[256,8,128]{2,1,0:T(8,128)S(1)}, f32[256,8,128]{2,1,0:T(8,128)}, u32[]{:S(2)}, u32[]{:S(2)}) collective-permute-start(f32[256,8,128]{2,1,0:T(8,128)S(1)} %constant_dynamic-update-slice_fusion.4.rest_0_), channel_id=1, source_target_pairs={{0,8},{1,9},{2,10},{3,11},{4,12},{5,13},{6,14},{7,15},{8,0},{9,1},... | collective-permute-start | bytes 3145736 | tf_op jit(solution)/shard_map/ppermute | solution.py:52
  98.6 5.3 %collective-permute-done.8.rest_3_ = f32[256,8,128]{2,1,0:T(8,128)S(1)} collective-permute-done((f32[256,8,128]{2,1,0:T(8,128)S(1)}, f32[256,8,128]{2,1,0:T(8,128)S(1)}, u32[]{:S(2)}, u32[]{:S(2)}) %collective-permute-start.8) | collective-permute-done | bytes 1048608 | tf_op jit(solution)/shard_map/ppermute | solution.py:44
  103.9 4.5 %collective-permute-start.12 = (f32[256,8,128]{2,1,0:T(8,128)S(1)}, f32[256,8,128]{2,1,0:T(8,128)}, u32[]{:S(2)}, u32[]{:S(2)}) collective-permute-start(f32[256,8,128]{2,1,0:T(8,128)S(1)} %collective-permute-done.8.rest_3_), channel_id=1, source_target_pairs={{0,8},{1,9},{2,10},{3,11},{4,12},{5,13},{6,14},{7,15},{8,0},{9,1},... | collective-permute-start | bytes 3145736 | tf_op jit(solution)/shard_map/ppermute | solution.py:52
  108.4 0.0 collective-permute-done.7.rest_2_
  108.4 2.5 %collective-permute-start.11 = (f32[256,8,128]{2,1,0:T(8,128)S(1)}, f32[256,8,128]{2,1,0:T(8,128)}, u32[]{:S(2)}, u32[]{:S(2)}) collective-permute-start(f32[256,8,128]{2,1,0:T(8,128)S(1)} %collective-permute-done.7.rest_2_), channel_id=1, source_target_pairs={{0,8},{1,9},{2,10},{3,11},{4,12},{5,13},{6,14},{7,15},{8,0},{9,1},... | collective-permute-start | bytes 3145736 | tf_op jit(solution)/shard_map/ppermute | solution.py:52
  110.8 0.0 collective-permute-done.6.rest_1_
  110.8 1.5 collective-permute-start.10
  112.4 4.2 %all-to-all-start.1 = ((f32[16,16,8,128]{3,2,1,0:T(8,128)}), f32[16,16,8,128]{3,2,1,0:T(8,128)}, u32[]{:S(2)}, u32[]{:S(2)}) async-start(f32[16,16,8,128]{3,2,1,0:T(8,128)} %copy-done), calls=%async_computation.1 | async-start | bytes 2097152 | tf_op jit(solution)/shard_map/all_to_all | solution.py:244
  116.7 0.1 pad_add_fusion.place_ref
  116.7 17.2 %all-to-all-done.1.conv_ref = f32[16,16,8,128]{3,2,1,0:T(8,128)} async-done(((f32[16,16,8,128]{3,2,1,0:T(8,128)}), f32[16,16,8,128]{3,2,1,0:T(8,128)}, u32[]{:S(2)}, u32[]{:S(2)}) %all-to-all-start.1) | async-done | bytes 1048608 | tf_op jit(solution)/shard_map/all_to_all | solution.py:244
  133.9 9.0 %finish.1 = bf16[256,1024]{1,0:T(8,128)(2,1)} custom-call(f32[16,16,8,128]{3,2,1,0:T(8,128)} %all-to-all-done.1.conv_ref, bf16[256,1024]{1,0:T(8,128)(2,1)} %gate_ref.2), custom_call_target="tpu_custom_call" | custom-call | tf_op jit(solution)/shard_map/finish/pallas_call | solution.py:245
  142.9 0.0 collective-permute-done.9.rest_4_
  142.9 0.0 collective-permute-done.12.rest_7_
  142.9 0.0 collective-permute-done.11.rest_6_
  143.0 0.0 collective-permute-done.10.rest_5_
  143.0 0.0 copy-done.8
  143.0 0.0 copy-done.9
  143.0 22.6 %samples.1 = bf16[2,1024,2048]{2,1,0:T(8,128)(2,1)} custom-call(s32[4]{0:T(128)S(1)} %pad_add_fusion.place_ref, s32[2]{0:T(128)S(1)} %copy-done.9, f32[1,2048]{1,0:T(1,128)S(1)} %bitcast.6, bf16[2,1024,2048]{2,1,0:T(8,128)(2,1)} %input_ref.1, bf16[2,1024,2048]{2,1,0:T(8,128)(2,1)} %gate_ref.3, ...), custom_call_target="tpu_custom_call" | custom-call | tf_op jit(solution)/shard_map/samples/pallas_call | solution.py:259
  (7 shorter events, 0.1 us)
Async XLA Ops:
  0.6 142.3 %copy-start.8 = (f32[2048]{0:T(1024)S(1)}, f32[2048]{0:T(1024)}, u32[]{:S(2)}) copy-start(f32[2048]{0:T(1024)} %skip_ref.1) | copy-start | bytes 24580
  0.6 142.3 %copy-start.9 = (s32[2]{0:T(128)S(1)}, s32[2]{0:T(128)}, u32[]{:S(2)}) copy-start(s32[2]{0:T(128)} %lengths_ref.1) | copy-start | bytes 28
  10.3 36.9 %all-to-all-start = ((f32[16,2,16,8,128]{4,3,2,1,0:T(8,128)}), f32[16,2,16,8,128]{4,3,2,1,0:T(8,128)S(1)}, u32[]{:S(2)}, u32[]{:S(2)}) async-start(f32[16,2,16,8,128]{4,3,2,1,0:T(8,128)} %spread.1), calls=%async_computation | async-start | bytes 4194304 | tf_op jit(solution)/shard_map/all_to_all | solution.py:225
  47.2 1.0 copy-start.1
  48.1 0.9 copy-start.2
  49.1 0.9 copy-start.3
  50.0 0.9 copy-start.4
  50.9 0.9 copy-start.5
  51.8 0.9 copy-start.6
  52.7 0.7 copy-start.7
  64.1 1.0 copy-start
  65.1 13.6 %collective-permute-start.2 = (f32[16,8,128]{2,1,0:T(8,128)S(1)}, f32[16,8,128]{2,1,0:T(8,128)S(1)}, u32[]{:S(2)}, u32[]{:S(2)}) collective-permute-start(f32[16,8,128]{2,1,0:T(8,128)S(1)} %get-tuple-element.5), channel_id=1, source_target_pairs={{84,0},{85,1},{86,2},{87,3},{80,4},{81,5},{82,6},{83,7},{92,8},{93... | collective-permute-start | bytes 196616 | tf_op jit(solution)/shard_map/ppermute | solution.py:44
  70.2 8.5 %collective-permute-start.1 = (f32[16,8,128]{2,1,0:T(8,128)S(1)}, f32[16,8,128]{2,1,0:T(8,128)S(1)}, u32[]{:S(2)}, u32[]{:S(2)}) collective-permute-start(f32[16,8,128]{2,1,0:T(8,128)S(1)} %get-tuple-element.5), channel_id=1, source_target_pairs={{119,0},{102,1},{113,2},{96,3},{115,4},{98,5},{117,6},{100,7},{127... | collective-permute-start | bytes 196616 | tf_op jit(solution)/shard_map/ppermute | solution.py:44
  70.2 8.2 %collective-permute-start = (f32[16,8,128]{2,1,0:T(8,128)S(1)}, f32[16,8,128]{2,1,0:T(8,128)S(1)}, u32[]{:S(2)}, u32[]{:S(2)}) collective-permute-start(f32[16,8,128]{2,1,0:T(8,128)S(1)} %get-tuple-element.5), channel_id=1, source_target_pairs={{35,0},{50,1},{37,2},{52,3},{39,4},{54,5},{33,6},{48,7},{43,8},{58... | collective-permute-start | bytes 196616 | tf_op jit(solution)/shard_map/ppermute | solution.py:44
  78.7 7.2 %collective-permute-start.3 = (f32[64,8,128]{2,1,0:T(8,128)S(1)}, f32[64,8,128]{2,1,0:T(8,128)S(1)}, u32[]{:S(2)}, u32[]{:S(2)}) collective-permute-start(f32[64,8,128]{2,1,0:T(8,128)S(1)} %get-tuple-element.6), channel_id=1, source_target_pairs={{16,0},{17,1},{18,2},{19,3},{20,4},{21,5},{22,6},{23,7},{24,8},{25... | collective-permute-start | bytes 786440 | tf_op jit(solution)/shard_map/ppermute | solution.py:44
  79.4 7.0 %collective-permute-start.4 = (f32[64,8,128]{2,1,0:T(8,128)S(1)}, f32[64,8,128]{2,1,0:T(8,128)S(1)}, u32[]{:S(2)}, u32[]{:S(2)}) collective-permute-start(f32[64,8,128]{2,1,0:T(8,128)S(1)} %get-tuple-element.6), channel_id=1, source_target_pairs={{64,0},{65,1},{66,2},{67,3},{68,4},{69,5},{70,6},{71,7},{72,8},{73... | collective-permute-start | bytes 786440 | tf_op jit(solution)/shard_map/ppermute | solution.py:44
  81.8 7.0 %collective-permute-start.5 = (f32[64,8,128]{2,1,0:T(8,128)S(1)}, f32[64,8,128]{2,1,0:T(8,128)S(1)}, u32[]{:S(2)}, u32[]{:S(2)}) collective-permute-start(f32[64,8,128]{2,1,0:T(8,128)S(1)} %get-tuple-element.6), channel_id=1, source_target_pairs={{4,0},{5,1},{6,2},{7,3},{0,4},{1,5},{2,6},{3,7},{12,8},{13,9},{14,... | collective-permute-start | bytes 786440 | tf_op jit(solution)/shard_map/ppermute | solution.py:44
  88.8 15.1 %collective-permute-start.8 = (f32[256,8,128]{2,1,0:T(8,128)S(1)}, f32[256,8,128]{2,1,0:T(8,128)S(1)}, u32[]{:S(2)}, u32[]{:S(2)}) collective-permute-start(f32[256,8,128]{2,1,0:T(8,128)S(1)} %constant_dynamic-update-slice_fusion.4.rest_0_), channel_id=1, source_target_pairs={{2,0},{3,1},{4,2},{5,3},{6,4},{7,5},{0,6},{1,7},{14,8},{15,9},{8,1... | collective-permute-start | bytes 3145736 | tf_op jit(solution)/shard_map/ppermute | solution.py:44
  89.0 19.3 %collective-permute-start.7 = (f32[256,8,128]{2,1,0:T(8,128)S(1)}, f32[256,8,128]{2,1,0:T(8,128)S(1)}, u32[]{:S(2)}, u32[]{:S(2)}) collective-permute-start(f32[256,8,128]{2,1,0:T(8,128)S(1)} %constant_dynamic-update-slice_fusion.4.rest_0_), channel_id=1, source_target_pairs={{32,0},{33,1},{34,2},{35,3},{36,4},{37,5},{38,6},{39,7},{104,8},{1... | collective-permute-start | bytes 3145736 | tf_op jit(solution)/shard_map/ppermute | solution.py:44
  90.5 20.4 %collective-permute-start.6 = (f32[256,8,128]{2,1,0:T(8,128)S(1)}, f32[256,8,128]{2,1,0:T(8,128)}, u32[]{:S(2)}, u32[]{:S(2)}) collective-permute-start(f32[256,8,128]{2,1,0:T(8,128)S(1)} %constant_dynamic-update-slice_fusion.4.rest_0_), channel_id=1, source_target_pairs={{1,0},{16,1},{3,2},{18,3},{5,4},{20,5},{7,6},{22,7},{25,8},{8,9},{... | collective-permute-start | bytes 3145736 | tf_op jit(solution)/shard_map/ppermute | solution.py:44
  91.9 51.0 %collective-permute-start.9 = (f32[256,8,128]{2,1,0:T(8,128)S(1)}, f32[256,8,128]{2,1,0:T(8,128)}, u32[]{:S(2)}, u32[]{:S(2)}) collective-permute-start(f32[256,8,128]{2,1,0:T(8,128)S(1)} %constant_dynamic-update-slice_fusion.4.rest_0_), channel_id=1, source_target_pairs={{0,8},{1,9},{2,10},{3,11},{4,12},{5,13},{6,14},{7,15},{8,0},{9,1},... | collective-permute-start | bytes 3145736 | tf_op jit(solution)/shard_map/ppermute | solution.py:52
  103.9 39.0 %collective-permute-start.12 = (f32[256,8,128]{2,1,0:T(8,128)S(1)}, f32[256,8,128]{2,1,0:T(8,128)}, u32[]{:S(2)}, u32[]{:S(2)}) collective-permute-start(f32[256,8,128]{2,1,0:T(8,128)S(1)} %collective-permute-done.8.rest_3_), channel_id=1, source_target_pairs={{0,8},{1,9},{2,10},{3,11},{4,12},{5,13},{6,14},{7,15},{8,0},{9,1},... | collective-permute-start | bytes 3145736 | tf_op jit(solution)/shard_map/ppermute | solution.py:52
  108.4 34.6 %collective-permute-start.11 = (f32[256,8,128]{2,1,0:T(8,128)S(1)}, f32[256,8,128]{2,1,0:T(8,128)}, u32[]{:S(2)}, u32[]{:S(2)}) collective-permute-start(f32[256,8,128]{2,1,0:T(8,128)S(1)} %collective-permute-done.7.rest_2_), channel_id=1, source_target_pairs={{0,8},{1,9},{2,10},{3,11},{4,12},{5,13},{6,14},{7,15},{8,0},{9,1},... | collective-permute-start | bytes 3145736 | tf_op jit(solution)/shard_map/ppermute | solution.py:52
  110.8 32.1 %collective-permute-start.10 = (f32[256,8,128]{2,1,0:T(8,128)}, f32[256,8,128]{2,1,0:T(8,128)}, u32[]{:S(2)}, u32[]{:S(2)}) collective-permute-start(f32[256,8,128]{2,1,0:T(8,128)} %collective-permute-done.6.rest_1_), channel_id=1, source_target_pairs={{0,8},{1,9},{2,10},{3,11},{4,12},{5,13},{6,14},{7,15},{8,0},{9,1},... | collective-permute-start | bytes 3145736 | tf_op jit(solution)/shard_map/ppermute | solution.py:52
  112.4 21.5 %all-to-all-start.1 = ((f32[16,16,8,128]{3,2,1,0:T(8,128)}), f32[16,16,8,128]{3,2,1,0:T(8,128)}, u32[]{:S(2)}, u32[]{:S(2)}) async-start(f32[16,16,8,128]{3,2,1,0:T(8,128)} %copy-done), calls=%async_computation.1 | async-start | bytes 2097152 | tf_op jit(solution)/shard_map/all_to_all | solution.py:244

commit v2 on v1

v2 whole, which is shorter than its diff:
```python
import functools

import jax
import jax.numpy as jnp
import numpy as np
from jax import lax
from jax.experimental import pallas as pl
from jax.experimental.pallas import tpu as pltpu
from jax.sharding import PartitionSpec as P

F32 = jnp.float32
BF16 = jnp.bfloat16
R = 128
ROWS = 8
SIDE = 4
AXES = ("ctx", "smp")

FIRST = ((1, 1, 1), (3, 3, 3), (2, 2, 2))
SECOND = ((2, 0, 0), (0, 2, 0), (0, 0, 2))
THIRD = ((1, 0, 0), (0, 1, 0), (0, 0, 1))
HELD_FIRST = ((0, 0, 0),) + FIRST
HELD_SECOND = tuple(
    tuple((a + b) % SIDE for a, b in zip(o, h)) for o in ((0, 0, 0),) + SECOND for h in HELD_FIRST
)


def chip_of(index):
    ctx, smp = divmod(index, 8)
    return ((ctx >> 1 & 1) * 2 + (smp & 1), ctx >> 2, smp >> 1, ctx & 1)


def index_of(x, y, z, core):
    x, y, z = x % SIDE, y % SIDE, z % SIDE
    return ((y * 2 + x // 2) * 2 + core) * 8 + z * 2 + x % 2


def take_from(array, offset, mirrored=False):
    pairs = []
    for index in range(2 * SIDE**3):
        x, y, z, core = chip_of(index)
        sign = -1 if mirrored and core else 1
        source = index_of(x + sign * offset[0], y + sign * offset[1], z + sign * offset[2], core)
        pairs.append((source, index))
    return lax.ppermute(array, AXES, pairs)


def swap_cores(array):
    pairs = []
    for index in range(2 * SIDE**3):
        x, y, z, core = chip_of(index)
        pairs.append((index, index_of(x, y, z, 1 - core)))
    return lax.ppermute(array, AXES, pairs)


def halves(values):
    high = values.astype(BF16)
    return high, (values - high.astype(F32)).astype(BF16)


def np_halves(values):
    values = np.asarray(values, np.float32)
    high = values.astype(jnp.bfloat16)
    low = (values - high.astype(np.float32)).astype(jnp.bfloat16)
    return high, low


@functools.cache
def tables():
    period = R * R
    r = np.arange(R)
    shifted = r + 0.25
    outer = 2 * np.pi * np.outer(shifted, r) / R
    first = np.concatenate([np.cos(outer), -np.sin(outer)], 0)
    inner = 2 * np.pi * (np.outer(r, r) % R) / R
    c, s = np.cos(inner), np.sin(inner)
    second = np.block([[c, -s], [s, c]])
    back = np.block([[c, s], [-s, c]])
    twist = 2 * np.pi * np.outer(shifted, r) / period
    turn = np.stack([np.cos(twist), np.sin(twist)]).astype(np.float32)
    real = np.concatenate([np.cos(outer.T), -np.sin(outer.T)], 1)
    tail = -np.concatenate([np.sin(outer.T), np.cos(outer.T)], 1)[:ROWS]
    last = np.concatenate([real, tail, np.zeros((ROWS, 2 * R))], 0)
    f_hi, f_lo = np_halves(first)
    l_hi, l_lo = np_halves(last)
    return (
        np.concatenate([f_hi, f_lo], 1),
        np.stack(np_halves(second)),
        np.stack(np_halves(back)),
        np.stack([l_hi, l_lo]),
        turn,
        (turn / period).astype(np.float32),
    )


@functools.cache
def arrivals():
    table = np.zeros((2 * SIDE**3, 8 * 16), np.int32)
    for index in range(2 * SIDE**3):
        own = chip_of(index)
        for array in range(8):
            core = own[3] ^ (array // 4)
            extra = ((0, 0, 0),) + THIRD
            for slot, held in enumerate(HELD_SECOND):
                sign = -1 if core else 1
                x, y, z = [(own[i] + held[i] + sign * extra[array % 4][i]) % SIDE for i in range(3)]
                table[index, array * 16 + slot] = (z * 2 + x % 2) * 256 + core * 128 + (y * 2 + x // 2) * 16
    return table


def dot(left, right):
    return jnp.dot(left, right, preferred_element_type=F32)


WIDTH = 16


def spread_kernel(signal_ref, filter_ref, out_ref):
    for k in range(out_ref.shape[0]):
        rows = pl.ds(k * WIDTH, WIDTH)
        out_ref[k, 0, 0] = signal_ref[rows, :].astype(F32).reshape(WIDTH, ROWS, R)
        out_ref[k, 0, 1] = filter_ref[rows, :].reshape(WIDTH, ROWS, R)


def conv_kernel(base_ref, skip_ref, in_hbm, *refs):
    consts, (out_hbm, tail_ref), refs = refs[:6], refs[6:8], refs[8:]
    (in_ref, out_ref), held, (in_sem, table_sem, out_sem) = refs[:2], refs[2:8], refs[8:]
    first_ref, second_ref, back_ref, last_ref, turn_ref, unturn_ref = held
    ctx_count = in_hbm.shape[0]
    group = in_ref.shape[2] // in_sem.shape[0]
    parts = range(in_sem.shape[0])

    def fetch(part):
        chans = pl.ds(part * group, group)
        return pltpu.make_async_copy(in_hbm.at[:, :, chans], in_ref.at[:, :, chans], in_sem.at[part])

    def leave(part):
        chans = pl.ds(part * group, group)
        return pltpu.make_async_copy(out_ref.at[:, chans], out_hbm.at[:, chans], out_sem.at[part])

    loads = [pltpu.make_async_copy(a, b, table_sem.at[i]) for i, (a, b) in enumerate(zip(consts, held))]
    fetch(0).start()
    for load in loads:
        load.start()
    for part in parts[1:]:
        fetch(part).start()
    for load in loads:
        load.wait()
    f_both = first_ref[...]
    f_hi = first_ref[:, :R]

    for part in parts:
        fetch(part).wait()
        chans = [part * group + k for k in range(group)]
        signal = [in_ref[:, 0, c].reshape(R, R) for c in chans]
        taps = [in_ref[:, 1, c].reshape(R, R) for c in chans]
        x = jnp.concatenate(signal, 1).astype(BF16)
        h_hi, h_lo = halves(jnp.concatenate(taps, 1))
        xs = dot(f_both, jnp.concatenate([x, x], 0))
        hs = dot(f_both, jnp.concatenate([h_hi, h_hi], 0)) + dot(f_hi, h_lo)
        cos, sin = turn_ref[0], turn_ref[1]
        rows = []
        for spec in (xs, hs):
            for k in range(group):
                re, im = spec[:R, k * R : (k + 1) * R], spec[R:, k * R : (k + 1) * R]
                rows.append(jnp.concatenate([re * cos + im * sin, im * cos - re * sin], 1))
        hi, lo = halves(jnp.concatenate(rows, 0))
        spectra = dot(hi, second_ref[0]) + dot(lo, second_ref[0]) + dot(hi, second_ref[1])
        prods = []
        for k in range(group):
            xr, xi = spectra[k * R : (k + 1) * R, :R], spectra[k * R : (k + 1) * R, R:]
            other = group + k
            hr, hq = spectra[other * R : (other + 1) * R, :R], spectra[other * R : (other + 1) * R, R:]
            prods.append(jnp.concatenate([xr * hr - xi * hq, xr * hq + xi * hr], 1))
        hi, lo = halves(jnp.concatenate(prods, 0))
        timed = dot(hi, back_ref[0]) + dot(lo, back_ref[0]) + dot(hi, back_ref[1])
        cos, sin = unturn_ref[0], unturn_ref[1]
        cols = []
        for k in range(group):
            re, im = timed[k * R : (k + 1) * R, :R], timed[k * R : (k + 1) * R, R:]
            cols.append(jnp.concatenate([re * cos - im * sin, re * sin + im * cos], 0))
        hi, lo = halves(jnp.concatenate(cols, 1))
        result = dot(last_ref[0], hi) + dot(last_ref[0], lo) + dot(last_ref[1], hi)
        for k in range(group):
            skip = skip_ref[base_ref[0] + chans[k]]
            conv = result[:R, k * R : (k + 1) * R] + skip * signal[k]
            out_ref[:, chans[k]] = conv.reshape(ctx_count, ROWS, R)
            tail_ref[:, chans[k], :] = result[R : R + ROWS, k * R : (k + 1) * R]
        leave(part).start()
    for part in parts:
        leave(part).wait()


def finish_kernel(after_ref, conv_ref, gate_ref, out_ref):
    for k in range(conv_ref.shape[0]):
        rows = pl.ds(k * WIDTH, WIDTH)
        conv = conv_ref[k, 0].reshape(WIDTH, ROWS * R)
        out_ref[rows, :] = (gate_ref[rows, :].astype(F32) * conv).astype(BF16)


def sample_kernel(place_ref, lengths_ref, skip_ref, input_ref, gate_ref, *rest):
    pieces, (out_ref, done_ref, tail_ref, sem) = rest[:8], rest[8:]
    step = pl.program_id(0)

    @pl.when(step == 0)
    def _():
        done_ref[...] = jnp.zeros_like(done_ref)
        for array, piece_ref in enumerate(pieces):
            for slot in range(16):
                channel = pl.multiple_of(place_ref[array * 16 + slot], WIDTH)
                pltpu.make_async_copy(piece_ref.at[slot], tail_ref.at[:, pl.ds(channel, WIDTH)], sem).start()
        pltpu.make_async_copy(tail_ref, tail_ref, sem).wait()

    positions = step * R + lax.broadcasted_iota(jnp.int32, (R, R), 0)
    for block in range(tail_ref.shape[1] // R):
        cols = pl.ds(block * R, R)
        state = tail_ref[step, cols, :].T
        for i in range(input_ref.shape[0]):
            blended = gate_ref[i, :, cols].astype(F32) * (
                state + skip_ref[:, cols] * input_ref[i, :, cols].astype(F32)
            )
            out_ref[i, :, cols] = jnp.where(positions < lengths_ref[i], blended, 0.0).astype(BF16)


VMEM = pl.BlockSpec(memory_space=pltpu.VMEM)
SMEM = pl.BlockSpec(memory_space=pltpu.SMEM)
ANY = pl.BlockSpec(memory_space=pl.ANY)


def on_device(prompt_input, prompt_gate, filters, skip, sample_input, sample_gate, lengths):
    width_dev, span = prompt_input.shape
    ctx_count = 16
    half = ctx_count // 2
    ctx, smp = lax.axis_index("ctx"), lax.axis_index("smp")
    place = lax.dynamic_index_in_dim(jnp.asarray(arrivals()), ctx * 8 + smp, keepdims=False)
    base = (smp * width_dev + (ctx % 2 * half + ctx // 2) * WIDTH).astype(jnp.int32).reshape(1)

    spread = pl.pallas_call(
        spread_kernel,
        grid=(2,),
        in_specs=[pl.BlockSpec((width_dev // 2, span), lambda k: (k, 0))] * 2,
        out_specs=pl.BlockSpec((half, 1, 2, WIDTH, ROWS, R), lambda k: (0, k, 0, 0, 0, 0)),
        out_shape=jax.ShapeDtypeStruct((half, 2, 2, WIDTH, ROWS, R), F32),
        name="spread",
    )(prompt_input, filters)
    spread = spread.reshape(ctx_count, 2, WIDTH, ROWS, R)
    regrouped = lax.all_to_all(spread, "ctx", split_axis=0, concat_axis=0, tiled=True)

    consts = [jnp.asarray(table) for table in tables()]
    parts = 2
    convolved, tail = pl.pallas_call(
        conv_kernel,
        in_specs=[SMEM, SMEM] + [ANY] * 7,
        out_specs=[ANY, VMEM],
        out_shape=[
            jax.ShapeDtypeStruct((ctx_count, WIDTH, ROWS, R), F32),
            jax.ShapeDtypeStruct((ROWS, WIDTH, R), F32),
        ],
        scratch_shapes=[
            pltpu.VMEM(regrouped.shape, F32),
            pltpu.VMEM((ctx_count, WIDTH, ROWS, R), F32),
            *[pltpu.VMEM(table.shape, table.dtype) for table in consts],
            pltpu.SemaphoreType.DMA((parts,)),
            pltpu.SemaphoreType.DMA((len(consts),)),
            pltpu.SemaphoreType.DMA((parts,)),
        ],
        compiler_params=pltpu.CompilerParams(vmem_limit_bytes=56 * 2**20),
        name="conv",
    )(base, skip, regrouped, *consts)

    tail = tail[None]
    held = jnp.concatenate([tail] + [take_from(tail, o) for o in FIRST], 0)
    held = jnp.concatenate([held] + [take_from(held, o) for o in SECOND], 0)
    mine = [held] + [take_from(held, o, mirrored=True) for o in THIRD]
    other = [swap_cores(part) for part in mine]

    local, length, channels = sample_input.shape
    block = pl.BlockSpec((local, R, channels), lambda j: (0, j, 0))
    sample_output, done = pl.pallas_call(
        sample_kernel,
        grid=(length // R,),
        in_specs=[SMEM, SMEM, pl.BlockSpec((1, channels), lambda j: (0, 0)), block, block] + [ANY] * 8,
        out_specs=[block, pl.BlockSpec((8, R), lambda j: (0, 0))],
        out_shape=[jax.ShapeDtypeStruct(sample_input.shape, BF16), jax.ShapeDtypeStruct((8, R), F32)],
        scratch_shapes=[pltpu.VMEM((ROWS, channels, R), F32), pltpu.SemaphoreType.DMA],
        compiler_params=pltpu.CompilerParams(vmem_limit_bytes=56 * 2**20),
        name="samples",
    )(place, lengths, skip.reshape(1, channels), sample_input, sample_gate, *mine, *other)

    returned = lax.all_to_all(convolved, "ctx", split_axis=0, concat_axis=0, tiled=True)
    prompt_output = pl.pallas_call(
        finish_kernel,
        grid=(2,),
        in_specs=[
            ANY,
            pl.BlockSpec((half, 1, WIDTH, ROWS, R), lambda k: (0, k, 0, 0, 0)),
            pl.BlockSpec((width_dev // 2, span), lambda k: (k, 0)),
        ],
        out_specs=pl.BlockSpec((width_dev // 2, span), lambda k: (k, 0)),
        out_shape=jax.ShapeDtypeStruct((width_dev, span), BF16),
        name="finish",
    )(done, returned.reshape(half, 2, WIDTH, ROWS, R), prompt_gate)
    return prompt_output, sample_output


def solution(mesh):
    return jax.shard_map(
        on_device,
        mesh=mesh,
        in_specs=(
            P("smp", "ctx"),
            P("smp", "ctx"),
            P("smp", "ctx"),
            P(),
            P(("ctx", "smp"), None, None),
            P(("ctx", "smp"), None, None),
            P(("ctx", "smp")),
        ),
        out_specs=(P("smp", "ctx"), P(("ctx", "smp"), None, None)),
        check_vma=False,
    )
```

time: 167 us -> 126 us (0.75)
  Pallas kernels: 52 us -> 31.4 us
  waiting for transfers between devices: 58.9 us -> 38.4 us
  local copies, waits for them, and re-layouts: 7.29 us -> 4.47 us
  starting transfers between devices: 46.6 us -> 48.4 us
    all_to_all x1, waiting for transfers between devices: 17.2 us -> 0.01 us  [on_device(): lax.all_to_all(convolved, 'ctx', split_axis=0, concat_axis=0, tiled=True)]
    pallas_call x3, Pallas kernels: 29.4 us -> 15.4 us  [the longest x1 10.6 us: on_device(): pl.pallas_call(conv_kernel, in_specs=[SMEM, SMEM] + [ANY] * 7, out_specs=...]
    pallas_call x1, Pallas kernels: 22.6 us -> 16 us  [on_device(): pl.pallas_call(sample_kernel, grid=(length // R,), in_specs=[SMEM, SMEM,...]
    unnamed x25 -> x14, local copies, waits for them, and re-layouts: 7.26 us -> 3.25 us
    ppermute x9, waiting for transfers between devices: 13.2 us -> 9.95 us  [take_from(): return lax.ppermute(array, AXES, pairs)]
    ppermute x9, starting transfers between devices: 18.7 us -> 20.7 us  [take_from(): return lax.ppermute(array, AXES, pairs)]
  transfers between devices with their start and end apart: 15 -> 15, of which waited for: 8 -> 4; matrix products, arithmetic and copies ran while one was open for 0% -> 2% of each run, Pallas kernels for 5% -> 13%
where the time goes in v2:
time: 126 us; the launch traced here: 124 us
  starting transfers between devices  48.4 us (38%)
  waiting for transfers between devices  38.4 us (30%)
  Pallas kernels  31.4 us (25%)
  local copies, waits for them, and re-layouts  4.47 us (4%)
    all_to_all x1, waiting for transfers between devices, on_device(): lax.all_to_all(spread, 'ctx', split_axis=0, concat_axis=0, tiled=True)  28.5 us
    ppermute x9, starting transfers between devices, take_from(): return lax.ppermute(array, AXES, pairs)  20.7 us
    pallas_call x1, Pallas kernels, on_device(): pl.pallas_call(sample_kernel, grid=(length // R,), in_specs=[SMEM, SMEM,...  16 us
    ppermute x4, starting transfers between devices, swap_cores(): return lax.ppermute(array, AXES, pairs)  13.6 us
    pallas_call x1, Pallas kernels, on_device(): pl.pallas_call(conv_kernel, in_specs=[SMEM, SMEM] + [ANY] * 7, out_specs=...  10.6 us
    ppermute x9, waiting for transfers between devices, take_from(): return lax.ppermute(array, AXES, pairs)  9.95 us
    all_to_all x1, starting transfers between devices, on_device(): lax.all_to_all(spread, 'ctx', split_axis=0, concat_axis=0, tiled=True)  8.45 us
    all_to_all x1, starting transfers between devices, on_device(): lax.all_to_all(convolved, 'ctx', split_axis=0, concat_axis=0, tiled=True)  5.69 us
  transfers between devices with their start and end apart: 15, of which 4 were waited for; matrix products, arithmetic and copies ran while one was open for 2% of the time, Pallas kernels for 13%

profile of v2, /device:TPU:1, one launch (start us, length us, event | category | flops | bytes accessed | tf_op | source)
XLA Modules:
  0.0 124.3 jit_solution(852060270296299852)
XLA Ops:
  0.6 2.6 %spread.1 = f32[8,2,2,16,8,128]{5,4,3,2,1,0:T(8,128)} custom-call(bf16[256,1024]{1,0:T(8,128)(2,1)} %signal_ref.1, f32[256,1024]{1,0:T(8,128)} %filter_ref.1), custom_call_target="tpu_custom_call" | custom-call | tf_op jit(solution)/shard_map/spread/pallas_call | solution.py:237
  3.2 8.4 %all-to-all-start = ((f32[16,2,16,8,128]{4,3,2,1,0:T(8,128)}), f32[16,2,16,8,128]{4,3,2,1,0:T(8,128)S(1)}, u32[]{:S(2)}, u32[]{:S(2)}) async-start(f32[16,2,16,8,128]{4,3,2,1,0:T(8,128)} %bitcast.8), calls=%async_computation | async-start | bytes 4194304 | tf_op jit(solution)/shard_map/all_to_all | solution.py:246
  11.7 28.5 %all-to-all-done.in_hbm = f32[16,2,16,8,128]{4,3,2,1,0:T(8,128)S(1)} async-done(((f32[16,2,16,8,128]{4,3,2,1,0:T(8,128)}), f32[16,2,16,8,128]{4,3,2,1,0:T(8,128)S(1)}, u32[]{:S(2)}, u32[]{:S(2)}) %all-to-all-start) | async-done | bytes 2097184 | tf_op jit(solution)/shard_map/all_to_all | solution.py:246
  40.2 0.0 copy-start
  40.2 1.3 %copy-done = f32[16,2,16,8,128]{4,3,2,1,0:T(8,128)} copy-done((f32[16,2,16,8,128]{4,3,2,1,0:T(8,128)}, f32[16,2,16,8,128]{4,3,2,1,0:T(8,128)S(1)}, u32[]{:S(2)}) %copy-start) | copy-done | bytes 2097176
  41.5 10.6 %conv.1 = (f32[16,16,8,128]{3,2,1,0:T(8,128)}, f32[8,16,128]{2,1,0:T(8,128)}) custom-call(s32[1]{0:T(128)} %bitcast.2.base_ref, f32[2048]{0:T(1024)} %skip_ref.1, f32[16,2,16,8,128]{4,3,2,1,0:T(8,128)} %copy-done, bf16[256,256]{1,0:T(8,128)(2,1)} %constant.59.clone.refs_0_, bf16[2,256,256]{2,1,0:T(8,128)(2,1)} %constant.60.clone.refs_1_, ...), custom_call_target="tpu_custom_call" | custom-call | tf_op jit(solution)/shard_map/conv/pallas_call | solution.py:250
  52.1 5.1 %collective-permute-start.2 = (f32[1,8,16,128]{3,2,1,0:T(8,128)}, f32[1,8,16,128]{3,2,1,0:T(8,128)S(1)}, u32[]{:S(2)}, u32[]{:S(2)}) collective-permute-start(f32[1,8,16,128]{3,2,1,0:T(8,128)} %bitcast.10), channel_id=1, source_target_pairs={{84,0},{85,1},{86,2},{87,3},{80,4},{81,5},{82,6},{83,7},{92,8},{93... | collective-permute-start | bytes 196616 | tf_op jit(solution)/shard_map/ppermute | solution.py:44
  57.2 0.1 collective-permute-start.1
  57.3 6.8 %collective-permute-start = (f32[1,8,16,128]{3,2,1,0:T(8,128)}, f32[1,8,16,128]{3,2,1,0:T(8,128)S(1)}, u32[]{:S(2)}, u32[]{:S(2)}) collective-permute-start(f32[1,8,16,128]{3,2,1,0:T(8,128)} %bitcast.12), channel_id=1, source_target_pairs={{35,0},{50,1},{37,2},{52,3},{39,4},{54,5},{33,6},{48,7},{43,8},{58... | collective-permute-start | bytes 196616 | tf_op jit(solution)/shard_map/ppermute | solution.py:44
  64.1 0.9 constant_dynamic-update-slice_fusion.6
  65.0 0.0 collective-permute-done.2
  65.0 1.0 collective-permute-done.1
  66.0 0.0 collective-permute-done
  66.0 0.9 pad_maximum_fusion
  66.8 0.1 collective-permute-start.5
  66.9 1.2 collective-permute-start.4
  68.2 2.3 %collective-permute-start.3 = (f32[4,8,16,128]{3,2,1,0:T(8,128)S(1)}, f32[4,8,16,128]{3,2,1,0:T(8,128)S(1)}, u32[]{:S(2)}, u32[]{:S(2)}) collective-permute-start(f32[4,8,16,128]{3,2,1,0:T(8,128)S(1)} %pad_maximum_fusion), channel_id=1, source_target_pairs={{16,0},{17,1},{18,2},{19,3},{20,4},{21,5},{22,6},{23,7},{24,8},{25... | collective-permute-start | bytes 786440 | tf_op jit(solution)/shard_map/ppermute | solution.py:44
  70.5 4.7 %collective-permute-done.3 = f32[4,8,16,128]{3,2,1,0:T(8,128)S(1)} collective-permute-done((f32[4,8,16,128]{3,2,1,0:T(8,128)S(1)}, f32[4,8,16,128]{3,2,1,0:T(8,128)S(1)}, u32[]{:S(2)}, u32[]{:S(2)}) %collective-permute-start.3) | collective-permute-done | bytes 262176 | tf_op jit(solution)/shard_map/ppermute | solution.py:44
  75.2 0.0 collective-permute-done.4
  75.2 0.0 collective-permute-done.5
  75.3 0.0 copy-start.2
  75.3 2.2 %collective-permute-start.8 = (f32[16,8,16,128]{3,2,1,0:T(8,128)S(1)}, f32[16,8,16,128]{3,2,1,0:T(8,128)S(1)}, u32[]{:S(2)}, u32[]{:S(2)}) collective-permute-start(f32[16,8,16,128]{3,2,1,0:T(8,128)S(1)} %constant_dynamic-update-slice_fusion.rest_0_), channel_id=1, source_target_pairs={{2,0},{3,1},{4,2},{5,3},{6,4},{7,5},{0,6},{1,7},{14,8},{15,9},{8,1... | collective-permute-start | bytes 3145736 | tf_op jit(solution)/shard_map/ppermute | solution.py:44
  77.5 1.2 collective-permute-start.7
  78.6 1.7 %collective-permute-start.6 = (f32[16,8,16,128]{3,2,1,0:T(8,128)S(1)}, f32[16,8,16,128]{3,2,1,0:T(8,128)}, u32[]{:S(2)}, u32[]{:S(2)}) collective-permute-start(f32[16,8,16,128]{3,2,1,0:T(8,128)S(1)} %constant_dynamic-update-slice_fusion.rest_0_), channel_id=1, source_target_pairs={{1,0},{16,1},{3,2},{18,3},{5,4},{20,5},{7,6},{22,7},{25,8},{8,9},{... | collective-permute-start | bytes 3145736 | tf_op jit(solution)/shard_map/ppermute | solution.py:44
  80.3 5.6 %collective-permute-start.9 = (f32[16,8,16,128]{3,2,1,0:T(8,128)S(1)}, f32[16,8,16,128]{3,2,1,0:T(8,128)}, u32[]{:S(2)}, u32[]{:S(2)}) collective-permute-start(f32[16,8,16,128]{3,2,1,0:T(8,128)S(1)} %constant_dynamic-update-slice_fusion.rest_0_), channel_id=1, source_target_pairs={{0,8},{1,9},{2,10},{3,11},{4,12},{5,13},{6,14},{7,15},{8,0},{9,1},... | collective-permute-start | bytes 3145736 | tf_op jit(solution)/shard_map/ppermute | solution.py:52
  85.9 4.3 %collective-permute-done.8.rest_3_ = f32[16,8,16,128]{3,2,1,0:T(8,128)S(1)} collective-permute-done((f32[16,8,16,128]{3,2,1,0:T(8,128)S(1)}, f32[16,8,16,128]{3,2,1,0:T(8,128)S(1)}, u32[]{:S(2)}, u32[]{:S(2)}) %collective-permute-start.8) | collective-permute-done | bytes 1048608 | tf_op jit(solution)/shard_map/ppermute | solution.py:44
  90.2 0.0 copy-start.3
  90.2 4.1 %collective-permute-start.12 = (f32[16,8,16,128]{3,2,1,0:T(8,128)S(1)}, f32[16,8,16,128]{3,2,1,0:T(8,128)}, u32[]{:S(2)}, u32[]{:S(2)}) collective-permute-start(f32[16,8,16,128]{3,2,1,0:T(8,128)S(1)} %collective-permute-done.8.rest_3_), channel_id=1, source_target_pairs={{0,8},{1,9},{2,10},{3,11},{4,12},{5,13},{6,14},{7,15},{8,0},{9,1},... | collective-permute-start | bytes 3145736 | tf_op jit(solution)/shard_map/ppermute | solution.py:52
  94.3 0.0 collective-permute-done.7.rest_2_
  94.3 1.4 %collective-permute-start.11 = (f32[16,8,16,128]{3,2,1,0:T(8,128)}, f32[16,8,16,128]{3,2,1,0:T(8,128)}, u32[]{:S(2)}, u32[]{:S(2)}) collective-permute-start(f32[16,8,16,128]{3,2,1,0:T(8,128)} %collective-permute-done.7.rest_2_), channel_id=1, source_target_pairs={{0,8},{1,9},{2,10},{3,11},{4,12},{5,13},{6,14},{7,15},{8,0},{9,1},... | collective-permute-start | bytes 3145736 | tf_op jit(solution)/shard_map/ppermute | solution.py:52
  95.7 0.0 collective-permute-done.6.rest_1_
  95.7 2.6 %collective-permute-start.10 = (f32[16,8,16,128]{3,2,1,0:T(8,128)}, f32[16,8,16,128]{3,2,1,0:T(8,128)}, u32[]{:S(2)}, u32[]{:S(2)}) collective-permute-start(f32[16,8,16,128]{3,2,1,0:T(8,128)} %collective-permute-done.6.rest_1_), channel_id=1, source_target_pairs={{0,8},{1,9},{2,10},{3,11},{4,12},{5,13},{6,14},{7,15},{8,0},{9,1},... | collective-permute-start | bytes 3145736 | tf_op jit(solution)/shard_map/ppermute | solution.py:52
  98.2 5.7 %all-to-all-start.1 = ((f32[16,16,8,128]{3,2,1,0:T(8,128)}), f32[16,16,8,128]{3,2,1,0:T(8,128)S(1)}, u32[]{:S(2)}, u32[]{:S(2)}) async-start(f32[16,16,8,128]{3,2,1,0:T(8,128)} %get-tuple-element.8), calls=%async_computation.1 | async-start | bytes 2097152 | tf_op jit(solution)/shard_map/all_to_all | solution.py:289
  103.9 1.2 dynamic-slice_bitcast_fusion.place_ref
  105.1 0.0 collective-permute-done.9.rest_4_
  105.1 0.0 collective-permute-done.12.rest_7_
  105.1 0.0 collective-permute-done.11.rest_6_
  105.1 0.0 collective-permute-done.10.rest_5_
  105.1 0.0 copy-done.2
  105.2 0.0 copy-done.3
  105.2 16.0 %samples.1 = (bf16[2,1024,2048]{2,1,0:T(8,128)(2,1)}, f32[8,128]{1,0:T(8,128)}) custom-call(s32[128]{0:T(128)} %dynamic-slice_bitcast_fusion.place_ref, s32[2]{0:T(128)} %lengths_ref.1, f32[1,2048]{1,0:T(1,128)} %bitcast.14, bf16[2,1024,2048]{2,1,0:T(8,128)(2,1)} %input_ref.1, bf16[2,1024,2048]{2,1,0:T(8,128)(2,1)} %gate_ref.2, ...), custom_call_target="tpu_custom_call" | custom-call | tf_op jit(solution)/shard_map/samples/pallas_call | solution.py:278
  121.1 0.0 all-to-all-done.1
  121.1 0.0 copy-start.1
  121.2 1.0 copy-done.1
  122.2 2.2 %finish.1 = bf16[256,1024]{1,0:T(8,128)(2,1)} custom-call(f32[8,128]{1,0:T(8,128)} %get-tuple-element.7.after_ref, f32[8,2,16,8,128]{4,3,2,1,0:T(8,128)} %bitcast.9, bf16[256,1024]{1,0:T(8,128)(2,1)} %gate_ref.3), custom_call_target="tpu_custom_call" | custom-call | tf_op jit(solution)/shard_map/finish/pallas_call | solution.py:290
  (6 shorter events, 0.1 us)
Async XLA Ops:
  3.2 36.9 %all-to-all-start = ((f32[16,2,16,8,128]{4,3,2,1,0:T(8,128)}), f32[16,2,16,8,128]{4,3,2,1,0:T(8,128)S(1)}, u32[]{:S(2)}, u32[]{:S(2)}) async-start(f32[16,2,16,8,128]{4,3,2,1,0:T(8,128)} %bitcast.8), calls=%async_computation | async-start | bytes 4194304 | tf_op jit(solution)/shard_map/all_to_all | solution.py:246
  40.2 1.3 %copy-start = (f32[16,2,16,8,128]{4,3,2,1,0:T(8,128)}, f32[16,2,16,8,128]{4,3,2,1,0:T(8,128)S(1)}, u32[]{:S(2)}) copy-start(f32[16,2,16,8,128]{4,3,2,1,0:T(8,128)S(1)} %all-to-all-done.in_hbm) | copy-start | bytes 6291460
  52.1 12.9 %collective-permute-start.2 = (f32[1,8,16,128]{3,2,1,0:T(8,128)}, f32[1,8,16,128]{3,2,1,0:T(8,128)S(1)}, u32[]{:S(2)}, u32[]{:S(2)}) collective-permute-start(f32[1,8,16,128]{3,2,1,0:T(8,128)} %bitcast.10), channel_id=1, source_target_pairs={{84,0},{85,1},{86,2},{87,3},{80,4},{81,5},{82,6},{83,7},{92,8},{93... | collective-permute-start | bytes 196616 | tf_op jit(solution)/shard_map/ppermute | solution.py:44
  57.2 8.8 %collective-permute-start.1 = (f32[1,8,16,128]{3,2,1,0:T(8,128)}, f32[1,8,16,128]{3,2,1,0:T(8,128)S(1)}, u32[]{:S(2)}, u32[]{:S(2)}) collective-permute-start(f32[1,8,16,128]{3,2,1,0:T(8,128)} %bitcast.11), channel_id=1, source_target_pairs={{119,0},{102,1},{113,2},{96,3},{115,4},{98,5},{117,6},{100,7},{127... | collective-permute-start | bytes 196616 | tf_op jit(solution)/shard_map/ppermute | solution.py:44
  57.3 8.7 %collective-permute-start = (f32[1,8,16,128]{3,2,1,0:T(8,128)}, f32[1,8,16,128]{3,2,1,0:T(8,128)S(1)}, u32[]{:S(2)}, u32[]{:S(2)}) collective-permute-start(f32[1,8,16,128]{3,2,1,0:T(8,128)} %bitcast.12), channel_id=1, source_target_pairs={{35,0},{50,1},{37,2},{52,3},{39,4},{54,5},{33,6},{48,7},{43,8},{58... | collective-permute-start | bytes 196616 | tf_op jit(solution)/shard_map/ppermute | solution.py:44
  66.8 8.4 %collective-permute-start.5 = (f32[4,8,16,128]{3,2,1,0:T(8,128)S(1)}, f32[4,8,16,128]{3,2,1,0:T(8,128)S(1)}, u32[]{:S(2)}, u32[]{:S(2)}) collective-permute-start(f32[4,8,16,128]{3,2,1,0:T(8,128)S(1)} %pad_maximum_fusion), channel_id=1, source_target_pairs={{4,0},{5,1},{6,2},{7,3},{0,4},{1,5},{2,6},{3,7},{12,8},{13,9},{14,... | collective-permute-start | bytes 786440 | tf_op jit(solution)/shard_map/ppermute | solution.py:44
  66.9 8.3 %collective-permute-start.4 = (f32[4,8,16,128]{3,2,1,0:T(8,128)S(1)}, f32[4,8,16,128]{3,2,1,0:T(8,128)S(1)}, u32[]{:S(2)}, u32[]{:S(2)}) collective-permute-start(f32[4,8,16,128]{3,2,1,0:T(8,128)S(1)} %pad_maximum_fusion), channel_id=1, source_target_pairs={{64,0},{65,1},{66,2},{67,3},{68,4},{69,5},{70,6},{71,7},{72,8},{73... | collective-permute-start | bytes 786440 | tf_op jit(solution)/shard_map/ppermute | solution.py:44
  68.2 7.0 %collective-permute-start.3 = (f32[4,8,16,128]{3,2,1,0:T(8,128)S(1)}, f32[4,8,16,128]{3,2,1,0:T(8,128)S(1)}, u32[]{:S(2)}, u32[]{:S(2)}) collective-permute-start(f32[4,8,16,128]{3,2,1,0:T(8,128)S(1)} %pad_maximum_fusion), channel_id=1, source_target_pairs={{16,0},{17,1},{18,2},{19,3},{20,4},{21,5},{22,6},{23,7},{24,8},{25... | collective-permute-start | bytes 786440 | tf_op jit(solution)/shard_map/ppermute | solution.py:44
  75.3 29.9 %copy-start.2 = (f32[16,8,16,128]{3,2,1,0:T(8,128)}, f32[16,8,16,128]{3,2,1,0:T(8,128)S(1)}, u32[]{:S(2)}) copy-start(f32[16,8,16,128]{3,2,1,0:T(8,128)S(1)} %constant_dynamic-update-slice_fusion.rest_0_) | copy-start | bytes 3145732
  75.3 14.9 %collective-permute-start.8 = (f32[16,8,16,128]{3,2,1,0:T(8,128)S(1)}, f32[16,8,16,128]{3,2,1,0:T(8,128)S(1)}, u32[]{:S(2)}, u32[]{:S(2)}) collective-permute-start(f32[16,8,16,128]{3,2,1,0:T(8,128)S(1)} %constant_dynamic-update-slice_fusion.rest_0_), channel_id=1, source_target_pairs={{2,0},{3,1},{4,2},{5,3},{6,4},{7,5},{0,6},{1,7},{14,8},{15,9},{8,1... | collective-permute-start | bytes 3145736 | tf_op jit(solution)/shard_map/ppermute | solution.py:44
  77.5 16.8 %collective-permute-start.7 = (f32[16,8,16,128]{3,2,1,0:T(8,128)S(1)}, f32[16,8,16,128]{3,2,1,0:T(8,128)}, u32[]{:S(2)}, u32[]{:S(2)}) collective-permute-start(f32[16,8,16,128]{3,2,1,0:T(8,128)S(1)} %constant_dynamic-update-slice_fusion.rest_0_), channel_id=1, source_target_pairs={{32,0},{33,1},{34,2},{35,3},{36,4},{37,5},{38,6},{39,7},{104,8},{1... | collective-permute-start | bytes 3145736 | tf_op jit(solution)/shard_map/ppermute | solution.py:44
  78.6 17.0 %collective-permute-start.6 = (f32[16,8,16,128]{3,2,1,0:T(8,128)S(1)}, f32[16,8,16,128]{3,2,1,0:T(8,128)}, u32[]{:S(2)}, u32[]{:S(2)}) collective-permute-start(f32[16,8,16,128]{3,2,1,0:T(8,128)S(1)} %constant_dynamic-update-slice_fusion.rest_0_), channel_id=1, source_target_pairs={{1,0},{16,1},{3,2},{18,3},{5,4},{20,5},{7,6},{22,7},{25,8},{8,9},{... | collective-permute-start | bytes 3145736 | tf_op jit(solution)/shard_map/ppermute | solution.py:44
  80.3 24.8 %collective-permute-start.9 = (f32[16,8,16,128]{3,2,1,0:T(8,128)S(1)}, f32[16,8,16,128]{3,2,1,0:T(8,128)}, u32[]{:S(2)}, u32[]{:S(2)}) collective-permute-start(f32[16,8,16,128]{3,2,1,0:T(8,128)S(1)} %constant_dynamic-update-slice_fusion.rest_0_), channel_id=1, source_target_pairs={{0,8},{1,9},{2,10},{3,11},{4,12},{5,13},{6,14},{7,15},{8,0},{9,1},... | collective-permute-start | bytes 3145736 | tf_op jit(solution)/shard_map/ppermute | solution.py:52
  90.2 14.9 %copy-start.3 = (f32[16,8,16,128]{3,2,1,0:T(8,128)}, f32[16,8,16,128]{3,2,1,0:T(8,128)S(1)}, u32[]{:S(2)}) copy-start(f32[16,8,16,128]{3,2,1,0:T(8,128)S(1)} %collective-permute-done.8.rest_3_) | copy-start | bytes 3145732
  90.2 14.9 %collective-permute-start.12 = (f32[16,8,16,128]{3,2,1,0:T(8,128)S(1)}, f32[16,8,16,128]{3,2,1,0:T(8,128)}, u32[]{:S(2)}, u32[]{:S(2)}) collective-permute-start(f32[16,8,16,128]{3,2,1,0:T(8,128)S(1)} %collective-permute-done.8.rest_3_), channel_id=1, source_target_pairs={{0,8},{1,9},{2,10},{3,11},{4,12},{5,13},{6,14},{7,15},{8,0},{9,1},... | collective-permute-start | bytes 3145736 | tf_op jit(solution)/shard_map/ppermute | solution.py:52
  94.3 10.8 %collective-permute-start.11 = (f32[16,8,16,128]{3,2,1,0:T(8,128)}, f32[16,8,16,128]{3,2,1,0:T(8,128)}, u32[]{:S(2)}, u32[]{:S(2)}) collective-permute-start(f32[16,8,16,128]{3,2,1,0:T(8,128)} %collective-permute-done.7.rest_2_), channel_id=1, source_target_pairs={{0,8},{1,9},{2,10},{3,11},{4,12},{5,13},{6,14},{7,15},{8,0},{9,1},... | collective-permute-start | bytes 3145736 | tf_op jit(solution)/shard_map/ppermute | solution.py:52
  95.7 9.5 %collective-permute-start.10 = (f32[16,8,16,128]{3,2,1,0:T(8,128)}, f32[16,8,16,128]{3,2,1,0:T(8,128)}, u32[]{:S(2)}, u32[]{:S(2)}) collective-permute-start(f32[16,8,16,128]{3,2,1,0:T(8,128)} %collective-permute-done.6.rest_1_), channel_id=1, source_target_pairs={{0,8},{1,9},{2,10},{3,11},{4,12},{5,13},{6,14},{7,15},{8,0},{9,1},... | collective-permute-start | bytes 3145736 | tf_op jit(solution)/shard_map/ppermute | solution.py:52
  98.2 22.9 %all-to-all-start.1 = ((f32[16,16,8,128]{3,2,1,0:T(8,128)}), f32[16,16,8,128]{3,2,1,0:T(8,128)S(1)}, u32[]{:S(2)}, u32[]{:S(2)}) async-start(f32[16,16,8,128]{3,2,1,0:T(8,128)} %get-tuple-element.8), calls=%async_computation.1 | async-start | bytes 2097152 | tf_op jit(solution)/shard_map/all_to_all | solution.py:289
  121.1 1.0 copy-start.1

commit v3 on v2

--- a/solution.py
+++ b/solution.py
@@ -81,14 +81,13 @@
     tail = -np.concatenate([np.sin(outer.T), np.cos(outer.T)], 1)[:ROWS]
     last = np.concatenate([real, tail, np.zeros((ROWS, 2 * R))], 0)
     f_hi, f_lo = np_halves(first)
-    l_hi, l_lo = np_halves(last)
+    l_hi, l_lo = np_halves(last / period)
     return (
         np.concatenate([f_hi, f_lo], 1),
         np.stack(np_halves(second)),
         np.stack(np_halves(back)),
         np.stack([l_hi, l_lo]),
         turn,
-        (turn / period).astype(np.float32),
     )
 
 
@@ -112,6 +111,7 @@
 
 
 WIDTH = 16
+GROUP = 2
 
 
 def spread_kernel(signal_ref, filter_ref, out_ref):
@@ -121,38 +121,23 @@
         out_ref[k, 0, 1] = filter_ref[rows, :].reshape(WIDTH, ROWS, R)
 
 
-def conv_kernel(base_ref, skip_ref, in_hbm, *refs):
-    consts, (out_hbm, tail_ref), refs = refs[:6], refs[6:8], refs[8:]
-    (in_ref, out_ref), held, (in_sem, table_sem, out_sem) = refs[:2], refs[2:8], refs[8:]
-    first_ref, second_ref, back_ref, last_ref, turn_ref, unturn_ref = held
-    ctx_count = in_hbm.shape[0]
-    group = in_ref.shape[2] // in_sem.shape[0]
-    parts = range(in_sem.shape[0])
-
-    def fetch(part):
-        chans = pl.ds(part * group, group)
-        return pltpu.make_async_copy(in_hbm.at[:, :, chans], in_ref.at[:, :, chans], in_sem.at[part])
-
-    def leave(part):
-        chans = pl.ds(part * group, group)
-        return pltpu.make_async_copy(out_ref.at[:, chans], out_hbm.at[:, chans], out_sem.at[part])
-
-    loads = [pltpu.make_async_copy(a, b, table_sem.at[i]) for i, (a, b) in enumerate(zip(consts, held))]
-    fetch(0).start()
-    for load in loads:
-        load.start()
-    for part in parts[1:]:
-        fetch(part).start()
-    for load in loads:
-        load.wait()
+def conv_kernel(base_ref, place_ref, in_ref, skip_hbm, *refs):
+    first_ref, second_ref, back_ref, last_ref, turn_ref = refs[:5]
+    out_hbm, tail_ref, skip_ref, out_ref, skip_sem, out_sem = refs[-6:]
+    ctx_count = in_ref.shape[0]
+    parts = in_ref.shape[2] // GROUP
+    load = pltpu.make_async_copy(skip_hbm, skip_ref, skip_sem)
+    load.start()
+    load.wait()
     f_both = first_ref[...]
     f_hi = first_ref[:, :R]
 
-    for part in parts:
-        fetch(part).wait()
-        chans = [part * group + k for k in range(group)]
-        signal = [in_ref[:, 0, c].reshape(R, R) for c in chans]
-        taps = [in_ref[:, 1, c].reshape(R, R) for c in chans]
+    def chans(part):
+        return [part * GROUP + k for k in range(GROUP)]
+
+    def columns(part):
+        signal = [in_ref[:, 0, c].reshape(R, R) for c in chans(part)]
+        taps = [in_ref[:, 1, c].reshape(R, R) for c in chans(part)]
         x = jnp.concatenate(signal, 1).astype(BF16)
         h_hi, h_lo = halves(jnp.concatenate(taps, 1))
         xs = dot(f_both, jnp.concatenate([x, x], 0))
@@ -160,34 +145,49 @@
         cos, sin = turn_ref[0], turn_ref[1]
         rows = []
         for spec in (xs, hs):
-            for k in range(group):
+            for k in range(GROUP):
                 re, im = spec[:R, k * R : (k + 1) * R], spec[R:, k * R : (k + 1) * R]
                 rows.append(jnp.concatenate([re * cos + im * sin, im * cos - re * sin], 1))
-        hi, lo = halves(jnp.concatenate(rows, 0))
+        return halves(jnp.concatenate(rows, 0))
+
+    def product(part, value):
+        hi, lo = value
         spectra = dot(hi, second_ref[0]) + dot(lo, second_ref[0]) + dot(hi, second_ref[1])
         prods = []
-        for k in range(group):
+        for k in range(GROUP):
             xr, xi = spectra[k * R : (k + 1) * R, :R], spectra[k * R : (k + 1) * R, R:]
-            other = group + k
+            other = GROUP + k
             hr, hq = spectra[other * R : (other + 1) * R, :R], spectra[other * R : (other + 1) * R, R:]
             prods.append(jnp.concatenate([xr * hr - xi * hq, xr * hq + xi * hr], 1))
-        hi, lo = halves(jnp.concatenate(prods, 0))
+        return halves(jnp.concatenate(prods, 0))
+
+    def returning(part, value):
+        hi, lo = value
         timed = dot(hi, back_ref[0]) + dot(lo, back_ref[0]) + dot(hi, back_ref[1])
-        cos, sin = unturn_ref[0], unturn_ref[1]
+        cos, sin = turn_ref[0], turn_ref[1]
         cols = []
-        for k in range(group):
+        for k in range(GROUP):
             re, im = timed[k * R : (k + 1) * R, :R], timed[k * R : (k + 1) * R, R:]
             cols.append(jnp.concatenate([re * cos - im * sin, re * sin + im * cos], 0))
-        hi, lo = halves(jnp.concatenate(cols, 1))
+        return halves(jnp.concatenate(cols, 1))
+
+    def positions(part, value):
+        hi, lo = value
         result = dot(last_ref[0], hi) + dot(last_ref[0], lo) + dot(last_ref[1], hi)
-        for k in range(group):
-            skip = skip_ref[base_ref[0] + chans[k]]
-            conv = result[:R, k * R : (k + 1) * R] + skip * signal[k]
-            out_ref[:, chans[k]] = conv.reshape(ctx_count, ROWS, R)
-            tail_ref[:, chans[k], :] = result[R : R + ROWS, k * R : (k + 1) * R]
-        leave(part).start()
-    for part in parts:
-        leave(part).wait()
+        for k, c in enumerate(chans(part)):
+            conv = result[:R, k * R : (k + 1) * R] + skip_ref[base_ref[0] + c] * in_ref[:, 0, c].reshape(R, R)
+            out_ref[:, c] = conv.reshape(ctx_count, ROWS, R)
+            tail_ref[:, c, :] = result[R : R + ROWS, k * R : (k + 1) * R]
+
+    values = {}
+    for step in range(parts + 3):
+        for stage, section in ((3, positions), (2, returning), (1, product), (0, columns)):
+            part = step - stage
+            if 0 <= part < parts:
+                values[part] = section(part, values[part]) if stage else section(part)
+    leave = pltpu.make_async_copy(out_ref, out_hbm, out_sem)
+    leave.start()
+    leave.wait()
 
 
 def finish_kernel(after_ref, conv_ref, gate_ref, out_ref):
@@ -195,6 +195,15 @@
         rows = pl.ds(k * WIDTH, WIDTH)
         conv = conv_ref[k, 0].reshape(WIDTH, ROWS * R)
         out_ref[rows, :] = (gate_ref[rows, :].astype(F32) * conv).astype(BF16)
+
+
+def hold_kernel(after_ref, *refs):
+    count = len(refs) // 2
+    copies = [pltpu.make_async_copy(refs[i], refs[count + i], refs[-1].at[i]) for i in range(count)]
+    for copy in copies:
+        copy.start()
+    for copy in copies:
+        copy.wait()
 
 
 def sample_kernel(place_ref, lengths_ref, skip_ref, input_ref, gate_ref, *rest):
@@ -246,26 +255,34 @@
     regrouped = lax.all_to_all(spread, "ctx", split_axis=0, concat_axis=0, tiled=True)
 
     consts = [jnp.asarray(table) for table in tables()]
-    parts = 2
+    consts = consts
+    consts = pl.pallas_call(
+        hold_kernel,
+        in_specs=[ANY] * (1 + len(consts)),
+        out_specs=[VMEM] * len(consts),
+        out_shape=[jax.ShapeDtypeStruct(table.shape, table.dtype) for table in consts],
+        scratch_shapes=[pltpu.SemaphoreType.DMA((len(consts),))],
+        compiler_params=pltpu.CompilerParams(vmem_limit_bytes=40 * 2**20),
+        name="hold",
+    )(spread, *consts)
+    consts, holds = consts[:5], consts[5:]
     convolved, tail = pl.pallas_call(
         conv_kernel,
-        in_specs=[SMEM, SMEM] + [ANY] * 7,
+        in_specs=[SMEM, ANY, VMEM, ANY] + [VMEM] * 5 + [ANY] * len(holds),
         out_specs=[ANY, VMEM],
         out_shape=[
             jax.ShapeDtypeStruct((ctx_count, WIDTH, ROWS, R), F32),
             jax.ShapeDtypeStruct((ROWS, WIDTH, R), F32),
         ],
         scratch_shapes=[
-            pltpu.VMEM(regrouped.shape, F32),
+            pltpu.SMEM(skip.shape, F32),
             pltpu.VMEM((ctx_count, WIDTH, ROWS, R), F32),
-            *[pltpu.VMEM(table.shape, table.dtype) for table in consts],
-            pltpu.SemaphoreType.DMA((parts,)),
-            pltpu.SemaphoreType.DMA((len(consts),)),
-            pltpu.SemaphoreType.DMA((parts,)),
+            pltpu.SemaphoreType.DMA,
+            pltpu.SemaphoreType.DMA,
         ],
-        compiler_params=pltpu.CompilerParams(vmem_limit_bytes=56 * 2**20),
+        compiler_params=pltpu.CompilerParams(vmem_limit_bytes=30 * 2**20),
         name="conv",
-    )(base, skip, regrouped, *consts)
+    )(base, place, regrouped, skip, *consts, *holds)
 
     tail = tail[None]
     held = jnp.concatenate([tail] + [take_from(tail, o) for o in FIRST], 0)
@@ -282,7 +299,7 @@
         out_specs=[block, pl.BlockSpec((8, R), lambda j: (0, 0))],
         out_shape=[jax.ShapeDtypeStruct(sample_input.shape, BF16), jax.ShapeDtypeStruct((8, R), F32)],
         scratch_shapes=[pltpu.VMEM((ROWS, channels, R), F32), pltpu.SemaphoreType.DMA],
-        compiler_params=pltpu.CompilerParams(vmem_limit_bytes=56 * 2**20),
+        compiler_params=pltpu.CompilerParams(vmem_limit_bytes=50 * 2**20),
         name="samples",
     )(place, lengths, skip.reshape(1, channels), sample_input, sample_gate, *mine, *other)
 

time: 126 us -> 117 us (0.929)
  waiting for transfers between devices: 38.4 us -> 32.6 us
  Pallas kernels: 31.4 us -> 26.8 us
  local copies, waits for them, and re-layouts: 4.47 us -> 7.59 us
    all_to_all x1, waiting for transfers between devices: 28.5 us -> 20.9 us  [on_device(): lax.all_to_all(spread, 'ctx', split_axis=0, concat_axis=0, tiled=True)]
    pallas_call x1 -> x2, Pallas kernels: 10.6 us -> 6.25 us  [the longest x1 5.67 us: on_device(): pl.pallas_call(conv_kernel, in_specs=[SMEM, ANY, VMEM, ANY] + [VMEM] * 5...]
    unnamed x14 -> x26, local copies, waits for them, and re-layouts: 3.25 us -> 6.88 us
  transfers between devices with their start and end apart: 15 -> 15, of which waited for: 4 -> 5; matrix products, arithmetic and copies ran while one was open for 2% -> 1% of each run, Pallas kernels for 13% -> 14%
where the time goes in v3:
time: 117 us; the launch traced here: 116 us
  starting transfers between devices  48.4 us (41%)
  waiting for transfers between devices  32.6 us (28%)
  Pallas kernels  26.8 us (23%)
  local copies, waits for them, and re-layouts  7.59 us (6%)
    all_to_all x1, waiting for transfers between devices, on_device(): lax.all_to_all(spread, 'ctx', split_axis=0, concat_axis=0, tiled=True)  20.9 us
    ppermute x9, starting transfers between devices, take_from(): return lax.ppermute(array, AXES, pairs)  20.7 us
    pallas_call x1, Pallas kernels, on_device(): pl.pallas_call(sample_kernel, grid=(length // R,), in_specs=[SMEM, SMEM,...  15.8 us
    ppermute x4, starting transfers between devices, swap_cores(): return lax.ppermute(array, AXES, pairs)  13.5 us
    ppermute x9, waiting for transfers between devices, take_from(): return lax.ppermute(array, AXES, pairs)  10.7 us
    all_to_all x1, starting transfers between devices, on_device(): lax.all_to_all(spread, 'ctx', split_axis=0, concat_axis=0, tiled=True)  8.58 us
    unnamed x26, local copies, waits for them, and re-layouts  6.88 us
    pallas_call x1, Pallas kernels, on_device(): pl.pallas_call(conv_kernel, in_specs=[SMEM, ANY, VMEM, ANY] + [VMEM] * 5...  5.67 us
  transfers between devices with their start and end apart: 15, of which 5 were waited for; matrix products, arithmetic and copies ran while one was open for 1% of the time, Pallas kernels for 14%

profile of v3, /device:TPU:1, one launch (start us, length us, event | category | flops | bytes accessed | tf_op | source)
XLA Modules:
  0.0 116.1 jit_solution(2548396084829609053)
XLA Ops:
  0.6 0.0 copy-start.7
  0.6 2.6 %spread.1 = f32[8,2,2,16,8,128]{5,4,3,2,1,0:T(8,128)} custom-call(bf16[256,1024]{1,0:T(8,128)(2,1)} %signal_ref.1, f32[256,1024]{1,0:T(8,128)} %filter_ref.1), custom_call_target="tpu_custom_call" | custom-call | tf_op jit(solution)/shard_map/spread/pallas_call | solution.py:246
  3.2 0.0 copy-start.9
  3.2 8.6 %all-to-all-start = ((f32[16,2,16,8,128]{4,3,2,1,0:T(8,128)}), f32[16,2,16,8,128]{4,3,2,1,0:T(8,128)S(1)}, u32[]{:S(2)}, u32[]{:S(2)}) async-start(f32[16,2,16,8,128]{4,3,2,1,0:T(8,128)} %bitcast.8), calls=%async_computation | async-start | bytes 4194304 | tf_op jit(solution)/shard_map/all_to_all | solution.py:255
  11.8 0.0 copy-start
  11.8 1.6 %copy-done = f32[8,2,2,16,8,128]{5,4,3,2,1,0:T(8,128)S(1)} copy-done((f32[8,2,2,16,8,128]{5,4,3,2,1,0:T(8,128)S(1)}, f32[8,2,2,16,8,128]{5,4,3,2,1,0:T(8,128)}, u32[]{:S(2)}) %copy-start) | copy-done | bytes 2097176
  13.4 0.0 copy-start.2
  13.5 0.9 copy-done.2
  14.4 0.0 copy-start.3
  14.4 0.9 copy-done.3
  15.4 0.0 copy-start.4
  15.4 0.9 copy-done.4
  16.3 0.0 copy-start.5
  16.3 0.9 copy-done.5
  17.2 0.0 copy-start.6
  17.2 0.9 copy-done.6
  18.1 0.6 hold.1
  18.7 0.7 dynamic-slice_bitcast_fusion.place_ref
  19.4 20.9 %all-to-all-done.in_ref = f32[16,2,16,8,128]{4,3,2,1,0:T(8,128)S(1)} async-done(((f32[16,2,16,8,128]{4,3,2,1,0:T(8,128)}), f32[16,2,16,8,128]{4,3,2,1,0:T(8,128)S(1)}, u32[]{:S(2)}, u32[]{:S(2)}) %all-to-all-start) | async-done | bytes 2097184 | tf_op jit(solution)/shard_map/all_to_all | solution.py:255
  40.3 0.0 copy-done.7
  40.3 5.7 %conv.1 = (f32[16,16,8,128]{3,2,1,0:T(8,128)S(1)}, f32[8,16,128]{2,1,0:T(8,128)S(1)}) custom-call(s32[1]{0:T(128)} %bitcast.2.base_ref, s32[128]{0:T(128)S(1)} %dynamic-slice_bitcast_fusion.place_ref, f32[16,2,16,8,128]{4,3,2,1,0:T(8,128)S(1)} %all-to-all-done.in_ref, f32[2048]{0:T(1024)S(1)} %copy-done.7, bf16[256,256]{1,0:T(8,128)(2,1)S(1)} %get-tuple-element.11.refs_0_, ...), custom_call_target="tpu_custom_call" | custom-call | tf_op jit(solution)/shard_map/conv/pallas_call | solution.py:269
  46.0 0.0 copy-start.1
  46.0 5.1 %collective-permute-start.2 = (f32[1,8,16,128]{3,2,1,0:T(8,128)S(1)}, f32[1,8,16,128]{3,2,1,0:T(8,128)S(1)}, u32[]{:S(2)}, u32[]{:S(2)}) collective-permute-start(f32[1,8,16,128]{3,2,1,0:T(8,128)S(1)} %bitcast.10), channel_id=1, source_target_pairs={{84,0},{85,1},{86,2},{87,3},{80,4},{81,5},{82,6},{83,7},{92,8},{93... | collective-permute-start | bytes 196616 | tf_op jit(solution)/shard_map/ppermute | solution.py:44
  51.1 0.1 collective-permute-start.1
  51.2 6.8 %collective-permute-start = (f32[1,8,16,128]{3,2,1,0:T(8,128)S(1)}, f32[1,8,16,128]{3,2,1,0:T(8,128)S(1)}, u32[]{:S(2)}, u32[]{:S(2)}) collective-permute-start(f32[1,8,16,128]{3,2,1,0:T(8,128)S(1)} %bitcast.12), channel_id=1, source_target_pairs={{35,0},{50,1},{37,2},{52,3},{39,4},{54,5},{33,6},{48,7},{43,8},{58... | collective-permute-start | bytes 196616 | tf_op jit(solution)/shard_map/ppermute | solution.py:44
  58.0 0.0 collective-permute-done.2
  58.0 1.6 %collective-permute-done.1 = f32[1,8,16,128]{3,2,1,0:T(8,128)S(1)} collective-permute-done((f32[1,8,16,128]{3,2,1,0:T(8,128)S(1)}, f32[1,8,16,128]{3,2,1,0:T(8,128)S(1)}, u32[]{:S(2)}, u32[]{:S(2)}) %collective-permute-start.1) | collective-permute-done | bytes 65568 | tf_op jit(solution)/shard_map/ppermute | solution.py:44
  59.6 0.0 collective-permute-done
  59.7 0.1 collective-permute-start.5
  59.8 1.2 %collective-permute-start.4 = (f32[4,8,16,128]{3,2,1,0:T(8,128)S(1)}, f32[4,8,16,128]{3,2,1,0:T(8,128)S(1)}, u32[]{:S(2)}, u32[]{:S(2)}) collective-permute-start(f32[4,8,16,128]{3,2,1,0:T(8,128)S(1)} %pad_maximum_fusion), channel_id=1, source_target_pairs={{64,0},{65,1},{66,2},{67,3},{68,4},{69,5},{70,6},{71,7},{72,8},{73... | collective-permute-start | bytes 786440 | tf_op jit(solution)/shard_map/ppermute | solution.py:44
  61.0 2.3 %collective-permute-start.3 = (f32[4,8,16,128]{3,2,1,0:T(8,128)S(1)}, f32[4,8,16,128]{3,2,1,0:T(8,128)S(1)}, u32[]{:S(2)}, u32[]{:S(2)}) collective-permute-start(f32[4,8,16,128]{3,2,1,0:T(8,128)S(1)} %pad_maximum_fusion), channel_id=1, source_target_pairs={{16,0},{17,1},{18,2},{19,3},{20,4},{21,5},{22,6},{23,7},{24,8},{25... | collective-permute-start | bytes 786440 | tf_op jit(solution)/shard_map/ppermute | solution.py:44
  63.3 4.7 %collective-permute-done.3 = f32[4,8,16,128]{3,2,1,0:T(8,128)S(1)} collective-permute-done((f32[4,8,16,128]{3,2,1,0:T(8,128)S(1)}, f32[4,8,16,128]{3,2,1,0:T(8,128)S(1)}, u32[]{:S(2)}, u32[]{:S(2)}) %collective-permute-start.3) | collective-permute-done | bytes 262176 | tf_op jit(solution)/shard_map/ppermute | solution.py:44
  68.0 0.0 collective-permute-done.4
  68.0 0.0 collective-permute-done.5
  68.1 2.2 %collective-permute-start.8 = (f32[16,8,16,128]{3,2,1,0:T(8,128)S(1)}, f32[16,8,16,128]{3,2,1,0:T(8,128)}, u32[]{:S(2)}, u32[]{:S(2)}) collective-permute-start(f32[16,8,16,128]{3,2,1,0:T(8,128)S(1)} %constant_dynamic-update-slice_fusion.rest_0_), channel_id=1, source_target_pairs={{2,0},{3,1},{4,2},{5,3},{6,4},{7,5},{0,6},{1,7},{14,8},{15,9},{8,1... | collective-permute-start | bytes 3145736 | tf_op jit(solution)/shard_map/ppermute | solution.py:44
  70.3 1.1 collective-permute-start.7
  71.4 1.7 %collective-permute-start.6 = (f32[16,8,16,128]{3,2,1,0:T(8,128)S(1)}, f32[16,8,16,128]{3,2,1,0:T(8,128)S(1)}, u32[]{:S(2)}, u32[]{:S(2)}) collective-permute-start(f32[16,8,16,128]{3,2,1,0:T(8,128)S(1)} %constant_dynamic-update-slice_fusion.rest_0_), channel_id=1, source_target_pairs={{1,0},{16,1},{3,2},{18,3},{5,4},{20,5},{7,6},{22,7},{25,8},{8,9},{... | collective-permute-start | bytes 3145736 | tf_op jit(solution)/shard_map/ppermute | solution.py:44
  73.2 5.6 %collective-permute-start.9 = (f32[16,8,16,128]{3,2,1,0:T(8,128)S(1)}, f32[16,8,16,128]{3,2,1,0:T(8,128)}, u32[]{:S(2)}, u32[]{:S(2)}) collective-permute-start(f32[16,8,16,128]{3,2,1,0:T(8,128)S(1)} %constant_dynamic-update-slice_fusion.rest_0_), channel_id=1, source_target_pairs={{0,8},{1,9},{2,10},{3,11},{4,12},{5,13},{6,14},{7,15},{8,0},{9,1},... | collective-permute-start | bytes 3145736 | tf_op jit(solution)/shard_map/ppermute | solution.py:52
  78.7 4.4 %collective-permute-done.8.rest_3_ = f32[16,8,16,128]{3,2,1,0:T(8,128)} collective-permute-done((f32[16,8,16,128]{3,2,1,0:T(8,128)S(1)}, f32[16,8,16,128]{3,2,1,0:T(8,128)}, u32[]{:S(2)}, u32[]{:S(2)}) %collective-permute-start.8) | collective-permute-done | bytes 1048608 | tf_op jit(solution)/shard_map/ppermute | solution.py:44
  83.1 4.1 %collective-permute-start.12 = (f32[16,8,16,128]{3,2,1,0:T(8,128)}, f32[16,8,16,128]{3,2,1,0:T(8,128)}, u32[]{:S(2)}, u32[]{:S(2)}) collective-permute-start(f32[16,8,16,128]{3,2,1,0:T(8,128)} %collective-permute-done.8.rest_3_), channel_id=1, source_target_pairs={{0,8},{1,9},{2,10},{3,11},{4,12},{5,13},{6,14},{7,15},{8,0},{9,1},... | collective-permute-start | bytes 3145736 | tf_op jit(solution)/shard_map/ppermute | solution.py:52
  87.2 0.0 collective-permute-done.7.rest_2_
  87.2 1.1 collective-permute-start.11
  88.4 0.0 collective-permute-done.6.rest_1_
  88.4 2.7 %collective-permute-start.10 = (f32[16,8,16,128]{3,2,1,0:T(8,128)S(1)}, f32[16,8,16,128]{3,2,1,0:T(8,128)}, u32[]{:S(2)}, u32[]{:S(2)}) collective-permute-start(f32[16,8,16,128]{3,2,1,0:T(8,128)S(1)} %collective-permute-done.6.rest_1_), channel_id=1, source_target_pairs={{0,8},{1,9},{2,10},{3,11},{4,12},{5,13},{6,14},{7,15},{8,0},{9,1},... | collective-permute-start | bytes 3145736 | tf_op jit(solution)/shard_map/ppermute | solution.py:52
  91.1 0.0 copy-done.1
  91.1 5.6 %all-to-all-start.1 = ((f32[16,16,8,128]{3,2,1,0:T(8,128)}), f32[16,16,8,128]{3,2,1,0:T(8,128)}, u32[]{:S(2)}, u32[]{:S(2)}) async-start(f32[16,16,8,128]{3,2,1,0:T(8,128)} %copy-done.1), calls=%async_computation.1 | async-start | bytes 2097152 | tf_op jit(solution)/shard_map/all_to_all | solution.py:306
  96.6 0.0 collective-permute-done.9.rest_4_
  96.7 0.0 collective-permute-done.12.rest_7_
  96.7 0.0 collective-permute-done.11.rest_6_
  96.7 0.0 collective-permute-done.10.rest_5_
  96.7 0.0 copy-done.9
  96.7 15.8 %samples.1 = (bf16[2,1024,2048]{2,1,0:T(8,128)(2,1)}, f32[8,128]{1,0:T(8,128)S(1)}) custom-call(s32[128]{0:T(128)S(1)} %dynamic-slice_bitcast_fusion.place_ref, s32[2]{0:T(128)S(1)} %copy-done.9, f32[1,2048]{1,0:T(1,128)S(1)} %bitcast.14, bf16[2,1024,2048]{2,1,0:T(8,128)(2,1)} %input_ref.1, bf16[2,1024,2048]{2,1,0:T(8,128)(2,1)} %gate_ref.2, ...), custom_call_target="tpu_custom_call" | custom-call | tf_op jit(solution)/shard_map/samples/pallas_call | solution.py:295
  112.5 0.0 copy-start.8
  112.5 0.6 copy-done.8
  113.0 0.9 all-to-all-done.1
  114.0 2.2 %finish.1 = bf16[256,1024]{1,0:T(8,128)(2,1)} custom-call(f32[8,128]{1,0:T(8,128)} %copy-done.8, f32[8,2,16,8,128]{4,3,2,1,0:T(8,128)} %bitcast.5.conv_ref, bf16[256,1024]{1,0:T(8,128)(2,1)} %gate_ref.3), custom_call_target="tpu_custom_call" | custom-call | tf_op jit(solution)/shard_map/finish/pallas_call | solution.py:307
  (8 shorter events, 0.1 us)
Async XLA Ops:
  0.6 39.7 %copy-start.7 = (f32[2048]{0:T(1024)S(1)}, f32[2048]{0:T(1024)}, u32[]{:S(2)}) copy-start(f32[2048]{0:T(1024)} %skip_hbm.1) | copy-start | bytes 24580
  3.2 93.4 %copy-start.9 = (s32[2]{0:T(128)S(1)}, s32[2]{0:T(128)}, u32[]{:S(2)}) copy-start(s32[2]{0:T(128)} %lengths_ref.1) | copy-start | bytes 28
  3.2 37.1 %all-to-all-start = ((f32[16,2,16,8,128]{4,3,2,1,0:T(8,128)}), f32[16,2,16,8,128]{4,3,2,1,0:T(8,128)S(1)}, u32[]{:S(2)}, u32[]{:S(2)}) async-start(f32[16,2,16,8,128]{4,3,2,1,0:T(8,128)} %bitcast.8), calls=%async_computation | async-start | bytes 4194304 | tf_op jit(solution)/shard_map/all_to_all | solution.py:255
  11.8 1.6 %copy-start = (f32[8,2,2,16,8,128]{5,4,3,2,1,0:T(8,128)S(1)}, f32[8,2,2,16,8,128]{5,4,3,2,1,0:T(8,128)}, u32[]{:S(2)}) copy-start(f32[8,2,2,16,8,128]{5,4,3,2,1,0:T(8,128)} %spread.1) | copy-start | bytes 6291460
  13.4 0.9 copy-start.2
  14.4 0.9 copy-start.3
  15.4 0.9 copy-start.4
  16.3 0.9 copy-start.5
  17.2 0.9 copy-start.6
  46.0 45.1 %copy-start.1 = (f32[16,16,8,128]{3,2,1,0:T(8,128)}, f32[16,16,8,128]{3,2,1,0:T(8,128)S(1)}, u32[]{:S(2)}) copy-start(f32[16,16,8,128]{3,2,1,0:T(8,128)S(1)} %get-tuple-element.18) | copy-start | bytes 3145732
  46.0 12.0 %collective-permute-start.2 = (f32[1,8,16,128]{3,2,1,0:T(8,128)S(1)}, f32[1,8,16,128]{3,2,1,0:T(8,128)S(1)}, u32[]{:S(2)}, u32[]{:S(2)}) collective-permute-start(f32[1,8,16,128]{3,2,1,0:T(8,128)S(1)} %bitcast.10), channel_id=1, source_target_pairs={{84,0},{85,1},{86,2},{87,3},{80,4},{81,5},{82,6},{83,7},{92,8},{93... | collective-permute-start | bytes 196616 | tf_op jit(solution)/shard_map/ppermute | solution.py:44
  51.1 8.5 %collective-permute-start.1 = (f32[1,8,16,128]{3,2,1,0:T(8,128)S(1)}, f32[1,8,16,128]{3,2,1,0:T(8,128)S(1)}, u32[]{:S(2)}, u32[]{:S(2)}) collective-permute-start(f32[1,8,16,128]{3,2,1,0:T(8,128)S(1)} %bitcast.11), channel_id=1, source_target_pairs={{119,0},{102,1},{113,2},{96,3},{115,4},{98,5},{117,6},{100,7},{127... | collective-permute-start | bytes 196616 | tf_op jit(solution)/shard_map/ppermute | solution.py:44
  51.2 8.5 %collective-permute-start = (f32[1,8,16,128]{3,2,1,0:T(8,128)S(1)}, f32[1,8,16,128]{3,2,1,0:T(8,128)S(1)}, u32[]{:S(2)}, u32[]{:S(2)}) collective-permute-start(f32[1,8,16,128]{3,2,1,0:T(8,128)S(1)} %bitcast.12), channel_id=1, source_target_pairs={{35,0},{50,1},{37,2},{52,3},{39,4},{54,5},{33,6},{48,7},{43,8},{58... | collective-permute-start | bytes 196616 | tf_op jit(solution)/shard_map/ppermute | solution.py:44
  59.7 8.4 %collective-permute-start.5 = (f32[4,8,16,128]{3,2,1,0:T(8,128)S(1)}, f32[4,8,16,128]{3,2,1,0:T(8,128)S(1)}, u32[]{:S(2)}, u32[]{:S(2)}) collective-permute-start(f32[4,8,16,128]{3,2,1,0:T(8,128)S(1)} %pad_maximum_fusion), channel_id=1, source_target_pairs={{4,0},{5,1},{6,2},{7,3},{0,4},{1,5},{2,6},{3,7},{12,8},{13,9},{14,... | collective-permute-start | bytes 786440 | tf_op jit(solution)/shard_map/ppermute | solution.py:44
  59.8 8.2 %collective-permute-start.4 = (f32[4,8,16,128]{3,2,1,0:T(8,128)S(1)}, f32[4,8,16,128]{3,2,1,0:T(8,128)S(1)}, u32[]{:S(2)}, u32[]{:S(2)}) collective-permute-start(f32[4,8,16,128]{3,2,1,0:T(8,128)S(1)} %pad_maximum_fusion), channel_id=1, source_target_pairs={{64,0},{65,1},{66,2},{67,3},{68,4},{69,5},{70,6},{71,7},{72,8},{73... | collective-permute-start | bytes 786440 | tf_op jit(solution)/shard_map/ppermute | solution.py:44
  61.0 7.0 %collective-permute-start.3 = (f32[4,8,16,128]{3,2,1,0:T(8,128)S(1)}, f32[4,8,16,128]{3,2,1,0:T(8,128)S(1)}, u32[]{:S(2)}, u32[]{:S(2)}) collective-permute-start(f32[4,8,16,128]{3,2,1,0:T(8,128)S(1)} %pad_maximum_fusion), channel_id=1, source_target_pairs={{16,0},{17,1},{18,2},{19,3},{20,4},{21,5},{22,6},{23,7},{24,8},{25... | collective-permute-start | bytes 786440 | tf_op jit(solution)/shard_map/ppermute | solution.py:44
  68.1 15.0 %collective-permute-start.8 = (f32[16,8,16,128]{3,2,1,0:T(8,128)S(1)}, f32[16,8,16,128]{3,2,1,0:T(8,128)}, u32[]{:S(2)}, u32[]{:S(2)}) collective-permute-start(f32[16,8,16,128]{3,2,1,0:T(8,128)S(1)} %constant_dynamic-update-slice_fusion.rest_0_), channel_id=1, source_target_pairs={{2,0},{3,1},{4,2},{5,3},{6,4},{7,5},{0,6},{1,7},{14,8},{15,9},{8,1... | collective-permute-start | bytes 3145736 | tf_op jit(solution)/shard_map/ppermute | solution.py:44
  70.3 16.9 %collective-permute-start.7 = (f32[16,8,16,128]{3,2,1,0:T(8,128)S(1)}, f32[16,8,16,128]{3,2,1,0:T(8,128)S(1)}, u32[]{:S(2)}, u32[]{:S(2)}) collective-permute-start(f32[16,8,16,128]{3,2,1,0:T(8,128)S(1)} %constant_dynamic-update-slice_fusion.rest_0_), channel_id=1, source_target_pairs={{32,0},{33,1},{34,2},{35,3},{36,4},{37,5},{38,6},{39,7},{104,8},{1... | collective-permute-start | bytes 3145736 | tf_op jit(solution)/shard_map/ppermute | solution.py:44
  71.4 16.9 %collective-permute-start.6 = (f32[16,8,16,128]{3,2,1,0:T(8,128)S(1)}, f32[16,8,16,128]{3,2,1,0:T(8,128)S(1)}, u32[]{:S(2)}, u32[]{:S(2)}) collective-permute-start(f32[16,8,16,128]{3,2,1,0:T(8,128)S(1)} %constant_dynamic-update-slice_fusion.rest_0_), channel_id=1, source_target_pairs={{1,0},{16,1},{3,2},{18,3},{5,4},{20,5},{7,6},{22,7},{25,8},{8,9},{... | collective-permute-start | bytes 3145736 | tf_op jit(solution)/shard_map/ppermute | solution.py:44
  73.2 23.5 %collective-permute-start.9 = (f32[16,8,16,128]{3,2,1,0:T(8,128)S(1)}, f32[16,8,16,128]{3,2,1,0:T(8,128)}, u32[]{:S(2)}, u32[]{:S(2)}) collective-permute-start(f32[16,8,16,128]{3,2,1,0:T(8,128)S(1)} %constant_dynamic-update-slice_fusion.rest_0_), channel_id=1, source_target_pairs={{0,8},{1,9},{2,10},{3,11},{4,12},{5,13},{6,14},{7,15},{8,0},{9,1},... | collective-permute-start | bytes 3145736 | tf_op jit(solution)/shard_map/ppermute | solution.py:52
  83.1 13.5 %collective-permute-start.12 = (f32[16,8,16,128]{3,2,1,0:T(8,128)}, f32[16,8,16,128]{3,2,1,0:T(8,128)}, u32[]{:S(2)}, u32[]{:S(2)}) collective-permute-start(f32[16,8,16,128]{3,2,1,0:T(8,128)} %collective-permute-done.8.rest_3_), channel_id=1, source_target_pairs={{0,8},{1,9},{2,10},{3,11},{4,12},{5,13},{6,14},{7,15},{8,0},{9,1},... | collective-permute-start | bytes 3145736 | tf_op jit(solution)/shard_map/ppermute | solution.py:52
  87.2 9.4 %collective-permute-start.11 = (f32[16,8,16,128]{3,2,1,0:T(8,128)S(1)}, f32[16,8,16,128]{3,2,1,0:T(8,128)}, u32[]{:S(2)}, u32[]{:S(2)}) collective-permute-start(f32[16,8,16,128]{3,2,1,0:T(8,128)S(1)} %collective-permute-done.7.rest_2_), channel_id=1, source_target_pairs={{0,8},{1,9},{2,10},{3,11},{4,12},{5,13},{6,14},{7,15},{8,0},{9,1},... | collective-permute-start | bytes 3145736 | tf_op jit(solution)/shard_map/ppermute | solution.py:52
  88.4 8.3 %collective-permute-start.10 = (f32[16,8,16,128]{3,2,1,0:T(8,128)S(1)}, f32[16,8,16,128]{3,2,1,0:T(8,128)}, u32[]{:S(2)}, u32[]{:S(2)}) collective-permute-start(f32[16,8,16,128]{3,2,1,0:T(8,128)S(1)} %collective-permute-done.6.rest_1_), channel_id=1, source_target_pairs={{0,8},{1,9},{2,10},{3,11},{4,12},{5,13},{6,14},{7,15},{8,0},{9,1},... | collective-permute-start | bytes 3145736 | tf_op jit(solution)/shard_map/ppermute | solution.py:52
  91.1 22.9 %all-to-all-start.1 = ((f32[16,16,8,128]{3,2,1,0:T(8,128)}), f32[16,16,8,128]{3,2,1,0:T(8,128)}, u32[]{:S(2)}, u32[]{:S(2)}) async-start(f32[16,16,8,128]{3,2,1,0:T(8,128)} %copy-done.1), calls=%async_computation.1 | async-start | bytes 2097152 | tf_op jit(solution)/shard_map/all_to_all | solution.py:306
  112.5 0.6 copy-start.8

commit v4 on v3

--- a/solution.py
+++ b/solution.py
@@ -15,9 +15,9 @@
 SIDE = 4
 AXES = ("ctx", "smp")
 
-FIRST = ((1, 1, 1), (3, 3, 3), (2, 2, 2))
+FIRST = ((1, 1, 1), (2, 2, 2), (3, 3, 3))
 SECOND = ((2, 0, 0), (0, 2, 0), (0, 0, 2))
-THIRD = ((1, 0, 0), (0, 1, 0), (0, 0, 1))
+THIRD = ((0, 1, 0), (0, 0, 1), (1, 0, 0))
 HELD_FIRST = ((0, 0, 0),) + FIRST
 HELD_SECOND = tuple(
     tuple((a + b) % SIDE for a, b in zip(o, h)) for o in ((0, 0, 0),) + SECOND for h in HELD_FIRST
@@ -32,6 +32,11 @@
 def index_of(x, y, z, core):
     x, y, z = x % SIDE, y % SIDE, z % SIDE
     return ((y * 2 + x // 2) * 2 + core) * 8 + z * 2 + x % 2
+
+
+def over_ctx(array):
+    groups = [[((slot % 8) * 2 + slot // 8) * 8 + smp for slot in range(16)] for smp in range(8)]
+    return lax.all_to_all(array, AXES, split_axis=0, concat_axis=0, tiled=True, axis_index_groups=groups)
 
 
 def take_from(array, offset, mirrored=False):
@@ -69,7 +74,8 @@
     period = R * R
     r = np.arange(R)
     shifted = r + 0.25
-    outer = 2 * np.pi * np.outer(shifted, r) / R
+    rows = np.concatenate([((slot % 8) * 2 + slot // 8) * ROWS + np.arange(ROWS) for slot in range(16)])
+    outer = 2 * np.pi * np.outer(shifted, rows) / R
     first = np.concatenate([np.cos(outer), -np.sin(outer)], 0)
     inner = 2 * np.pi * (np.outer(r, r) % R) / R
     c, s = np.cos(inner), np.sin(inner)
@@ -78,7 +84,8 @@
     twist = 2 * np.pi * np.outer(shifted, r) / period
     turn = np.stack([np.cos(twist), np.sin(twist)]).astype(np.float32)
     real = np.concatenate([np.cos(outer.T), -np.sin(outer.T)], 1)
-    tail = -np.concatenate([np.sin(outer.T), np.cos(outer.T)], 1)[:ROWS]
+    leading = 2 * np.pi * np.outer(r[:ROWS], shifted) / R
+    tail = -np.concatenate([np.sin(leading), np.cos(leading)], 1)
     last = np.concatenate([real, tail, np.zeros((ROWS, 2 * R))], 0)
     f_hi, f_lo = np_halves(first)
     l_hi, l_lo = np_halves(last / period)
@@ -117,8 +124,8 @@
 def spread_kernel(signal_ref, filter_ref, out_ref):
     for k in range(out_ref.shape[0]):
         rows = pl.ds(k * WIDTH, WIDTH)
-        out_ref[k, 0, 0] = signal_ref[rows, :].astype(F32).reshape(WIDTH, ROWS, R)
-        out_ref[k, 0, 1] = filter_ref[rows, :].reshape(WIDTH, ROWS, R)
+        out_ref[k, 0] = signal_ref[rows, :].astype(F32).reshape(WIDTH, ROWS, R)
+        out_ref[k, 1] = filter_ref[rows, :].reshape(WIDTH, ROWS, R)
 
 
 def conv_kernel(base_ref, place_ref, in_ref, skip_hbm, *refs):
@@ -128,7 +135,6 @@
     parts = in_ref.shape[2] // GROUP
     load = pltpu.make_async_copy(skip_hbm, skip_ref, skip_sem)
     load.start()
-    load.wait()
     f_both = first_ref[...]
     f_hi = first_ref[:, :R]
 
@@ -183,6 +189,8 @@
     for step in range(parts + 3):
         for stage, section in ((3, positions), (2, returning), (1, product), (0, columns)):
             part = step - stage
+            if stage == 3 and part == 0:
+                load.wait()
             if 0 <= part < parts:
                 values[part] = section(part, values[part]) if stage else section(part)
     leave = pltpu.make_async_copy(out_ref, out_hbm, out_sem)
@@ -193,7 +201,7 @@
 def finish_kernel(after_ref, conv_ref, gate_ref, out_ref):
     for k in range(conv_ref.shape[0]):
         rows = pl.ds(k * WIDTH, WIDTH)
-        conv = conv_ref[k, 0].reshape(WIDTH, ROWS * R)
+        conv = conv_ref[k].reshape(WIDTH, ROWS * R)
         out_ref[rows, :] = (gate_ref[rows, :].astype(F32) * conv).astype(BF16)
 
 
@@ -247,12 +255,11 @@
         spread_kernel,
         grid=(2,),
         in_specs=[pl.BlockSpec((width_dev // 2, span), lambda k: (k, 0))] * 2,
-        out_specs=pl.BlockSpec((half, 1, 2, WIDTH, ROWS, R), lambda k: (0, k, 0, 0, 0, 0)),
-        out_shape=jax.ShapeDtypeStruct((half, 2, 2, WIDTH, ROWS, R), F32),
+        out_specs=pl.BlockSpec((half, 2, WIDTH, ROWS, R), lambda k: (k, 0, 0, 0, 0)),
+        out_shape=jax.ShapeDtypeStruct((ctx_count, 2, WIDTH, ROWS, R), F32),
         name="spread",
     )(prompt_input, filters)
-    spread = spread.reshape(ctx_count, 2, WIDTH, ROWS, R)
-    regrouped = lax.all_to_all(spread, "ctx", split_axis=0, concat_axis=0, tiled=True)
+    regrouped = over_ctx(spread)
 
     consts = [jnp.asarray(table) for table in tables()]
     consts = consts
@@ -303,19 +310,19 @@
         name="samples",
     )(place, lengths, skip.reshape(1, channels), sample_input, sample_gate, *mine, *other)
 
-    returned = lax.all_to_all(convolved, "ctx", split_axis=0, concat_axis=0, tiled=True)
+    returned = over_ctx(convolved)
     prompt_output = pl.pallas_call(
         finish_kernel,
         grid=(2,),
         in_specs=[
             ANY,
-            pl.BlockSpec((half, 1, WIDTH, ROWS, R), lambda k: (0, k, 0, 0, 0)),
+            pl.BlockSpec((half, WIDTH, ROWS, R), lambda k: (k, 0, 0, 0)),
             pl.BlockSpec((width_dev // 2, span), lambda k: (k, 0)),
         ],
         out_specs=pl.BlockSpec((width_dev // 2, span), lambda k: (k, 0)),
         out_shape=jax.ShapeDtypeStruct((width_dev, span), BF16),
         name="finish",
-    )(done, returned.reshape(half, 2, WIDTH, ROWS, R), prompt_gate)
+    )(done, returned, prompt_gate)
     return prompt_output, sample_output
 
 

time: 117 us -> 115 us (0.983)
  starting transfers between devices: 48.4 us -> 45.2 us
  waiting for transfers between devices: 32.6 us -> 34 us
    ppermute x9, waiting for transfers between devices: 10.7 us -> 14.9 us  [take_from(): return lax.ppermute(array, AXES, pairs)]
    all_to_all x2, waiting for transfers between devices: 21.9 us -> 19.1 us  [over_ctx(): lax.all_to_all(array, AXES, split_axis=0, concat_axis=0, tiled=True, axis...]
    all_to_all x2, starting transfers between devices: 14.2 us -> 12.8 us  [over_ctx(): lax.all_to_all(array, AXES, split_axis=0, concat_axis=0, tiled=True, axis...]
where the time goes in v4:
time: 115 us; the launch traced here: 114 us
  starting transfers between devices  45.2 us (39%)
  waiting for transfers between devices  34 us (30%)
  Pallas kernels  26.3 us (23%)
  local copies, waits for them, and re-layouts  7.59 us (7%)
    ppermute x9, starting transfers between devices, take_from(): return lax.ppermute(array, AXES, pairs)  20 us
    all_to_all x2, waiting for transfers between devices, over_ctx(): lax.all_to_all(array, AXES, split_axis=0, concat_axis=0, tiled=True, axis...  19.1 us
    pallas_call x1, Pallas kernels, on_device(): pl.pallas_call(sample_kernel, grid=(length // R,), in_specs=[SMEM, SMEM,...  15.8 us
    ppermute x9, waiting for transfers between devices, take_from(): return lax.ppermute(array, AXES, pairs)  14.9 us
    all_to_all x2, starting transfers between devices, over_ctx(): lax.all_to_all(array, AXES, split_axis=0, concat_axis=0, tiled=True, axis...  12.8 us
    ppermute x4, starting transfers between devices, swap_cores(): return lax.ppermute(array, AXES, pairs)  12.4 us
    unnamed x26, local copies, waits for them, and re-layouts  6.88 us
    pallas_call x1, Pallas kernels, on_device(): pl.pallas_call(conv_kernel, in_specs=[SMEM, ANY, VMEM, ANY] + [VMEM] * 5...  5.24 us
  transfers between devices with their start and end apart: 15, of which 5 were waited for; matrix products, arithmetic and copies ran while one was open for 1% of the time, Pallas kernels for 14%

profile of v4, /device:TPU:1, one launch (start us, length us, event | category | flops | bytes accessed | tf_op | source)
XLA Modules:
  0.0 114.0 jit_solution(14829420270356853302)
XLA Ops:
  0.6 0.0 copy-start.7
  0.6 2.6 %spread.1.after_ref = f32[16,2,16,8,128]{4,3,2,1,0:T(8,128)} custom-call(bf16[256,1024]{1,0:T(8,128)(2,1)} %signal_ref.1, f32[256,1024]{1,0:T(8,128)} %filter_ref.1), custom_call_target="tpu_custom_call" | custom-call | tf_op jit(solution)/shard_map/spread/pallas_call | solution.py:254
  3.2 0.0 copy-start.9
  3.2 8.6 %all-to-all-start = ((f32[16,2,16,8,128]{4,3,2,1,0:T(8,128)}), f32[16,2,16,8,128]{4,3,2,1,0:T(8,128)S(1)}, u32[]{:S(2)}, u32[]{:S(2)}) async-start(f32[16,2,16,8,128]{4,3,2,1,0:T(8,128)} %spread.1.after_ref), calls=%async_computation | async-start | bytes 4194304 | tf_op jit(solution)/shard_map/all_to_all | solution.py:39
  11.8 0.0 copy-start
  11.8 1.6 %copy-done = f32[16,2,16,8,128]{4,3,2,1,0:T(8,128)S(1)} copy-done((f32[16,2,16,8,128]{4,3,2,1,0:T(8,128)S(1)}, f32[16,2,16,8,128]{4,3,2,1,0:T(8,128)}, u32[]{:S(2)}) %copy-start) | copy-done | bytes 2097176
  13.5 0.0 copy-start.2
  13.5 0.9 copy-done.2
  14.4 0.0 copy-start.3
  14.4 0.9 copy-done.3
  15.4 0.0 copy-start.4
  15.4 0.9 copy-done.4
  16.3 0.0 copy-start.5
  16.3 0.9 copy-done.5
  17.2 0.0 copy-start.6
  17.2 0.9 copy-done.6
  18.1 0.6 hold.1
  18.7 0.7 dynamic-slice_bitcast_fusion.place_ref
  19.4 19.1 %all-to-all-done.in_ref = f32[16,2,16,8,128]{4,3,2,1,0:T(8,128)S(1)} async-done(((f32[16,2,16,8,128]{4,3,2,1,0:T(8,128)}), f32[16,2,16,8,128]{4,3,2,1,0:T(8,128)S(1)}, u32[]{:S(2)}, u32[]{:S(2)}) %all-to-all-start) | async-done | bytes 2097184 | tf_op jit(solution)/shard_map/all_to_all | solution.py:39
  38.5 0.0 copy-done.7
  38.5 5.2 %conv.1 = (f32[16,16,8,128]{3,2,1,0:T(8,128)S(1)}, f32[8,16,128]{2,1,0:T(8,128)S(1)}) custom-call(s32[1]{0:T(128)} %bitcast.2.base_ref, s32[128]{0:T(128)S(1)} %dynamic-slice_bitcast_fusion.place_ref, f32[16,2,16,8,128]{4,3,2,1,0:T(8,128)S(1)} %all-to-all-done.in_ref, f32[2048]{0:T(1024)S(1)} %copy-done.7, bf16[256,256]{1,0:T(8,128)(2,1)S(1)} %get-tuple-element.11.refs_0_, ...), custom_call_target="tpu_custom_call" | custom-call | tf_op jit(solution)/shard_map/conv/pallas_call | solution.py:276
  43.7 0.0 copy-start.1
  43.7 2.6 %collective-permute-start.2 = (f32[1,8,16,128]{3,2,1,0:T(8,128)S(1)}, f32[1,8,16,128]{3,2,1,0:T(8,128)S(1)}, u32[]{:S(2)}, u32[]{:S(2)}) collective-permute-start(f32[1,8,16,128]{3,2,1,0:T(8,128)S(1)} %bitcast.6), channel_id=1, source_target_pairs={{119,0},{102,1},{113,2},{96,3},{115,4},{98,5},{117,6},{100,7},{127... | collective-permute-start | bytes 196616 | tf_op jit(solution)/shard_map/ppermute | solution.py:49
  46.3 6.9 %collective-permute-start.1 = (f32[1,8,16,128]{3,2,1,0:T(8,128)S(1)}, f32[1,8,16,128]{3,2,1,0:T(8,128)S(1)}, u32[]{:S(2)}, u32[]{:S(2)}) collective-permute-start(f32[1,8,16,128]{3,2,1,0:T(8,128)S(1)} %bitcast.7), channel_id=1, source_target_pairs={{84,0},{85,1},{86,2},{87,3},{80,4},{81,5},{82,6},{83,7},{92,8},{93... | collective-permute-start | bytes 196616 | tf_op jit(solution)/shard_map/ppermute | solution.py:49
  53.2 2.3 %collective-permute-start = (f32[1,8,16,128]{3,2,1,0:T(8,128)S(1)}, f32[1,8,16,128]{3,2,1,0:T(8,128)S(1)}, u32[]{:S(2)}, u32[]{:S(2)}) collective-permute-start(f32[1,8,16,128]{3,2,1,0:T(8,128)S(1)} %bitcast.8), channel_id=1, source_target_pairs={{35,0},{50,1},{37,2},{52,3},{39,4},{54,5},{33,6},{48,7},{43,8},{58... | collective-permute-start | bytes 196616 | tf_op jit(solution)/shard_map/ppermute | solution.py:49
  55.5 0.0 collective-permute-done.2
  55.5 1.1 collective-permute-done.1
  56.6 1.5 %collective-permute-done = f32[1,8,16,128]{3,2,1,0:T(8,128)S(1)} collective-permute-done((f32[1,8,16,128]{3,2,1,0:T(8,128)S(1)}, f32[1,8,16,128]{3,2,1,0:T(8,128)S(1)}, u32[]{:S(2)}, u32[]{:S(2)}) %collective-permute-start) | collective-permute-done | bytes 65568 | tf_op jit(solution)/shard_map/ppermute | solution.py:49
  58.1 1.0 collective-permute-start.5
  59.2 2.8 %collective-permute-start.4 = (f32[4,8,16,128]{3,2,1,0:T(8,128)S(1)}, f32[4,8,16,128]{3,2,1,0:T(8,128)S(1)}, u32[]{:S(2)}, u32[]{:S(2)}) collective-permute-start(f32[4,8,16,128]{3,2,1,0:T(8,128)S(1)} %pad_maximum_fusion), channel_id=1, source_target_pairs={{64,0},{65,1},{66,2},{67,3},{68,4},{69,5},{70,6},{71,7},{72,8},{73... | collective-permute-start | bytes 786440 | tf_op jit(solution)/shard_map/ppermute | solution.py:49
  62.0 1.3 %collective-permute-start.3 = (f32[4,8,16,128]{3,2,1,0:T(8,128)S(1)}, f32[4,8,16,128]{3,2,1,0:T(8,128)S(1)}, u32[]{:S(2)}, u32[]{:S(2)}) collective-permute-start(f32[4,8,16,128]{3,2,1,0:T(8,128)S(1)} %pad_maximum_fusion), channel_id=1, source_target_pairs={{16,0},{17,1},{18,2},{19,3},{20,4},{21,5},{22,6},{23,7},{24,8},{25... | collective-permute-start | bytes 786440 | tf_op jit(solution)/shard_map/ppermute | solution.py:49
  63.3 5.7 %collective-permute-done.3 = f32[4,8,16,128]{3,2,1,0:T(8,128)S(1)} collective-permute-done((f32[4,8,16,128]{3,2,1,0:T(8,128)S(1)}, f32[4,8,16,128]{3,2,1,0:T(8,128)S(1)}, u32[]{:S(2)}, u32[]{:S(2)}) %collective-permute-start.3) | collective-permute-done | bytes 262176 | tf_op jit(solution)/shard_map/ppermute | solution.py:49
  69.1 0.0 collective-permute-done.4
  69.1 0.0 collective-permute-done.5
  69.1 0.4 collective-permute-start.8
  69.5 0.3 collective-permute-start.7
  69.8 2.4 %collective-permute-start.6 = (f32[16,8,16,128]{3,2,1,0:T(8,128)S(1)}, f32[16,8,16,128]{3,2,1,0:T(8,128)S(1)}, u32[]{:S(2)}, u32[]{:S(2)}) collective-permute-start(f32[16,8,16,128]{3,2,1,0:T(8,128)S(1)} %constant_dynamic-update-slice_fusion.rest_0_), channel_id=1, source_target_pairs={{32,0},{33,1},{34,2},{35,3},{36,4},{37,5},{38,6},{39,7},{104,8},{1... | collective-permute-start | bytes 3145736 | tf_op jit(solution)/shard_map/ppermute | solution.py:49
  72.2 5.4 %collective-permute-start.9 = (f32[16,8,16,128]{3,2,1,0:T(8,128)S(1)}, f32[16,8,16,128]{3,2,1,0:T(8,128)}, u32[]{:S(2)}, u32[]{:S(2)}) collective-permute-start(f32[16,8,16,128]{3,2,1,0:T(8,128)S(1)} %constant_dynamic-update-slice_fusion.rest_0_), channel_id=1, source_target_pairs={{0,8},{1,9},{2,10},{3,11},{4,12},{5,13},{6,14},{7,15},{8,0},{9,1},... | collective-permute-start | bytes 3145736 | tf_op jit(solution)/shard_map/ppermute | solution.py:57
  77.6 6.5 %collective-permute-done.8.rest_3_ = f32[16,8,16,128]{3,2,1,0:T(8,128)} collective-permute-done((f32[16,8,16,128]{3,2,1,0:T(8,128)S(1)}, f32[16,8,16,128]{3,2,1,0:T(8,128)}, u32[]{:S(2)}, u32[]{:S(2)}) %collective-permute-start.8) | collective-permute-done | bytes 1048608 | tf_op jit(solution)/shard_map/ppermute | solution.py:49
  84.2 3.7 %collective-permute-start.12 = (f32[16,8,16,128]{3,2,1,0:T(8,128)}, f32[16,8,16,128]{3,2,1,0:T(8,128)}, u32[]{:S(2)}, u32[]{:S(2)}) collective-permute-start(f32[16,8,16,128]{3,2,1,0:T(8,128)} %collective-permute-done.8.rest_3_), channel_id=1, source_target_pairs={{0,8},{1,9},{2,10},{3,11},{4,12},{5,13},{6,14},{7,15},{8,0},{9,1},... | collective-permute-start | bytes 3145736 | tf_op jit(solution)/shard_map/ppermute | solution.py:57
  87.9 0.0 collective-permute-done.7.rest_2_
  87.9 2.2 %collective-permute-start.11 = (f32[16,8,16,128]{3,2,1,0:T(8,128)S(1)}, f32[16,8,16,128]{3,2,1,0:T(8,128)}, u32[]{:S(2)}, u32[]{:S(2)}) collective-permute-start(f32[16,8,16,128]{3,2,1,0:T(8,128)S(1)} %collective-permute-done.7.rest_2_), channel_id=1, source_target_pairs={{0,8},{1,9},{2,10},{3,11},{4,12},{5,13},{6,14},{7,15},{8,0},{9,1},... | collective-permute-start | bytes 3145736 | tf_op jit(solution)/shard_map/ppermute | solution.py:57
  90.1 0.0 collective-permute-done.6.rest_1_
  90.1 1.1 collective-permute-start.10
  91.2 0.0 copy-done.1
  91.2 4.2 %all-to-all-start.1 = ((f32[16,16,8,128]{3,2,1,0:T(8,128)}), f32[16,16,8,128]{3,2,1,0:T(8,128)}, u32[]{:S(2)}, u32[]{:S(2)}) async-start(f32[16,16,8,128]{3,2,1,0:T(8,128)} %copy-done.1), calls=%async_computation.1 | async-start | bytes 2097152 | tf_op jit(solution)/shard_map/all_to_all | solution.py:39
  95.4 0.0 collective-permute-done.9.rest_4_
  95.4 0.0 collective-permute-done.12.rest_7_
  95.4 0.0 collective-permute-done.11.rest_6_
  95.4 0.0 collective-permute-done.10.rest_5_
  95.4 0.0 copy-done.9
  95.5 15.8 %samples.1 = (bf16[2,1024,2048]{2,1,0:T(8,128)(2,1)}, f32[8,128]{1,0:T(8,128)S(1)}) custom-call(s32[128]{0:T(128)S(1)} %dynamic-slice_bitcast_fusion.place_ref, s32[2]{0:T(128)S(1)} %copy-done.9, f32[1,2048]{1,0:T(1,128)S(1)} %bitcast.10, bf16[2,1024,2048]{2,1,0:T(8,128)(2,1)} %input_ref.1, bf16[2,1024,2048]{2,1,0:T(8,128)(2,1)} %gate_ref.2, ...), custom_call_target="tpu_custom_call" | custom-call | tf_op jit(solution)/shard_map/samples/pallas_call | solution.py:302
  111.2 0.0 copy-start.8
  111.2 0.6 copy-done.8
  111.8 0.0 all-to-all-done.1.conv_ref
  111.8 2.2 %finish.1 = bf16[256,1024]{1,0:T(8,128)(2,1)} custom-call(f32[8,128]{1,0:T(8,128)} %copy-done.8, f32[16,16,8,128]{3,2,1,0:T(8,128)} %all-to-all-done.1.conv_ref, bf16[256,1024]{1,0:T(8,128)(2,1)} %gate_ref.3), custom_call_target="tpu_custom_call" | custom-call | tf_op jit(solution)/shard_map/finish/pallas_call | solution.py:314
  (8 shorter events, 0.1 us)
Async XLA Ops:
  0.6 37.9 %copy-start.7 = (f32[2048]{0:T(1024)S(1)}, f32[2048]{0:T(1024)}, u32[]{:S(2)}) copy-start(f32[2048]{0:T(1024)} %skip_hbm.1) | copy-start | bytes 24580
  3.2 92.2 %copy-start.9 = (s32[2]{0:T(128)S(1)}, s32[2]{0:T(128)}, u32[]{:S(2)}) copy-start(s32[2]{0:T(128)} %lengths_ref.1) | copy-start | bytes 28
  3.2 35.2 %all-to-all-start = ((f32[16,2,16,8,128]{4,3,2,1,0:T(8,128)}), f32[16,2,16,8,128]{4,3,2,1,0:T(8,128)S(1)}, u32[]{:S(2)}, u32[]{:S(2)}) async-start(f32[16,2,16,8,128]{4,3,2,1,0:T(8,128)} %spread.1.after_ref), calls=%async_computation | async-start | bytes 4194304 | tf_op jit(solution)/shard_map/all_to_all | solution.py:39
  11.8 1.6 %copy-start = (f32[16,2,16,8,128]{4,3,2,1,0:T(8,128)S(1)}, f32[16,2,16,8,128]{4,3,2,1,0:T(8,128)}, u32[]{:S(2)}) copy-start(f32[16,2,16,8,128]{4,3,2,1,0:T(8,128)} %spread.1.after_ref) | copy-start | bytes 6291460
  13.5 0.9 copy-start.2
  14.4 0.9 copy-start.3
  15.4 0.9 copy-start.4
  16.3 0.9 copy-start.5
  17.2 0.9 copy-start.6
  43.7 47.4 %copy-start.1 = (f32[16,16,8,128]{3,2,1,0:T(8,128)}, f32[16,16,8,128]{3,2,1,0:T(8,128)S(1)}, u32[]{:S(2)}) copy-start(f32[16,16,8,128]{3,2,1,0:T(8,128)S(1)} %get-tuple-element.18) | copy-start | bytes 3145732
  43.7 11.8 %collective-permute-start.2 = (f32[1,8,16,128]{3,2,1,0:T(8,128)S(1)}, f32[1,8,16,128]{3,2,1,0:T(8,128)S(1)}, u32[]{:S(2)}, u32[]{:S(2)}) collective-permute-start(f32[1,8,16,128]{3,2,1,0:T(8,128)S(1)} %bitcast.6), channel_id=1, source_target_pairs={{119,0},{102,1},{113,2},{96,3},{115,4},{98,5},{117,6},{100,7},{127... | collective-permute-start | bytes 196616 | tf_op jit(solution)/shard_map/ppermute | solution.py:49
  46.3 10.2 %collective-permute-start.1 = (f32[1,8,16,128]{3,2,1,0:T(8,128)S(1)}, f32[1,8,16,128]{3,2,1,0:T(8,128)S(1)}, u32[]{:S(2)}, u32[]{:S(2)}) collective-permute-start(f32[1,8,16,128]{3,2,1,0:T(8,128)S(1)} %bitcast.7), channel_id=1, source_target_pairs={{84,0},{85,1},{86,2},{87,3},{80,4},{81,5},{82,6},{83,7},{92,8},{93... | collective-permute-start | bytes 196616 | tf_op jit(solution)/shard_map/ppermute | solution.py:49
  53.2 4.9 %collective-permute-start = (f32[1,8,16,128]{3,2,1,0:T(8,128)S(1)}, f32[1,8,16,128]{3,2,1,0:T(8,128)S(1)}, u32[]{:S(2)}, u32[]{:S(2)}) collective-permute-start(f32[1,8,16,128]{3,2,1,0:T(8,128)S(1)} %bitcast.8), channel_id=1, source_target_pairs={{35,0},{50,1},{37,2},{52,3},{39,4},{54,5},{33,6},{48,7},{43,8},{58... | collective-permute-start | bytes 196616 | tf_op jit(solution)/shard_map/ppermute | solution.py:49
  58.1 11.0 %collective-permute-start.5 = (f32[4,8,16,128]{3,2,1,0:T(8,128)S(1)}, f32[4,8,16,128]{3,2,1,0:T(8,128)S(1)}, u32[]{:S(2)}, u32[]{:S(2)}) collective-permute-start(f32[4,8,16,128]{3,2,1,0:T(8,128)S(1)} %pad_maximum_fusion), channel_id=1, source_target_pairs={{4,0},{5,1},{6,2},{7,3},{0,4},{1,5},{2,6},{3,7},{12,8},{13,9},{14,... | collective-permute-start | bytes 786440 | tf_op jit(solution)/shard_map/ppermute | solution.py:49
  59.2 9.9 %collective-permute-start.4 = (f32[4,8,16,128]{3,2,1,0:T(8,128)S(1)}, f32[4,8,16,128]{3,2,1,0:T(8,128)S(1)}, u32[]{:S(2)}, u32[]{:S(2)}) collective-permute-start(f32[4,8,16,128]{3,2,1,0:T(8,128)S(1)} %pad_maximum_fusion), channel_id=1, source_target_pairs={{64,0},{65,1},{66,2},{67,3},{68,4},{69,5},{70,6},{71,7},{72,8},{73... | collective-permute-start | bytes 786440 | tf_op jit(solution)/shard_map/ppermute | solution.py:49
  62.0 7.0 %collective-permute-start.3 = (f32[4,8,16,128]{3,2,1,0:T(8,128)S(1)}, f32[4,8,16,128]{3,2,1,0:T(8,128)S(1)}, u32[]{:S(2)}, u32[]{:S(2)}) collective-permute-start(f32[4,8,16,128]{3,2,1,0:T(8,128)S(1)} %pad_maximum_fusion), channel_id=1, source_target_pairs={{16,0},{17,1},{18,2},{19,3},{20,4},{21,5},{22,6},{23,7},{24,8},{25... | collective-permute-start | bytes 786440 | tf_op jit(solution)/shard_map/ppermute | solution.py:49
  69.1 15.0 %collective-permute-start.8 = (f32[16,8,16,128]{3,2,1,0:T(8,128)S(1)}, f32[16,8,16,128]{3,2,1,0:T(8,128)}, u32[]{:S(2)}, u32[]{:S(2)}) collective-permute-start(f32[16,8,16,128]{3,2,1,0:T(8,128)S(1)} %constant_dynamic-update-slice_fusion.rest_0_), channel_id=1, source_target_pairs={{1,0},{16,1},{3,2},{18,3},{5,4},{20,5},{7,6},{22,7},{25,8},{8,9},{... | collective-permute-start | bytes 3145736 | tf_op jit(solution)/shard_map/ppermute | solution.py:49
  69.5 18.4 %collective-permute-start.7 = (f32[16,8,16,128]{3,2,1,0:T(8,128)S(1)}, f32[16,8,16,128]{3,2,1,0:T(8,128)S(1)}, u32[]{:S(2)}, u32[]{:S(2)}) collective-permute-start(f32[16,8,16,128]{3,2,1,0:T(8,128)S(1)} %constant_dynamic-update-slice_fusion.rest_0_), channel_id=1, source_target_pairs={{2,0},{3,1},{4,2},{5,3},{6,4},{7,5},{0,6},{1,7},{14,8},{15,9},{8,1... | collective-permute-start | bytes 3145736 | tf_op jit(solution)/shard_map/ppermute | solution.py:49
  69.8 20.3 %collective-permute-start.6 = (f32[16,8,16,128]{3,2,1,0:T(8,128)S(1)}, f32[16,8,16,128]{3,2,1,0:T(8,128)S(1)}, u32[]{:S(2)}, u32[]{:S(2)}) collective-permute-start(f32[16,8,16,128]{3,2,1,0:T(8,128)S(1)} %constant_dynamic-update-slice_fusion.rest_0_), channel_id=1, source_target_pairs={{32,0},{33,1},{34,2},{35,3},{36,4},{37,5},{38,6},{39,7},{104,8},{1... | collective-permute-start | bytes 3145736 | tf_op jit(solution)/shard_map/ppermute | solution.py:49
  72.2 23.2 %collective-permute-start.9 = (f32[16,8,16,128]{3,2,1,0:T(8,128)S(1)}, f32[16,8,16,128]{3,2,1,0:T(8,128)}, u32[]{:S(2)}, u32[]{:S(2)}) collective-permute-start(f32[16,8,16,128]{3,2,1,0:T(8,128)S(1)} %constant_dynamic-update-slice_fusion.rest_0_), channel_id=1, source_target_pairs={{0,8},{1,9},{2,10},{3,11},{4,12},{5,13},{6,14},{7,15},{8,0},{9,1},... | collective-permute-start | bytes 3145736 | tf_op jit(solution)/shard_map/ppermute | solution.py:57
  84.2 11.3 %collective-permute-start.12 = (f32[16,8,16,128]{3,2,1,0:T(8,128)}, f32[16,8,16,128]{3,2,1,0:T(8,128)}, u32[]{:S(2)}, u32[]{:S(2)}) collective-permute-start(f32[16,8,16,128]{3,2,1,0:T(8,128)} %collective-permute-done.8.rest_3_), channel_id=1, source_target_pairs={{0,8},{1,9},{2,10},{3,11},{4,12},{5,13},{6,14},{7,15},{8,0},{9,1},... | collective-permute-start | bytes 3145736 | tf_op jit(solution)/shard_map/ppermute | solution.py:57
  87.9 7.5 %collective-permute-start.11 = (f32[16,8,16,128]{3,2,1,0:T(8,128)S(1)}, f32[16,8,16,128]{3,2,1,0:T(8,128)}, u32[]{:S(2)}, u32[]{:S(2)}) collective-permute-start(f32[16,8,16,128]{3,2,1,0:T(8,128)S(1)} %collective-permute-done.7.rest_2_), channel_id=1, source_target_pairs={{0,8},{1,9},{2,10},{3,11},{4,12},{5,13},{6,14},{7,15},{8,0},{9,1},... | collective-permute-start | bytes 3145736 | tf_op jit(solution)/shard_map/ppermute | solution.py:57
  90.1 5.4 %collective-permute-start.10 = (f32[16,8,16,128]{3,2,1,0:T(8,128)S(1)}, f32[16,8,16,128]{3,2,1,0:T(8,128)}, u32[]{:S(2)}, u32[]{:S(2)}) collective-permute-start(f32[16,8,16,128]{3,2,1,0:T(8,128)S(1)} %collective-permute-done.6.rest_1_), channel_id=1, source_target_pairs={{0,8},{1,9},{2,10},{3,11},{4,12},{5,13},{6,14},{7,15},{8,0},{9,1},... | collective-permute-start | bytes 3145736 | tf_op jit(solution)/shard_map/ppermute | solution.py:57
  91.2 20.6 %all-to-all-start.1 = ((f32[16,16,8,128]{3,2,1,0:T(8,128)}), f32[16,16,8,128]{3,2,1,0:T(8,128)}, u32[]{:S(2)}, u32[]{:S(2)}) async-start(f32[16,16,8,128]{3,2,1,0:T(8,128)} %copy-done.1), calls=%async_computation.1 | async-start | bytes 2097152 | tf_op jit(solution)/shard_map/all_to_all | solution.py:39
  111.2 0.6 copy-start.8

commit v5 on v4

--- a/solution.py
+++ b/solution.py
@@ -214,28 +214,47 @@
         copy.wait()
 
 
-def sample_kernel(place_ref, lengths_ref, skip_ref, input_ref, gate_ref, *rest):
-    pieces, (out_ref, done_ref, tail_ref, sem) = rest[:8], rest[8:]
-    step = pl.program_id(0)
-
-    @pl.when(step == 0)
-    def _():
-        done_ref[...] = jnp.zeros_like(done_ref)
-        for array, piece_ref in enumerate(pieces):
-            for slot in range(16):
-                channel = pl.multiple_of(place_ref[array * 16 + slot], WIDTH)
-                pltpu.make_async_copy(piece_ref.at[slot], tail_ref.at[:, pl.ds(channel, WIDTH)], sem).start()
-        pltpu.make_async_copy(tail_ref, tail_ref, sem).wait()
-
-    positions = step * R + lax.broadcasted_iota(jnp.int32, (R, R), 0)
-    for block in range(tail_ref.shape[1] // R):
-        cols = pl.ds(block * R, R)
-        state = tail_ref[step, cols, :].T
+def sample_kernel(place_ref, lengths_ref, skip_ref, input_hbm, gate_hbm, *rest):
+    pieces, (out_hbm, tail_ref, input_ref, gate_ref, out_ref, tail_sem, in_sem, out_sem) = rest[:8], rest[8:]
+    steps = input_ref.shape[1] // R
+
+    def fetches(step, i):
+        rows = pl.ds(pl.multiple_of(step * R, R), R)
+        return [
+            pltpu.make_async_copy(input_hbm.at[i, rows], input_ref.at[i, rows], in_sem.at[step, i, 0]),
+            pltpu.make_async_copy(gate_hbm.at[i, rows], gate_ref.at[i, rows], in_sem.at[step, i, 1]),
+        ]
+
+    for array, piece_ref in enumerate(pieces):
+        for slot in range(16):
+            channel = pl.multiple_of(place_ref[array * 16 + slot], WIDTH)
+            pltpu.make_async_copy(piece_ref.at[slot], tail_ref.at[:, pl.ds(channel, WIDTH)], tail_sem).start()
+    for step in range(steps):
         for i in range(input_ref.shape[0]):
-            blended = gate_ref[i, :, cols].astype(F32) * (
-                state + skip_ref[:, cols] * input_ref[i, :, cols].astype(F32)
-            )
-            out_ref[i, :, cols] = jnp.where(positions < lengths_ref[i], blended, 0.0).astype(BF16)
+            for fetch in fetches(step, i):
+                fetch.start()
+    pltpu.make_async_copy(tail_ref, tail_ref, tail_sem).wait()
+
+    def rows_of(step, carry):
+        here = pl.ds(pl.multiple_of(step * R, R), R)
+        positions = step * R + lax.broadcasted_iota(jnp.int32, (R, R), 0)
+        for i in range(input_ref.shape[0]):
+            for fetch in fetches(step, i):
+                fetch.wait()
+        for block in range(tail_ref.shape[1] // R):
+            cols = pl.ds(block * R, R)
+            state = tail_ref[step, cols, :].T
+            for i in range(input_ref.shape[0]):
+                blended = gate_ref[i, here, cols].astype(F32) * (
+                    state + skip_ref[:, cols] * input_ref[i, here, cols].astype(F32)
+                )
+                out_ref[i, here, cols] = jnp.where(positions < lengths_ref[i], blended, 0.0).astype(BF16)
+        for i in range(input_ref.shape[0]):
+            pltpu.make_async_copy(out_ref.at[i, here], out_hbm.at[i, here], out_sem).start()
+        return carry
+
+    lax.fori_loop(0, steps, rows_of, 0)
+    pltpu.make_async_copy(out_ref, out_hbm, out_sem).wait()
 
 
 VMEM = pl.BlockSpec(memory_space=pltpu.VMEM)
@@ -298,14 +317,18 @@
     other = [swap_cores(part) for part in mine]
 
     local, length, channels = sample_input.shape
-    block = pl.BlockSpec((local, R, channels), lambda j: (0, j, 0))
-    sample_output, done = pl.pallas_call(
+    sample_output = pl.pallas_call(
         sample_kernel,
-        grid=(length // R,),
-        in_specs=[SMEM, SMEM, pl.BlockSpec((1, channels), lambda j: (0, 0)), block, block] + [ANY] * 8,
-        out_specs=[block, pl.BlockSpec((8, R), lambda j: (0, 0))],
-        out_shape=[jax.ShapeDtypeStruct(sample_input.shape, BF16), jax.ShapeDtypeStruct((8, R), F32)],
-        scratch_shapes=[pltpu.VMEM((ROWS, channels, R), F32), pltpu.SemaphoreType.DMA],
+        in_specs=[SMEM, SMEM, VMEM, ANY, ANY] + [ANY] * 8,
+        out_specs=ANY,
+        out_shape=jax.ShapeDtypeStruct(sample_input.shape, BF16),
+        scratch_shapes=[
+            pltpu.VMEM((ROWS, channels, R), F32),
+            *[pltpu.VMEM(sample_input.shape, BF16)] * 3,
+            pltpu.SemaphoreType.DMA,
+            pltpu.SemaphoreType.DMA((length // R, local, 2)),
+            pltpu.SemaphoreType.DMA,
+        ],
         compiler_params=pltpu.CompilerParams(vmem_limit_bytes=50 * 2**20),
         name="samples",
     )(place, lengths, skip.reshape(1, channels), sample_input, sample_gate, *mine, *other)
@@ -322,7 +345,7 @@
         out_specs=pl.BlockSpec((width_dev // 2, span), lambda k: (k, 0)),
         out_shape=jax.ShapeDtypeStruct((width_dev, span), BF16),
         name="finish",
-    )(done, returned, prompt_gate)
+    )(sample_output, returned, prompt_gate)
     return prompt_output, sample_output
 
 

time: 115 us -> 113 us (0.983)
  Pallas kernels: 26.3 us -> 24.7 us
    pallas_call x1, Pallas kernels: 15.8 us -> 14.1 us  [on_device(): pl.pallas_call(sample_kernel, in_specs=[SMEM, SMEM, VMEM, ANY, ANY] + [AN...]
    unnamed x26 -> x24, local copies, waits for them, and re-layouts: 6.88 us -> 6.31 us
  transfers between devices with their start and end apart: 15 -> 15, of which waited for: 5 -> 6; matrix products, arithmetic and copies ran while one was open for 1% -> 1% of each run, Pallas kernels for 14% -> 13%
where the time goes in v5:
time: 113 us
  starting transfers between devices  45.2 us (40%)
  waiting for transfers between devices  34.9 us (31%)
  Pallas kernels  24.7 us (22%)
  local copies, waits for them, and re-layouts  7.03 us (6%)
    all_to_all x2, waiting for transfers between devices, over_ctx(): lax.all_to_all(array, AXES, split_axis=0, concat_axis=0, tiled=True, axis...  20 us
    ppermute x9, starting transfers between devices, take_from(): return lax.ppermute(array, AXES, pairs)  20 us
    ppermute x9, waiting for transfers between devices, take_from(): return lax.ppermute(array, AXES, pairs)  14.9 us
    pallas_call x1, Pallas kernels, on_device(): pl.pallas_call(sample_kernel, in_specs=[SMEM, SMEM, VMEM, ANY, ANY] + [AN...  14.1 us
    all_to_all x2, starting transfers between devices, over_ctx(): lax.all_to_all(array, AXES, split_axis=0, concat_axis=0, tiled=True, axis...  12.8 us
    ppermute x4, starting transfers between devices, swap_cores(): return lax.ppermute(array, AXES, pairs)  12.4 us
    unnamed x24, local copies, waits for them, and re-layouts  6.31 us
    pallas_call x1, Pallas kernels, on_device(): pl.pallas_call(conv_kernel, in_specs=[SMEM, ANY, VMEM, ANY] + [VMEM] * 5...  5.24 us
  transfers between devices with their start and end apart: 15, of which 6 were waited for; matrix products, arithmetic and copies ran while one was open for 1% of the time, Pallas kernels for 13%

profile of v5, /device:TPU:1, one launch (start us, length us, event | category | flops | bytes accessed | tf_op | source)
XLA Modules:
  0.0 112.6 jit_solution(14432513237717887123)
XLA Ops:
  0.6 0.0 copy-start.7
  0.6 2.6 %spread.1.after_ref = f32[16,2,16,8,128]{4,3,2,1,0:T(8,128)} custom-call(bf16[256,1024]{1,0:T(8,128)(2,1)} %signal_ref.1, f32[256,1024]{1,0:T(8,128)} %filter_ref.1), custom_call_target="tpu_custom_call" | custom-call | tf_op jit(solution)/shard_map/spread/pallas_call | solution.py:273
  3.2 0.0 copy-start.8
  3.2 8.6 %all-to-all-start = ((f32[16,2,16,8,128]{4,3,2,1,0:T(8,128)}), f32[16,2,16,8,128]{4,3,2,1,0:T(8,128)S(1)}, u32[]{:S(2)}, u32[]{:S(2)}) async-start(f32[16,2,16,8,128]{4,3,2,1,0:T(8,128)} %spread.1.after_ref), calls=%async_computation | async-start | bytes 4194304 | tf_op jit(solution)/shard_map/all_to_all | solution.py:39
  11.8 0.0 copy-start
  11.8 1.6 %copy-done = f32[16,2,16,8,128]{4,3,2,1,0:T(8,128)S(1)} copy-done((f32[16,2,16,8,128]{4,3,2,1,0:T(8,128)S(1)}, f32[16,2,16,8,128]{4,3,2,1,0:T(8,128)}, u32[]{:S(2)}) %copy-start) | copy-done | bytes 2097176
  13.5 0.0 copy-start.2
  13.5 0.9 copy-done.2
  14.4 0.0 copy-start.3
  14.4 0.9 copy-done.3
  15.4 0.0 copy-start.4
  15.4 0.9 copy-done.4
  16.3 0.0 copy-start.5
  16.3 0.9 copy-done.5
  17.2 0.0 copy-start.6
  17.2 0.9 copy-done.6
  18.1 0.6 hold.1
  18.7 0.7 dynamic-slice_bitcast_fusion.place_ref
  19.4 19.1 %all-to-all-done.in_ref = f32[16,2,16,8,128]{4,3,2,1,0:T(8,128)S(1)} async-done(((f32[16,2,16,8,128]{4,3,2,1,0:T(8,128)}), f32[16,2,16,8,128]{4,3,2,1,0:T(8,128)S(1)}, u32[]{:S(2)}, u32[]{:S(2)}) %all-to-all-start) | async-done | bytes 2097184 | tf_op jit(solution)/shard_map/all_to_all | solution.py:39
  38.5 0.0 copy-done.7
  38.5 5.2 %conv.1 = (f32[16,16,8,128]{3,2,1,0:T(8,128)S(1)}, f32[8,16,128]{2,1,0:T(8,128)S(1)}) custom-call(s32[1]{0:T(128)} %bitcast.2.base_ref, s32[128]{0:T(128)S(1)} %dynamic-slice_bitcast_fusion.place_ref, f32[16,2,16,8,128]{4,3,2,1,0:T(8,128)S(1)} %all-to-all-done.in_ref, f32[2048]{0:T(1024)S(1)} %copy-done.7, bf16[256,256]{1,0:T(8,128)(2,1)S(1)} %get-tuple-element.9.refs_0_, ...), custom_call_target="tpu_custom_call" | custom-call | tf_op jit(solution)/shard_map/conv/pallas_call | solution.py:295
  43.7 0.0 copy-start.1
  43.7 2.6 %collective-permute-start.2 = (f32[1,8,16,128]{3,2,1,0:T(8,128)S(1)}, f32[1,8,16,128]{3,2,1,0:T(8,128)S(1)}, u32[]{:S(2)}, u32[]{:S(2)}) collective-permute-start(f32[1,8,16,128]{3,2,1,0:T(8,128)S(1)} %bitcast.6), channel_id=1, source_target_pairs={{119,0},{102,1},{113,2},{96,3},{115,4},{98,5},{117,6},{100,7},{127... | collective-permute-start | bytes 196616 | tf_op jit(solution)/shard_map/ppermute | solution.py:49
  46.3 6.9 %collective-permute-start.1 = (f32[1,8,16,128]{3,2,1,0:T(8,128)S(1)}, f32[1,8,16,128]{3,2,1,0:T(8,128)S(1)}, u32[]{:S(2)}, u32[]{:S(2)}) collective-permute-start(f32[1,8,16,128]{3,2,1,0:T(8,128)S(1)} %bitcast.7), channel_id=1, source_target_pairs={{84,0},{85,1},{86,2},{87,3},{80,4},{81,5},{82,6},{83,7},{92,8},{93... | collective-permute-start | bytes 196616 | tf_op jit(solution)/shard_map/ppermute | solution.py:49
  53.2 2.3 %collective-permute-start = (f32[1,8,16,128]{3,2,1,0:T(8,128)S(1)}, f32[1,8,16,128]{3,2,1,0:T(8,128)S(1)}, u32[]{:S(2)}, u32[]{:S(2)}) collective-permute-start(f32[1,8,16,128]{3,2,1,0:T(8,128)S(1)} %bitcast.8), channel_id=1, source_target_pairs={{35,0},{50,1},{37,2},{52,3},{39,4},{54,5},{33,6},{48,7},{43,8},{58... | collective-permute-start | bytes 196616 | tf_op jit(solution)/shard_map/ppermute | solution.py:49
  55.5 0.0 collective-permute-done.2
  55.5 1.1 collective-permute-done.1
  56.6 1.5 %collective-permute-done = f32[1,8,16,128]{3,2,1,0:T(8,128)S(1)} collective-permute-done((f32[1,8,16,128]{3,2,1,0:T(8,128)S(1)}, f32[1,8,16,128]{3,2,1,0:T(8,128)S(1)}, u32[]{:S(2)}, u32[]{:S(2)}) %collective-permute-start) | collective-permute-done | bytes 65568 | tf_op jit(solution)/shard_map/ppermute | solution.py:49
  58.1 1.0 collective-permute-start.5
  59.2 2.8 %collective-permute-start.4 = (f32[4,8,16,128]{3,2,1,0:T(8,128)S(1)}, f32[4,8,16,128]{3,2,1,0:T(8,128)S(1)}, u32[]{:S(2)}, u32[]{:S(2)}) collective-permute-start(f32[4,8,16,128]{3,2,1,0:T(8,128)S(1)} %pad_maximum_fusion), channel_id=1, source_target_pairs={{64,0},{65,1},{66,2},{67,3},{68,4},{69,5},{70,6},{71,7},{72,8},{73... | collective-permute-start | bytes 786440 | tf_op jit(solution)/shard_map/ppermute | solution.py:49
  62.0 1.3 %collective-permute-start.3 = (f32[4,8,16,128]{3,2,1,0:T(8,128)S(1)}, f32[4,8,16,128]{3,2,1,0:T(8,128)S(1)}, u32[]{:S(2)}, u32[]{:S(2)}) collective-permute-start(f32[4,8,16,128]{3,2,1,0:T(8,128)S(1)} %pad_maximum_fusion), channel_id=1, source_target_pairs={{16,0},{17,1},{18,2},{19,3},{20,4},{21,5},{22,6},{23,7},{24,8},{25... | collective-permute-start | bytes 786440 | tf_op jit(solution)/shard_map/ppermute | solution.py:49
  63.3 5.7 %collective-permute-done.3 = f32[4,8,16,128]{3,2,1,0:T(8,128)S(1)} collective-permute-done((f32[4,8,16,128]{3,2,1,0:T(8,128)S(1)}, f32[4,8,16,128]{3,2,1,0:T(8,128)S(1)}, u32[]{:S(2)}, u32[]{:S(2)}) %collective-permute-start.3) | collective-permute-done | bytes 262176 | tf_op jit(solution)/shard_map/ppermute | solution.py:49
  69.1 0.0 collective-permute-done.4
  69.1 0.0 collective-permute-done.5
  69.1 0.4 collective-permute-start.8
  69.5 0.3 collective-permute-start.7
  69.8 2.4 %collective-permute-start.6 = (f32[16,8,16,128]{3,2,1,0:T(8,128)S(1)}, f32[16,8,16,128]{3,2,1,0:T(8,128)S(1)}, u32[]{:S(2)}, u32[]{:S(2)}) collective-permute-start(f32[16,8,16,128]{3,2,1,0:T(8,128)S(1)} %constant_dynamic-update-slice_fusion.rest_0_), channel_id=1, source_target_pairs={{32,0},{33,1},{34,2},{35,3},{36,4},{37,5},{38,6},{39,7},{104,8},{1... | collective-permute-start | bytes 3145736 | tf_op jit(solution)/shard_map/ppermute | solution.py:49
  72.2 5.4 %collective-permute-start.9 = (f32[16,8,16,128]{3,2,1,0:T(8,128)S(1)}, f32[16,8,16,128]{3,2,1,0:T(8,128)}, u32[]{:S(2)}, u32[]{:S(2)}) collective-permute-start(f32[16,8,16,128]{3,2,1,0:T(8,128)S(1)} %constant_dynamic-update-slice_fusion.rest_0_), channel_id=1, source_target_pairs={{0,8},{1,9},{2,10},{3,11},{4,12},{5,13},{6,14},{7,15},{8,0},{9,1},... | collective-permute-start | bytes 3145736 | tf_op jit(solution)/shard_map/ppermute | solution.py:57
  77.6 6.5 %collective-permute-done.8.rest_3_ = f32[16,8,16,128]{3,2,1,0:T(8,128)} collective-permute-done((f32[16,8,16,128]{3,2,1,0:T(8,128)S(1)}, f32[16,8,16,128]{3,2,1,0:T(8,128)}, u32[]{:S(2)}, u32[]{:S(2)}) %collective-permute-start.8) | collective-permute-done | bytes 1048608 | tf_op jit(solution)/shard_map/ppermute | solution.py:49
  84.2 3.7 %collective-permute-start.12 = (f32[16,8,16,128]{3,2,1,0:T(8,128)}, f32[16,8,16,128]{3,2,1,0:T(8,128)}, u32[]{:S(2)}, u32[]{:S(2)}) collective-permute-start(f32[16,8,16,128]{3,2,1,0:T(8,128)} %collective-permute-done.8.rest_3_), channel_id=1, source_target_pairs={{0,8},{1,9},{2,10},{3,11},{4,12},{5,13},{6,14},{7,15},{8,0},{9,1},... | collective-permute-start | bytes 3145736 | tf_op jit(solution)/shard_map/ppermute | solution.py:57
  87.9 0.0 collective-permute-done.7.rest_2_
  87.9 2.2 %collective-permute-start.11 = (f32[16,8,16,128]{3,2,1,0:T(8,128)S(1)}, f32[16,8,16,128]{3,2,1,0:T(8,128)}, u32[]{:S(2)}, u32[]{:S(2)}) collective-permute-start(f32[16,8,16,128]{3,2,1,0:T(8,128)S(1)} %collective-permute-done.7.rest_2_), channel_id=1, source_target_pairs={{0,8},{1,9},{2,10},{3,11},{4,12},{5,13},{6,14},{7,15},{8,0},{9,1},... | collective-permute-start | bytes 3145736 | tf_op jit(solution)/shard_map/ppermute | solution.py:57
  90.1 0.0 collective-permute-done.6.rest_1_
  90.1 1.1 collective-permute-start.10
  91.2 0.0 copy-done.1
  91.2 4.2 %all-to-all-start.1 = ((f32[16,16,8,128]{3,2,1,0:T(8,128)}), f32[16,16,8,128]{3,2,1,0:T(8,128)}, u32[]{:S(2)}, u32[]{:S(2)}) async-start(f32[16,16,8,128]{3,2,1,0:T(8,128)} %copy-done.1), calls=%async_computation.1 | async-start | bytes 2097152 | tf_op jit(solution)/shard_map/all_to_all | solution.py:39
  95.4 0.0 collective-permute-done.9.rest_4_
  95.4 0.0 collective-permute-done.12.rest_7_
  95.4 0.0 collective-permute-done.11.rest_6_
  95.4 0.0 collective-permute-done.10.rest_5_
  95.5 0.0 copy-done.8
  95.5 14.1 %samples.1.after_ref = bf16[2,1024,2048]{2,1,0:T(8,128)(2,1)} custom-call(s32[128]{0:T(128)S(1)} %dynamic-slice_bitcast_fusion.place_ref, s32[2]{0:T(128)S(1)} %copy-done.8, f32[1,2048]{1,0:T(1,128)S(1)} %bitcast.10, bf16[2,1024,2048]{2,1,0:T(8,128)(2,1)} %input_hbm.1, bf16[2,1024,2048]{2,1,0:T(8,128)(2,1)} %gate_hbm.1, ...), custom_call_target="tpu_custom_call" | custom-call | tf_op jit(solution)/shard_map/samples/pallas_call | solution.py:320
  109.6 0.9 all-to-all-done.1.conv_ref
  110.5 2.2 %finish.1 = bf16[256,1024]{1,0:T(8,128)(2,1)} custom-call(bf16[2,1024,2048]{2,1,0:T(8,128)(2,1)} %samples.1.after_ref, f32[16,16,8,128]{3,2,1,0:T(8,128)} %all-to-all-done.1.conv_ref, bf16[256,1024]{1,0:T(8,128)(2,1)} %gate_ref.1), custom_call_target="tpu_custom_call" | custom-call | tf_op jit(solution)/shard_map/finish/pallas_call | solution.py:337
  (8 shorter events, 0.1 us)
Async XLA Ops:
  0.6 37.9 %copy-start.7 = (f32[2048]{0:T(1024)S(1)}, f32[2048]{0:T(1024)}, u32[]{:S(2)}) copy-start(f32[2048]{0:T(1024)} %skip_hbm.1) | copy-start | bytes 24580
  3.2 92.2 %copy-start.8 = (s32[2]{0:T(128)S(1)}, s32[2]{0:T(128)}, u32[]{:S(2)}) copy-start(s32[2]{0:T(128)} %lengths_ref.1) | copy-start | bytes 28
  3.2 35.2 %all-to-all-start = ((f32[16,2,16,8,128]{4,3,2,1,0:T(8,128)}), f32[16,2,16,8,128]{4,3,2,1,0:T(8,128)S(1)}, u32[]{:S(2)}, u32[]{:S(2)}) async-start(f32[16,2,16,8,128]{4,3,2,1,0:T(8,128)} %spread.1.after_ref), calls=%async_computation | async-start | bytes 4194304 | tf_op jit(solution)/shard_map/all_to_all | solution.py:39
  11.8 1.6 %copy-start = (f32[16,2,16,8,128]{4,3,2,1,0:T(8,128)S(1)}, f32[16,2,16,8,128]{4,3,2,1,0:T(8,128)}, u32[]{:S(2)}) copy-start(f32[16,2,16,8,128]{4,3,2,1,0:T(8,128)} %spread.1.after_ref) | copy-start | bytes 6291460
  13.5 0.9 copy-start.2
  14.4 0.9 copy-start.3
  15.4 0.9 copy-start.4
  16.3 0.9 copy-start.5
  17.2 0.9 copy-start.6
  43.7 47.4 %copy-start.1 = (f32[16,16,8,128]{3,2,1,0:T(8,128)}, f32[16,16,8,128]{3,2,1,0:T(8,128)S(1)}, u32[]{:S(2)}) copy-start(f32[16,16,8,128]{3,2,1,0:T(8,128)S(1)} %get-tuple-element.15) | copy-start | bytes 3145732
  43.7 11.8 %collective-permute-start.2 = (f32[1,8,16,128]{3,2,1,0:T(8,128)S(1)}, f32[1,8,16,128]{3,2,1,0:T(8,128)S(1)}, u32[]{:S(2)}, u32[]{:S(2)}) collective-permute-start(f32[1,8,16,128]{3,2,1,0:T(8,128)S(1)} %bitcast.6), channel_id=1, source_target_pairs={{119,0},{102,1},{113,2},{96,3},{115,4},{98,5},{117,6},{100,7},{127... | collective-permute-start | bytes 196616 | tf_op jit(solution)/shard_map/ppermute | solution.py:49
  46.3 10.2 %collective-permute-start.1 = (f32[1,8,16,128]{3,2,1,0:T(8,128)S(1)}, f32[1,8,16,128]{3,2,1,0:T(8,128)S(1)}, u32[]{:S(2)}, u32[]{:S(2)}) collective-permute-start(f32[1,8,16,128]{3,2,1,0:T(8,128)S(1)} %bitcast.7), channel_id=1, source_target_pairs={{84,0},{85,1},{86,2},{87,3},{80,4},{81,5},{82,6},{83,7},{92,8},{93... | collective-permute-start | bytes 196616 | tf_op jit(solution)/shard_map/ppermute | solution.py:49
  53.2 4.9 %collective-permute-start = (f32[1,8,16,128]{3,2,1,0:T(8,128)S(1)}, f32[1,8,16,128]{3,2,1,0:T(8,128)S(1)}, u32[]{:S(2)}, u32[]{:S(2)}) collective-permute-start(f32[1,8,16,128]{3,2,1,0:T(8,128)S(1)} %bitcast.8), channel_id=1, source_target_pairs={{35,0},{50,1},{37,2},{52,3},{39,4},{54,5},{33,6},{48,7},{43,8},{58... | collective-permute-start | bytes 196616 | tf_op jit(solution)/shard_map/ppermute | solution.py:49
  58.1 11.0 %collective-permute-start.5 = (f32[4,8,16,128]{3,2,1,0:T(8,128)S(1)}, f32[4,8,16,128]{3,2,1,0:T(8,128)S(1)}, u32[]{:S(2)}, u32[]{:S(2)}) collective-permute-start(f32[4,8,16,128]{3,2,1,0:T(8,128)S(1)} %pad_maximum_fusion), channel_id=1, source_target_pairs={{4,0},{5,1},{6,2},{7,3},{0,4},{1,5},{2,6},{3,7},{12,8},{13,9},{14,... | collective-permute-start | bytes 786440 | tf_op jit(solution)/shard_map/ppermute | solution.py:49
  59.2 9.9 %collective-permute-start.4 = (f32[4,8,16,128]{3,2,1,0:T(8,128)S(1)}, f32[4,8,16,128]{3,2,1,0:T(8,128)S(1)}, u32[]{:S(2)}, u32[]{:S(2)}) collective-permute-start(f32[4,8,16,128]{3,2,1,0:T(8,128)S(1)} %pad_maximum_fusion), channel_id=1, source_target_pairs={{64,0},{65,1},{66,2},{67,3},{68,4},{69,5},{70,6},{71,7},{72,8},{73... | collective-permute-start | bytes 786440 | tf_op jit(solution)/shard_map/ppermute | solution.py:49
  62.0 7.0 %collective-permute-start.3 = (f32[4,8,16,128]{3,2,1,0:T(8,128)S(1)}, f32[4,8,16,128]{3,2,1,0:T(8,128)S(1)}, u32[]{:S(2)}, u32[]{:S(2)}) collective-permute-start(f32[4,8,16,128]{3,2,1,0:T(8,128)S(1)} %pad_maximum_fusion), channel_id=1, source_target_pairs={{16,0},{17,1},{18,2},{19,3},{20,4},{21,5},{22,6},{23,7},{24,8},{25... | collective-permute-start | bytes 786440 | tf_op jit(solution)/shard_map/ppermute | solution.py:49
  69.1 15.0 %collective-permute-start.8 = (f32[16,8,16,128]{3,2,1,0:T(8,128)S(1)}, f32[16,8,16,128]{3,2,1,0:T(8,128)}, u32[]{:S(2)}, u32[]{:S(2)}) collective-permute-start(f32[16,8,16,128]{3,2,1,0:T(8,128)S(1)} %constant_dynamic-update-slice_fusion.rest_0_), channel_id=1, source_target_pairs={{1,0},{16,1},{3,2},{18,3},{5,4},{20,5},{7,6},{22,7},{25,8},{8,9},{... | collective-permute-start | bytes 3145736 | tf_op jit(solution)/shard_map/ppermute | solution.py:49
  69.5 18.4 %collective-permute-start.7 = (f32[16,8,16,128]{3,2,1,0:T(8,128)S(1)}, f32[16,8,16,128]{3,2,1,0:T(8,128)S(1)}, u32[]{:S(2)}, u32[]{:S(2)}) collective-permute-start(f32[16,8,16,128]{3,2,1,0:T(8,128)S(1)} %constant_dynamic-update-slice_fusion.rest_0_), channel_id=1, source_target_pairs={{2,0},{3,1},{4,2},{5,3},{6,4},{7,5},{0,6},{1,7},{14,8},{15,9},{8,1... | collective-permute-start | bytes 3145736 | tf_op jit(solution)/shard_map/ppermute | solution.py:49
  69.8 20.3 %collective-permute-start.6 = (f32[16,8,16,128]{3,2,1,0:T(8,128)S(1)}, f32[16,8,16,128]{3,2,1,0:T(8,128)S(1)}, u32[]{:S(2)}, u32[]{:S(2)}) collective-permute-start(f32[16,8,16,128]{3,2,1,0:T(8,128)S(1)} %constant_dynamic-update-slice_fusion.rest_0_), channel_id=1, source_target_pairs={{32,0},{33,1},{34,2},{35,3},{36,4},{37,5},{38,6},{39,7},{104,8},{1... | collective-permute-start | bytes 3145736 | tf_op jit(solution)/shard_map/ppermute | solution.py:49
  72.2 23.2 %collective-permute-start.9 = (f32[16,8,16,128]{3,2,1,0:T(8,128)S(1)}, f32[16,8,16,128]{3,2,1,0:T(8,128)}, u32[]{:S(2)}, u32[]{:S(2)}) collective-permute-start(f32[16,8,16,128]{3,2,1,0:T(8,128)S(1)} %constant_dynamic-update-slice_fusion.rest_0_), channel_id=1, source_target_pairs={{0,8},{1,9},{2,10},{3,11},{4,12},{5,13},{6,14},{7,15},{8,0},{9,1},... | collective-permute-start | bytes 3145736 | tf_op jit(solution)/shard_map/ppermute | solution.py:57
  84.2 11.3 %collective-permute-start.12 = (f32[16,8,16,128]{3,2,1,0:T(8,128)}, f32[16,8,16,128]{3,2,1,0:T(8,128)}, u32[]{:S(2)}, u32[]{:S(2)}) collective-permute-start(f32[16,8,16,128]{3,2,1,0:T(8,128)} %collective-permute-done.8.rest_3_), channel_id=1, source_target_pairs={{0,8},{1,9},{2,10},{3,11},{4,12},{5,13},{6,14},{7,15},{8,0},{9,1},... | collective-permute-start | bytes 3145736 | tf_op jit(solution)/shard_map/ppermute | solution.py:57
  87.9 7.6 %collective-permute-start.11 = (f32[16,8,16,128]{3,2,1,0:T(8,128)S(1)}, f32[16,8,16,128]{3,2,1,0:T(8,128)}, u32[]{:S(2)}, u32[]{:S(2)}) collective-permute-start(f32[16,8,16,128]{3,2,1,0:T(8,128)S(1)} %collective-permute-done.7.rest_2_), channel_id=1, source_target_pairs={{0,8},{1,9},{2,10},{3,11},{4,12},{5,13},{6,14},{7,15},{8,0},{9,1},... | collective-permute-start | bytes 3145736 | tf_op jit(solution)/shard_map/ppermute | solution.py:57
  90.1 5.4 %collective-permute-start.10 = (f32[16,8,16,128]{3,2,1,0:T(8,128)S(1)}, f32[16,8,16,128]{3,2,1,0:T(8,128)}, u32[]{:S(2)}, u32[]{:S(2)}) collective-permute-start(f32[16,8,16,128]{3,2,1,0:T(8,128)S(1)} %collective-permute-done.6.rest_1_), channel_id=1, source_target_pairs={{0,8},{1,9},{2,10},{3,11},{4,12},{5,13},{6,14},{7,15},{8,0},{9,1},... | collective-permute-start | bytes 3145736 | tf_op jit(solution)/shard_map/ppermute | solution.py:57
  91.2 19.3 %all-to-all-start.1 = ((f32[16,16,8,128]{3,2,1,0:T(8,128)}), f32[16,16,8,128]{3,2,1,0:T(8,128)}, u32[]{:S(2)}, u32[]{:S(2)}) async-start(f32[16,16,8,128]{3,2,1,0:T(8,128)} %copy-done.1), calls=%async_computation.1 | async-start | bytes 2097152 | tf_op jit(solution)/shard_map/all_to_all | solution.py:39
